TPU v7x, 32 devices: a whole 2x2x4 slice. The times are simulated.
32 devices in a mesh: rep: 8 (over y, x, core), fsdp: 4 (over z).
Axes of the slice: x: 2, y: 2, z: 4, core: 2. Of those that a mesh axis runs over, the one named last changes fastest.
Arguments:
- base: float32 [128, 8192], P('fsdp'), as said below
- local: bfloat16 [8, 128, 8192], P('rep', 'fsdp'), as said below
- momentum: float32 [128, 8192], P('fsdp'), may hold values from -3 to 3
- tokens: bfloat16 [8192, 128], P(('rep', 'fsdp')), may hold values from -0.5 to 0.5
Outputs:
- new_base: float32 [128, 8192], P('fsdp')
- new_momentum: float32 [128, 8192], P('fsdp')
- projected: bfloat16 [8192, 8192], P(('rep', 'fsdp'))
Inputs may be any that keep to these rules, and one draw needn't show every extreme that they name: `base`: entries of order one. `local`: each replica's copy of the rows lies near base, by block-wise differing amounts.
All inputs are finite; a program needn't handle non-finite values. Where the computation divides by a largest or mean magnitude, that divisor is 1e-20 or more.
Results may differ from a plain program's by a relative error of at most 0.008.
Values may be sent and summed in bfloat16 or wider, within the bound.
No kernel may reach another device: no remote copies, remote signals or barrier semaphores. Data moves between devices by JAX's collectives and lax.ppermute only.
A program may use at most 64 MiB of HBM per device.

v0:
```python
import jax
import jax.numpy as jnp
from jax import lax
from jax.sharding import PartitionSpec as P

BLOCK = 128


outer_lr = 0.7
outer_mu = 0.9


def encode(base, replica):
    delta = base - replica.astype(jnp.float32)
    blocks = delta.reshape(delta.shape[0], delta.shape[1] // BLOCK, BLOCK)
    scales = jnp.max(jnp.abs(blocks), axis=2) + 1e-06
    codes = (blocks / scales[:, :, None]).astype(jnp.bfloat16)
    return (codes.reshape(delta.shape), scales)


def decode(codes, scales):
    width = codes.shape[-1]
    blocks = codes.astype(jnp.float32).reshape(codes.shape[:-1] + (width // BLOCK, BLOCK))
    return (blocks * scales[..., None]).reshape(codes.shape)


def outer_step(total, base, momentum, replicas):
    average = total / replicas
    moved = outer_mu * momentum + average
    return (base - outer_lr * (average + outer_mu * moved), moved)


def on_device(base, local, momentum, tokens):
    replicas = lax.axis_size("rep")
    codes, scales = encode(base, local[0])
    codes = lax.optimization_barrier(codes)
    total = lax.psum(decode(codes, scales).astype(jnp.bfloat16), "rep").astype(jnp.float32)
    new_base, new_momentum = outer_step(total, base, momentum, replicas)
    fresh = new_base.astype(jnp.bfloat16)
    all_rows = lax.all_gather(fresh, "fsdp", axis=0, tiled=True)
    projected = jnp.dot(tokens, all_rows, preferred_element_type=jnp.float32)
    return (new_base, new_momentum, projected.astype(jnp.bfloat16))


def solution(mesh):
    in_specs = (P("fsdp", None), P("rep", "fsdp", None), P("fsdp", None), P(("rep", "fsdp"), None))
    out_specs = (P("fsdp", None), P("fsdp", None), P(("rep", "fsdp"), None))
    return jax.shard_map(
        on_device, mesh=mesh, in_specs=in_specs, out_specs=out_specs, check_vma=False
    )
```

profile of v0, /device:TPU:0, one launch (start us, length us, event | category | flops | bytes accessed | tf_op | source)
XLA Modules:
  0.0 135.5 jit_solution(2976646587650962573)
XLA Ops:
  7.2 0.0 copy-start
  7.2 0.0 copy-start.1
  7.2 0.0 copy-start.2
  7.2 0.0 all-reduce.2.cloned.1.call-start
  7.2 1.6 %abs_bitcast_fusion = f32[4,8,64,128]{3,1,2,0:T(8,128)S(1)} fusion(f32[32,8192]{1,0:T(8,128)} %param.4, bf16[1,32,8192]{2,1,0:T(8,128)(2,1)} %param.5), kind=kLoop, calls=%fused_computation.10 | loop fusion | flops 786432 | bytes 2621440
  8.8 0.2 copy.8
  9.0 0.3 reduce_max.9
  9.4 0.0 copy-start.3
  9.4 0.3 div.17
  9.7 0.0 copy-done.1
  9.7 0.0 copy-done.2
  9.7 0.7 fusion.1
  10.5 1.4 %fusion.2 = bf16[32,8192]{1,0:T(8,128)(2,1)} fusion(bf16[32,8192]{1,0:T(8,128)(2,1)S(1)} %fusion.1, f32[4,8,64,128]{3,2,1,0:T(8,128)S(1)} %bitcast.20), kind=kLoop, calls=%fused_computation.5 | loop fusion | flops 786432 | bytes 2097152 | tf_op jit(solution)/shard_map/convert_element_type | solution.py:37
  11.9 0.0 all-reduce.2.cloned.1.call-update
  11.9 0.0 all-gather.2.cloned.1.call-start
  11.9 57.3 %all-reduce.2.cloned.1.call-done = bf16[32,8192]{1,0:T(8,128)(2,1)} async-done(((bf16[32,8192]{1,0:T(8,128)(2,1)}), bf16[32,8192]{1,0:T(8,128)(2,1)}) %all-reduce.2.cloned.1.call-update) | async-done | bytes 524304 | tf_op jit(solution)/shard_map/psum | solution.py:37
  69.3 0.0 copy-done.3
  69.3 2.8 %fusion.3 = (bf16[32,8192]{1,0:T(8,128)(2,1)}, f32[32,8192]{1,0:T(8,128)}, f32[32,8192]{1,0:T(8,128)}) fusion(f32[32,8192]{1,0:T(8,128)S(1)} %copy-done.1, bf16[32,8192]{1,0:T(8,128)(2,1)} %all-reduce.2.cloned.1.call-done, f32[32,8192]{1,0:T(8,128)S(1)} %copy-done.3), kind=kLoop, calls=%fused_computation.12 | loop fusion | flops 2359296 | bytes 5242880 | tf_op jit(solution)/shard_map/convert_element_type | solution.py:39
  72.1 0.0 all-gather.2.cloned.1.call-update
  72.1 45.4 %all-gather.2.cloned.1.call-done = bf16[128,8192]{1,0:T(8,128)(2,1)} async-done(((bf16[32,8192]{1,0:T(8,128)(2,1)}), bf16[128,8192]{1,0:T(8,128)(2,1)}) %all-gather.2.cloned.1.call-update) | async-done | bytes 2097168 | tf_op jit(solution)/shard_map/all_gather | solution.py:40
  117.5 0.0 copy-done
  117.5 4.8 %fusion = bf16[256,8192]{0,1:T(8,128)(2,1)} fusion(bf16[128,8192]{1,0:T(8,128)(2,1)} %all-gather.2.cloned.1.call-done, bf16[256,128]{1,0:T(8,128)(2,1)S(1)} %copy-done), kind=kOutput, calls=%fused_computation.1 | convolution fusion | flops 538968064 | bytes 6356992 | tf_op jit(solution)/shard_map/dot_general | solution.py:41
  122.3 6.3 %copy.7 = bf16[256,8192]{1,0:T(8,128)(2,1)} copy(bf16[256,8192]{0,1:T(8,128)(2,1)} %fusion) | data formatting | bytes 8388608
  (1 shorter events, 0.0 us)
Async XLA Ops:
  7.2 110.3 %copy-start = (bf16[256,128]{1,0:T(8,128)(2,1)S(1)}, bf16[256,128]{1,0:T(8,128)(2,1)}, u32[]{:S(2)}) copy-start(bf16[256,128]{1,0:T(8,128)(2,1)} %param.7) | copy-start | bytes 196612
  7.2 2.6 %copy-start.1 = (f32[32,8192]{1,0:T(8,128)S(1)}, f32[32,8192]{1,0:T(8,128)}, u32[]{:S(2)}) copy-start(f32[32,8192]{1,0:T(8,128)} %param.4) | copy-start | bytes 3145732
  7.2 2.6 %copy-start.2 = (bf16[1,32,8192]{2,1,0:T(8,128)(2,1)S(1)}, bf16[1,32,8192]{2,1,0:T(8,128)(2,1)}, u32[]{:S(2)}) copy-start(bf16[1,32,8192]{2,1,0:T(8,128)(2,1)} %param.5) | copy-start | bytes 1572868
  7.2 62.1 %all-reduce.2.cloned.1.call-start = ((), (), s32[]{:S(2)}) async-start(), calls=%async_computation | async-start | bytes 1048576 | tf_op jit(solution)/shard_map/psum | solution.py:37
  9.4 59.9 %copy-start.3 = (f32[32,8192]{1,0:T(8,128)S(1)}, f32[32,8192]{1,0:T(8,128)}, u32[]{:S(2)}) copy-start(f32[32,8192]{1,0:T(8,128)} %param.6) | copy-start | bytes 3145732
  11.9 105.6 %all-gather.2.cloned.1.call-start = ((), (), s32[]{:S(2)}) async-start(), calls=%async_computation.1 | async-start | bytes 2621440 | tf_op jit(solution)/shard_map/all_gather | solution.py:40
Sparse Core Ops, SparseCore 0:
  12.0 57.2 all-reduce.1
  72.2 45.2 all-gather.1
where the time goes:
time: 136 us; the launch traced here: 135 us
  waiting for transfers between devices  103 us (76%)
  between operations  14.1 us (10%)
  local copies, waits for them, and re-layouts  6.85 us (5%)
  other arithmetic  6.84 us (5%)
  matrix products  4.81 us (4%)
    psum x1, waiting for transfers between devices, on_device(): lax.psum(decode(codes, scales).astype(jnp.bfloat16), 'rep')  57.3 us
    all_gather x1, waiting for transfers between devices, on_device(): all_rows = lax.all_gather(fresh, 'fsdp', axis=0, tiled=True)  45.4 us
    unnamed x10, local copies, waits for them, and re-layouts  6.53 us
    dot_general x1, matrix products, on_device(): projected = jnp.dot(tokens, all_rows, preferred_element_type=jnp.float32)  4.81 us
    convert_element_type x1, other arithmetic, on_device(): fresh = new_base.astype(jnp.bfloat16)  2.81 us
  transfers between devices with their start and end apart: 2, of which 2 were waited for; matrix products, arithmetic and copies ran while one was open for 0% of the time, Pallas kernels for 0%

commit v1 on v0

v1 whole, which is shorter than its diff:
```python
import functools

import jax
import jax.numpy as jnp
from jax import lax
from jax.experimental import pallas as pl
from jax.experimental.pallas import tpu as pltpu
from jax.sharding import PartitionSpec as P

BLOCK = 128
MIB = 1 << 20

outer_lr = 0.7
outer_mu = 0.9


def params(mib=8):
    return pltpu.CompilerParams(vmem_limit_bytes=mib * MIB)


def decoded_block(base, replica):
    delta = base - replica.astype(jnp.float32)
    scale = jnp.max(jnp.abs(delta), axis=1, keepdims=True) + 1e-06
    code = (delta / scale).astype(jnp.bfloat16)
    return (code.astype(jnp.float32) * scale).astype(jnp.bfloat16)


def encode_kernel(at_ref, base_ref, local_ref, out_ref):
    for b in range(base_ref.shape[1] // BLOCK):
        cols = slice(b * BLOCK, (b + 1) * BLOCK)
        out_ref[0, :, cols] = decoded_block(base_ref[:, cols], local_ref[0, :, cols])


def encode(at, base, local, flip, chips, width):
    rows = base.shape[0]
    return pl.pallas_call(
        encode_kernel,
        out_shape=jax.ShapeDtypeStruct((chips, rows, width), jnp.bfloat16),
        grid_spec=pltpu.PrefetchScalarGridSpec(
            num_scalar_prefetch=1,
            grid=(chips,),
            in_specs=[
                pl.BlockSpec((rows, width), lambda j, at: (0, at[0] ^ flip ^ (2 * j))),
                pl.BlockSpec((1, rows, width), lambda j, at: (0, 0, at[0] ^ flip ^ (2 * j))),
            ],
            out_specs=pl.BlockSpec((1, rows, width), lambda j, at: (j, 0, 0)),
        ),
        compiler_params=params(),
    )(at, base, local)


def chip_sum_kernel(keep_ref, recv_ref, *out_refs):
    for j, out_ref in enumerate(out_refs):
        total = keep_ref[j].astype(jnp.float32) + recv_ref[j].astype(jnp.float32)
        out_ref[...] = total.astype(out_ref.dtype)


def chip_sum(keep, recv):
    chips, rows, width = keep.shape
    return pl.pallas_call(
        chip_sum_kernel,
        out_shape=[
            jax.ShapeDtypeStruct((rows, width), jnp.float32 if j == 0 else jnp.bfloat16)
            for j in range(chips)
        ],
        compiler_params=params(),
    )(keep, recv)


def stepped(average, base, momentum):
    moved = outer_mu * momentum + average
    return base - outer_lr * (average + outer_mu * moved), moved


def chunk_step_kernel(replicas, at_ref, base_ref, mom_ref, own_ref, *refs):
    parts, (avg_ref, fresh_ref) = refs[:-2], refs[-2:]
    total = own_ref[...]
    for part in parts:
        total = total + part[...].astype(jnp.float32)
    average = (total / replicas).astype(jnp.bfloat16)
    avg_ref[...] = average
    new_base, _ = stepped(average.astype(jnp.float32), base_ref[...], mom_ref[...])
    fresh_ref[...] = new_base.astype(jnp.bfloat16)


def chunk_step(at, base, momentum, own, parts, replicas):
    rows, width = own.shape
    whole = pl.BlockSpec((rows, width), lambda i, at: (0, 0))
    mine = pl.BlockSpec((rows, width), lambda i, at: (0, at[0]))
    return pl.pallas_call(
        functools.partial(chunk_step_kernel, replicas),
        out_shape=[jax.ShapeDtypeStruct((rows, width), jnp.bfloat16)] * 2,
        grid_spec=pltpu.PrefetchScalarGridSpec(
            num_scalar_prefetch=1,
            grid=(1,),
            in_specs=[mine, mine, whole] + [whole] * len(parts),
            out_specs=[whole, whole],
        ),
        compiler_params=params(),
    )(at, base, momentum, own, *parts)


def outer_kernel(replicas, at_ref, base_ref, mom_ref, *refs):
    parts, (new_base_ref, new_mom_ref, fresh_ref) = refs[:replicas], refs[replicas:]
    for k, part in enumerate(parts):

        @pl.when(pl.program_id(0) == k)
        def _():
            new_base, moved = stepped(part[...].astype(jnp.float32), base_ref[...], mom_ref[...])
            new_base_ref[...] = new_base
            new_mom_ref[...] = moved
            fresh_ref[0] = new_base.astype(jnp.bfloat16)


def outer(at, base, momentum, averages):
    rows, width = averages[0].shape
    replicas = len(averages)
    whole = pl.BlockSpec((rows, width), lambda k, at: (0, 0))
    chunk = pl.BlockSpec((rows, width), lambda k, at: (0, at[0] ^ k))
    return pl.pallas_call(
        functools.partial(outer_kernel, replicas),
        out_shape=[
            jax.ShapeDtypeStruct(base.shape, jnp.float32),
            jax.ShapeDtypeStruct(base.shape, jnp.float32),
            jax.ShapeDtypeStruct((replicas, rows, width), jnp.bfloat16),
        ],
        grid_spec=pltpu.PrefetchScalarGridSpec(
            num_scalar_prefetch=1,
            grid=(replicas,),
            in_specs=[chunk, chunk] + [whole] * replicas,
            out_specs=[chunk, chunk, pl.BlockSpec((1, rows, width), lambda k, at: (k, 0, 0))],
        ),
        compiler_params=params(),
    )(at, base, momentum, *averages)


def project_kernel(replicas, at_ref, tok_ref, own_ref, *refs):
    parts, (out_ref, rhs_ref) = refs[:replicas], refs[replicas:]
    rows = own_ref.shape[1]
    here = at_ref[1]

    def place(s):
        return pl.ds(pl.multiple_of((here ^ s) * rows, rows), rows)

    rhs_ref[place(0), :] = own_ref[0]
    for k, part in enumerate(parts):

        @pl.when(pl.program_id(0) == k)
        def _():
            for s in range(part.shape[0] // rows):
                rhs_ref[place(s + 1), :] = part[s * rows : (s + 1) * rows, :]

    out_ref[...] = jnp.dot(
        tok_ref[...], rhs_ref[...], preferred_element_type=jnp.float32
    ).astype(out_ref.dtype)


def project(at, tokens, own, others):
    replicas, rows, width = own.shape
    tall, depth = tokens.shape
    far = others[0].shape[0]
    return pl.pallas_call(
        functools.partial(project_kernel, replicas),
        out_shape=jax.ShapeDtypeStruct((tall, width * replicas), jnp.bfloat16),
        grid_spec=pltpu.PrefetchScalarGridSpec(
            num_scalar_prefetch=1,
            grid=(replicas,),
            in_specs=[
                pl.BlockSpec((tall, depth), lambda k, at: (0, 0)),
                pl.BlockSpec((1, rows, width), lambda k, at: (k, 0, 0)),
            ]
            + [pl.BlockSpec((far, width), lambda k, at: (0, 0))] * replicas,
            out_specs=pl.BlockSpec((tall, width), lambda k, at: (0, at[0] ^ k)),
            scratch_shapes=[pltpu.VMEM((depth, width), jnp.bfloat16)],
        ),
        compiler_params=params(24),
    )(at, tokens, own, *others)


def swap(x, axis, flip):
    return lax.ppermute(x, axis, [(i, i ^ flip) for i in range(lax.axis_size(axis))])


def on_device(base, local, momentum, tokens):
    replicas, groups = lax.axis_size("rep"), lax.axis_size("fsdp")
    chips = replicas // 2
    width = base.shape[1] // replicas
    at = jnp.stack([lax.axis_index("rep"), lax.axis_index("fsdp")]).astype(jnp.int32)

    send = encode(at, base, local, 1, chips, width)
    recv = swap(send, "rep", 1)
    keep = encode(at, base, local, 0, chips, width)
    sums = chip_sum(keep, recv)
    parts = [swap(sums[j], "rep", 2 * j) for j in range(1, chips)]
    average, fresh = chunk_step(at, base, momentum, sums[0], parts, replicas)

    far = jnp.concatenate([swap(fresh, "fsdp", s) for s in range(1, groups)], axis=0)
    averages = [average] + [swap(average, "rep", 2 * j) for j in range(1, chips)]
    averages = [x for a in averages for x in (a, swap(a, "rep", 1))]
    new_base, new_momentum, own = outer(at, base, momentum, averages)

    others = [far] + [swap(far, "rep", 2 * j) for j in range(1, chips)]
    others = [x for a in others for x in (a, swap(a, "rep", 1))]
    projected = project(at, tokens, own, others)
    return new_base, new_momentum, projected


def solution(mesh):
    in_specs = (P("fsdp", None), P("rep", "fsdp", None), P("fsdp", None), P(("rep", "fsdp"), None))
    out_specs = (P("fsdp", None), P("fsdp", None), P(("rep", "fsdp"), None))
    return jax.shard_map(
        on_device, mesh=mesh, in_specs=in_specs, out_specs=out_specs, check_vma=False
    )
```

time: 136 us -> 55.5 us (0.41)
  waiting for transfers between devices: 103 us -> 22.9 us
  starting transfers between devices: 0.08 us -> 16.9 us
  between operations: 14.1 us -> 0.74 us
  Pallas kernels: 0 us -> 12.4 us
  other arithmetic: 6.84 us -> 0.08 us
  matrix products: 4.81 us -> 0 us
  local copies, waits for them, and re-layouts: 6.85 us -> 2.3 us
    psum x1 -> x0, waiting for transfers between devices: 57.3 us -> none  [on_device(): lax.psum(decode(codes, scales).astype(jnp.bfloat16), 'rep')]
    all_gather x1 -> x0, waiting for transfers between devices: 45.4 us -> none  [on_device(): all_rows = lax.all_gather(fresh, 'fsdp', axis=0, tiled=True)]
    ppermute x0 -> x21, waiting for transfers between devices: none -> 22.9 us  [swap(): lax.ppermute(x, axis, [(i, i ^ flip) for i in range(lax.axis_size(axis))])]
    ppermute x0 -> x21, starting transfers between devices: none -> 16.9 us  [swap(): lax.ppermute(x, axis, [(i, i ^ flip) for i in range(lax.axis_size(axis))])]
    pallas_call x0 -> x6, Pallas kernels: none -> 12.4 us  [the longest x1 5.4 us: project(): pl.pallas_call(functools.partial(project_kernel, replicas), out_shape=jax...]
    convert_element_type x3 -> x0, other arithmetic: 4.91 us -> none  [the longest x1 2.81 us: on_device(): fresh = new_base.astype(jnp.bfloat16)]
    dot_general x1 -> x0, matrix products: 4.81 us -> none  [on_device(): projected = jnp.dot(tokens, all_rows, preferred_element_type=jnp.float32)]
    unnamed x10 -> x12, local copies, waits for them, and re-layouts: 6.53 us -> 2.29 us
  transfers between devices with their start and end apart: 2 -> 21, of which waited for: 2 -> 11; matrix products, arithmetic and copies ran while one was open for 0% -> 0% of each run, Pallas kernels for 0% -> 9%
where the time goes in v1:
time: 55.5 us; the launch traced here: 55.3 us
  waiting for transfers between devices  22.9 us (41%)
  starting transfers between devices  16.9 us (30%)
  Pallas kernels  12.4 us (22%)
  local copies, waits for them, and re-layouts  2.3 us (4%)
  between operations  0.74 us (1%)
    ppermute x21, waiting for transfers between devices, swap(): lax.ppermute(x, axis, [(i, i ^ flip) for i in range(lax.axis_size(axis))])  22.9 us
    ppermute x21, starting transfers between devices, swap(): lax.ppermute(x, axis, [(i, i ^ flip) for i in range(lax.axis_size(axis))])  16.9 us
    pallas_call x1, Pallas kernels, project(): pl.pallas_call(functools.partial(project_kernel, replicas), out_shape=jax...  5.4 us
    pallas_call x1, Pallas kernels, outer(): pl.pallas_call(functools.partial(outer_kernel, replicas), out_shape=[jax....  3.92 us
    pallas_call x2, Pallas kernels, encode(): pl.pallas_call(encode_kernel, out_shape=jax.ShapeDtypeStruct((chips, rows...  2.43 us
    unnamed x12, local copies, waits for them, and re-layouts  2.29 us
  transfers between devices with their start and end apart: 21, of which 11 were waited for; matrix products, arithmetic and copies ran while one was open for 0% of the time, Pallas kernels for 9%

profile of v1, /device:TPU:0, one launch (start us, length us, event | category | flops | bytes accessed | tf_op | source)
XLA Modules:
  0.0 55.3 jit_solution(6301234240186648046)
XLA Ops:
  0.7 1.2 %copy-done = f32[32,8192]{1,0:T(8,128)S(1)} copy-done((f32[32,8192]{1,0:T(8,128)S(1)}, f32[32,8192]{1,0:T(8,128)}, u32[]{:S(2)}) %copy-start) | copy-done | bytes 1048600
  1.9 1.0 %copy-done.3 = bf16[1,32,8192]{2,1,0:T(8,128)(2,1)S(1)} copy-done((bf16[1,32,8192]{2,1,0:T(8,128)(2,1)S(1)}, bf16[1,32,8192]{2,1,0:T(8,128)(2,1)}, u32[]{:S(2)}) %copy-start.3) | copy-done | bytes 524312
  3.0 1.2 %shard_map.68 = bf16[4,32,1024]{2,1,0:T(8,128)(2,1)S(1)} custom-call(s32[2]{0:T(128)S(1)} %pad_add_fusion.at_ref, f32[32,8192]{1,0:T(8,128)S(1)} %copy-done, bf16[1,32,8192]{2,1,0:T(8,128)(2,1)S(1)} %copy-done.3), custom_call_target="tpu_custom_call" | custom-call | tf_op jit(solution)/shard_map/pallas_call | solution.py:36
  4.2 0.5 collective-permute-start
  4.7 1.2 %shard_map.67.keep_ref = bf16[4,32,1024]{2,1,0:T(8,128)(2,1)S(1)} custom-call(s32[2]{0:T(128)S(1)} %pad_add_fusion.at_ref, f32[32,8192]{1,0:T(8,128)S(1)} %copy-done, bf16[1,32,8192]{2,1,0:T(8,128)(2,1)S(1)} %copy-done.3), custom_call_target="tpu_custom_call" | custom-call | tf_op jit(solution)/shard_map/pallas_call | solution.py:36
  6.0 2.9 %collective-permute-start.1 = (bf16[32,1024]{1,0:T(8,128)(2,1)S(1)}, bf16[32,1024]{1,0:T(8,128)(2,1)S(1)}, u32[]{:S(2)}, u32[]{:S(2)}) collective-permute-start(bf16[32,1024]{1,0:T(8,128)(2,1)S(1)} %get-tuple-element.13), channel_id=1, source_target_pairs={{0,8},{4,12},{8,0},{12,4},{16,24},{20,28},{24,16},{28,20},{1,9},{5... | collective-permute-start | bytes 196616 | tf_op jit(solution)/shard_map/ppermute | solution.py:181
  8.9 1.5 %collective-permute-start.2 = (bf16[32,1024]{1,0:T(8,128)(2,1)S(1)}, bf16[32,1024]{1,0:T(8,128)(2,1)S(1)}, u32[]{:S(2)}, u32[]{:S(2)}) collective-permute-start(bf16[32,1024]{1,0:T(8,128)(2,1)S(1)} %get-tuple-element.14), channel_id=1, source_target_pairs={{0,16},{4,20},{8,24},{12,28},{16,0},{20,4},{24,8},{28,12},{1,17},{... | collective-permute-start | bytes 196616 | tf_op jit(solution)/shard_map/ppermute | solution.py:181
  10.4 0.9 %collective-permute-done.1.refs_0_ = bf16[32,1024]{1,0:T(8,128)(2,1)S(1)} collective-permute-done((bf16[32,1024]{1,0:T(8,128)(2,1)S(1)}, bf16[32,1024]{1,0:T(8,128)(2,1)S(1)}, u32[]{:S(2)}, u32[]{:S(2)}) %collective-permute-start.1) | collective-permute-done | bytes 65568 | tf_op jit(solution)/shard_map/ppermute | solution.py:181
  11.4 1.8 %collective-permute-done.2.refs_1_ = bf16[32,1024]{1,0:T(8,128)(2,1)S(1)} collective-permute-done((bf16[32,1024]{1,0:T(8,128)(2,1)S(1)}, bf16[32,1024]{1,0:T(8,128)(2,1)S(1)}, u32[]{:S(2)}, u32[]{:S(2)}) %collective-permute-start.2) | collective-permute-done | bytes 65568 | tf_op jit(solution)/shard_map/ppermute | solution.py:181
  13.2 2.4 %collective-permute-done.3.refs_2_ = bf16[32,1024]{1,0:T(8,128)(2,1)S(1)} collective-permute-done((bf16[32,1024]{1,0:T(8,128)(2,1)S(1)}, bf16[32,1024]{1,0:T(8,128)(2,1)S(1)}, u32[]{:S(2)}, u32[]{:S(2)}) %collective-permute-start.3) | collective-permute-done | bytes 65568 | tf_op jit(solution)/shard_map/ppermute | solution.py:181
  15.6 0.6 %shard_map.70 = (bf16[32,1024]{1,0:T(8,128)(2,1)S(1)}, bf16[32,1024]{1,0:T(8,128)(2,1)S(1)}) custom-call(s32[2]{0:T(128)S(1)} %pad_add_fusion.at_ref, f32[32,8192]{1,0:T(8,128)S(1)} %copy-done.1, f32[32,8192]{1,0:T(8,128)S(1)} %copy-done.2, f32[32,1024]{1,0:T(8,128)S(1)} %get-tuple-element.12.own_ref, bf16[32,1024]{1,0:T(8,128)(2,1)S(1)} %collective-permute-done.1.refs_0_, ...), custom_call_target="tpu_custom_call" | custom-call | tf_op jit(solution)/shard_map/pallas_call | solution.py:90
  16.2 1.6 %collective-permute-start.11 = (bf16[32,1024]{1,0:T(8,128)(2,1)S(1)}, bf16[32,1024]{1,0:T(8,128)(2,1)S(1)}, u32[]{:S(2)}, u32[]{:S(2)}) collective-permute-start(bf16[32,1024]{1,0:T(8,128)(2,1)S(1)} %get-tuple-element.20), channel_id=1, source_target_pairs={{0,1},{1,0},{2,3},{3,2},{4,5},{5,4},{6,7},{7,6},{8,9},{9,8},{10,11... | collective-permute-start | bytes 196616 | tf_op jit(solution)/shard_map/ppermute | solution.py:181
  17.8 2.5 %collective-permute-start.13 = (bf16[32,1024]{1,0:T(8,128)(2,1)S(1)}, bf16[32,1024]{1,0:T(8,128)(2,1)S(1)}, u32[]{:S(2)}, u32[]{:S(2)}) collective-permute-start(bf16[32,1024]{1,0:T(8,128)(2,1)S(1)} %get-tuple-element.20), channel_id=1, source_target_pairs={{0,3},{1,2},{2,1},{3,0},{4,7},{5,6},{6,5},{7,4},{8,11},{9,10},{10,... | collective-permute-start | bytes 196616 | tf_op jit(solution)/shard_map/ppermute | solution.py:181
  20.5 5.6 %collective-permute-done.12 = bf16[32,1024]{1,0:T(8,128)(2,1)S(1)} collective-permute-done((bf16[32,1024]{1,0:T(8,128)(2,1)S(1)}, bf16[32,1024]{1,0:T(8,128)(2,1)S(1)}, u32[]{:S(2)}, u32[]{:S(2)}) %collective-permute-start.12) | collective-permute-done | bytes 65568 | tf_op jit(solution)/shard_map/ppermute | solution.py:181
  26.2 0.5 collective-permute-start.19
  26.8 1.5 %collective-permute-start.17 = (bf16[96,1024]{1,0:T(8,128)(2,1)S(1)}, bf16[96,1024]{1,0:T(8,128)(2,1)S(1)}, u32[]{:S(2)}, u32[]{:S(2)}) collective-permute-start(bf16[96,1024]{1,0:T(8,128)(2,1)S(1)} %constant_dynamic-update-slice_fusion.refs_0_), channel_id=1, source_target_pairs={{0,16},{4,20},{8,24},{12,28},{16,0},{20,4},{24,8},{28,12},{1,17},{... | collective-permute-start | bytes 589832 | tf_op jit(solution)/shard_map/ppermute | solution.py:181
  28.3 1.5 %collective-permute-start.15 = (bf16[96,1024]{1,0:T(8,128)(2,1)S(1)}, bf16[96,1024]{1,0:T(8,128)(2,1)S(1)}, u32[]{:S(2)}, u32[]{:S(2)}) collective-permute-start(bf16[96,1024]{1,0:T(8,128)(2,1)S(1)} %constant_dynamic-update-slice_fusion.refs_0_), channel_id=1, source_target_pairs={{0,8},{4,12},{8,0},{12,4},{16,24},{20,28},{24,16},{28,20},{1,9},{5... | collective-permute-start | bytes 589832 | tf_op jit(solution)/shard_map/ppermute | solution.py:181
  29.8 0.4 collective-permute-start.9
  30.2 1.5 %collective-permute-start.7 = (bf16[32,1024]{1,0:T(8,128)(2,1)S(1)}, bf16[32,1024]{1,0:T(8,128)(2,1)S(1)}, u32[]{:S(2)}, u32[]{:S(2)}) collective-permute-start(bf16[32,1024]{1,0:T(8,128)(2,1)S(1)} %get-tuple-element.16.refs_0_), channel_id=1, source_target_pairs={{0,16},{4,20},{8,24},{12,28},{16,0},{20,4},{24,8},{28,12},{1,17},{... | collective-permute-start | bytes 196616 | tf_op jit(solution)/shard_map/ppermute | solution.py:181
  31.8 6.1 %collective-permute-done.9.refs_6_ = bf16[32,1024]{1,0:T(8,128)(2,1)S(1)} collective-permute-done((bf16[32,1024]{1,0:T(8,128)(2,1)S(1)}, bf16[32,1024]{1,0:T(8,128)(2,1)S(1)}, u32[]{:S(2)}, u32[]{:S(2)}) %collective-permute-start.9) | collective-permute-done | bytes 65568 | tf_op jit(solution)/shard_map/ppermute | solution.py:181
  37.8 0.6 collective-permute-start.5
  38.4 0.1 collective-permute-done.7.refs_4_
  38.5 3.6 %collective-permute-done.5.refs_2_ = bf16[32,1024]{1,0:T(8,128)(2,1)S(1)} collective-permute-done((bf16[32,1024]{1,0:T(8,128)(2,1)S(1)}, bf16[32,1024]{1,0:T(8,128)(2,1)S(1)}, u32[]{:S(2)}, u32[]{:S(2)}) %collective-permute-start.5) | collective-permute-done | bytes 65568 | tf_op jit(solution)/shard_map/ppermute | solution.py:181
  42.1 0.5 collective-permute-start.14
  42.7 0.4 collective-permute-start.18
  43.2 0.1 collective-permute-done.10.refs_7_
  43.3 0.3 collective-permute-start.8
  43.6 1.1 %collective-permute-done.8.refs_5_ = bf16[32,1024]{1,0:T(8,128)(2,1)S(1)} collective-permute-done((bf16[32,1024]{1,0:T(8,128)(2,1)S(1)}, bf16[32,1024]{1,0:T(8,128)(2,1)S(1)}, u32[]{:S(2)}, u32[]{:S(2)}) %collective-permute-start.8) | collective-permute-done | bytes 65568 | tf_op jit(solution)/shard_map/ppermute | solution.py:181
  44.7 0.3 collective-permute-start.6
  45.0 1.0 %collective-permute-done.6.refs_3_ = bf16[32,1024]{1,0:T(8,128)(2,1)S(1)} collective-permute-done((bf16[32,1024]{1,0:T(8,128)(2,1)S(1)}, bf16[32,1024]{1,0:T(8,128)(2,1)S(1)}, u32[]{:S(2)}, u32[]{:S(2)}) %collective-permute-start.6) | collective-permute-done | bytes 65568 | tf_op jit(solution)/shard_map/ppermute | solution.py:181
  46.0 3.9 %shard_map.71 = (f32[32,8192]{1,0:T(8,128)}, f32[32,8192]{1,0:T(8,128)}, bf16[8,32,1024]{2,1,0:T(8,128)(2,1)S(1)}) custom-call(s32[2]{0:T(128)S(1)} %pad_add_fusion.at_ref, f32[32,8192]{1,0:T(8,128)S(1)} %copy-done.1, f32[32,8192]{1,0:T(8,128)S(1)} %copy-done.2, bf16[32,1024]{1,0:T(8,128)(2,1)S(1)} %get-tuple-element.16.refs_0_, ...), custom_call_target="tpu_custom_call" | custom-call | tf_op jit(solution)/shard_map/pallas_call | solution.py:120
  49.9 5.4 %shard_map.72 = bf16[256,8192]{1,0:T(8,128)(2,1)} custom-call(s32[2]{0:T(128)S(1)} %pad_add_fusion.at_ref, bf16[256,128]{1,0:T(8,128)(2,1)S(1)} %copy-done.4, bf16[8,32,1024]{2,1,0:T(8,128)(2,1)S(1)} %get-tuple-element.19.own_ref, bf16[96,1024]{1,0:T(8,128)(2,1)S(1)} %constant_dynamic-update-slice_fusion.refs_0_, ...), custom_call_target="tpu_custom_call" | custom-call | tf_op jit(solution)/shard_map/pallas_call | solution.py:162
  (30 shorter events, 0.6 us)
Async XLA Ops:
  0.7 1.2 %copy-start = (f32[32,8192]{1,0:T(8,128)S(1)}, f32[32,8192]{1,0:T(8,128)}, u32[]{:S(2)}) copy-start(f32[32,8192]{1,0:T(8,128)} %base_ref.7) | copy-start | bytes 3145732
  1.9 1.0 %copy-start.3 = (bf16[1,32,8192]{2,1,0:T(8,128)(2,1)S(1)}, bf16[1,32,8192]{2,1,0:T(8,128)(2,1)}, u32[]{:S(2)}) copy-start(bf16[1,32,8192]{2,1,0:T(8,128)(2,1)} %local_ref.3) | copy-start | bytes 1572868
  3.0 12.6 %copy-start.1 = (f32[32,8192]{1,0:T(8,128)S(1)}, f32[32,8192]{1,0:T(8,128)}, u32[]{:S(2)}) copy-start(f32[32,8192]{1,0:T(8,128)} %base_ref.7) | copy-start | bytes 3145732
  3.0 12.6 %copy-start.2 = (f32[32,8192]{1,0:T(8,128)S(1)}, f32[32,8192]{1,0:T(8,128)}, u32[]{:S(2)}) copy-start(f32[32,8192]{1,0:T(8,128)} %mom_ref.3) | copy-start | bytes 3145732
  4.2 45.7 %copy-start.4 = (bf16[256,128]{1,0:T(8,128)(2,1)S(1)}, bf16[256,128]{1,0:T(8,128)(2,1)}, u32[]{:S(2)}) copy-start(bf16[256,128]{1,0:T(8,128)(2,1)} %tok_ref.1) | copy-start | bytes 196612
  4.2 1.7 %collective-permute-start = (bf16[4,32,1024]{2,1,0:T(8,128)(2,1)S(1)}, bf16[4,32,1024]{2,1,0:T(8,128)(2,1)S(1)}, u32[]{:S(2)}, u32[]{:S(2)}) collective-permute-start(bf16[4,32,1024]{2,1,0:T(8,128)(2,1)S(1)} %shard_map.68), channel_id=1, source_target_pairs={{0,4},{4,0},{8,12},{12,8},{16,20},{20,16},{24,28},{28,24},{1,5},{5... | collective-permute-start | bytes 786440 | tf_op jit(solution)/shard_map/ppermute | solution.py:181
  6.0 5.3 %collective-permute-start.1 = (bf16[32,1024]{1,0:T(8,128)(2,1)S(1)}, bf16[32,1024]{1,0:T(8,128)(2,1)S(1)}, u32[]{:S(2)}, u32[]{:S(2)}) collective-permute-start(bf16[32,1024]{1,0:T(8,128)(2,1)S(1)} %get-tuple-element.13), channel_id=1, source_target_pairs={{0,8},{4,12},{8,0},{12,4},{16,24},{20,28},{24,16},{28,20},{1,9},{5... | collective-permute-start | bytes 196616 | tf_op jit(solution)/shard_map/ppermute | solution.py:181
  8.9 4.3 %collective-permute-start.2 = (bf16[32,1024]{1,0:T(8,128)(2,1)S(1)}, bf16[32,1024]{1,0:T(8,128)(2,1)S(1)}, u32[]{:S(2)}, u32[]{:S(2)}) collective-permute-start(bf16[32,1024]{1,0:T(8,128)(2,1)S(1)} %get-tuple-element.14), channel_id=1, source_target_pairs={{0,16},{4,20},{8,24},{12,28},{16,0},{20,4},{24,8},{28,12},{1,17},{... | collective-permute-start | bytes 196616 | tf_op jit(solution)/shard_map/ppermute | solution.py:181
  10.4 5.2 %collective-permute-start.3 = (bf16[32,1024]{1,0:T(8,128)(2,1)S(1)}, bf16[32,1024]{1,0:T(8,128)(2,1)S(1)}, u32[]{:S(2)}, u32[]{:S(2)}) collective-permute-start(bf16[32,1024]{1,0:T(8,128)(2,1)S(1)} %get-tuple-element.15), channel_id=1, source_target_pairs={{0,24},{4,28},{8,16},{12,20},{16,8},{20,12},{24,0},{28,4},{1,25},{... | collective-permute-start | bytes 196616 | tf_op jit(solution)/shard_map/ppermute | solution.py:181
  16.2 4.3 %collective-permute-start.11 = (bf16[32,1024]{1,0:T(8,128)(2,1)S(1)}, bf16[32,1024]{1,0:T(8,128)(2,1)S(1)}, u32[]{:S(2)}, u32[]{:S(2)}) collective-permute-start(bf16[32,1024]{1,0:T(8,128)(2,1)S(1)} %get-tuple-element.20), channel_id=1, source_target_pairs={{0,1},{1,0},{2,3},{3,2},{4,5},{5,4},{6,7},{7,6},{8,9},{9,8},{10,11... | collective-permute-start | bytes 196616 | tf_op jit(solution)/shard_map/ppermute | solution.py:181
  17.8 8.4 %collective-permute-start.13 = (bf16[32,1024]{1,0:T(8,128)(2,1)S(1)}, bf16[32,1024]{1,0:T(8,128)(2,1)S(1)}, u32[]{:S(2)}, u32[]{:S(2)}) collective-permute-start(bf16[32,1024]{1,0:T(8,128)(2,1)S(1)} %get-tuple-element.20), channel_id=1, source_target_pairs={{0,3},{1,2},{2,1},{3,0},{4,7},{5,6},{6,5},{7,4},{8,11},{9,10},{10,... | collective-permute-start | bytes 196616 | tf_op jit(solution)/shard_map/ppermute | solution.py:181
  20.3 5.9 %collective-permute-start.12 = (bf16[32,1024]{1,0:T(8,128)(2,1)S(1)}, bf16[32,1024]{1,0:T(8,128)(2,1)S(1)}, u32[]{:S(2)}, u32[]{:S(2)}) collective-permute-start(bf16[32,1024]{1,0:T(8,128)(2,1)S(1)} %get-tuple-element.20), channel_id=1, source_target_pairs={{0,2},{1,3},{2,0},{3,1},{4,6},{5,7},{6,4},{7,5},{8,10},{9,11},{10,... | collective-permute-start | bytes 196616 | tf_op jit(solution)/shard_map/ppermute | solution.py:181
  26.2 16.4 %collective-permute-start.19 = (bf16[96,1024]{1,0:T(8,128)(2,1)S(1)}, bf16[96,1024]{1,0:T(8,128)(2,1)S(1)}, u32[]{:S(2)}, u32[]{:S(2)}) collective-permute-start(bf16[96,1024]{1,0:T(8,128)(2,1)S(1)} %constant_dynamic-update-slice_fusion.refs_0_), channel_id=1, source_target_pairs={{0,24},{4,28},{8,16},{12,20},{16,8},{20,12},{24,0},{28,4},{1,25},{... | collective-permute-start | bytes 589832 | tf_op jit(solution)/shard_map/ppermute | solution.py:181
  26.8 15.9 %collective-permute-start.17 = (bf16[96,1024]{1,0:T(8,128)(2,1)S(1)}, bf16[96,1024]{1,0:T(8,128)(2,1)S(1)}, u32[]{:S(2)}, u32[]{:S(2)}) collective-permute-start(bf16[96,1024]{1,0:T(8,128)(2,1)S(1)} %constant_dynamic-update-slice_fusion.refs_0_), channel_id=1, source_target_pairs={{0,16},{4,20},{8,24},{12,28},{16,0},{20,4},{24,8},{28,12},{1,17},{... | collective-permute-start | bytes 589832 | tf_op jit(solution)/shard_map/ppermute | solution.py:181
  28.3 14.8 %collective-permute-start.15 = (bf16[96,1024]{1,0:T(8,128)(2,1)S(1)}, bf16[96,1024]{1,0:T(8,128)(2,1)S(1)}, u32[]{:S(2)}, u32[]{:S(2)}) collective-permute-start(bf16[96,1024]{1,0:T(8,128)(2,1)S(1)} %constant_dynamic-update-slice_fusion.refs_0_), channel_id=1, source_target_pairs={{0,8},{4,12},{8,0},{12,4},{16,24},{20,28},{24,16},{28,20},{1,9},{5... | collective-permute-start | bytes 589832 | tf_op jit(solution)/shard_map/ppermute | solution.py:181
  29.8 8.0 %collective-permute-start.9 = (bf16[32,1024]{1,0:T(8,128)(2,1)S(1)}, bf16[32,1024]{1,0:T(8,128)(2,1)S(1)}, u32[]{:S(2)}, u32[]{:S(2)}) collective-permute-start(bf16[32,1024]{1,0:T(8,128)(2,1)S(1)} %get-tuple-element.16.refs_0_), channel_id=1, source_target_pairs={{0,24},{4,28},{8,16},{12,20},{16,8},{20,12},{24,0},{28,4},{1,25},{... | collective-permute-start | bytes 196616 | tf_op jit(solution)/shard_map/ppermute | solution.py:181
  30.2 8.3 %collective-permute-start.7 = (bf16[32,1024]{1,0:T(8,128)(2,1)S(1)}, bf16[32,1024]{1,0:T(8,128)(2,1)S(1)}, u32[]{:S(2)}, u32[]{:S(2)}) collective-permute-start(bf16[32,1024]{1,0:T(8,128)(2,1)S(1)} %get-tuple-element.16.refs_0_), channel_id=1, source_target_pairs={{0,16},{4,20},{8,24},{12,28},{16,0},{20,4},{24,8},{28,12},{1,17},{... | collective-permute-start | bytes 196616 | tf_op jit(solution)/shard_map/ppermute | solution.py:181
  37.8 4.3 %collective-permute-start.5 = (bf16[32,1024]{1,0:T(8,128)(2,1)S(1)}, bf16[32,1024]{1,0:T(8,128)(2,1)S(1)}, u32[]{:S(2)}, u32[]{:S(2)}) collective-permute-start(bf16[32,1024]{1,0:T(8,128)(2,1)S(1)} %get-tuple-element.16.refs_0_), channel_id=1, source_target_pairs={{0,8},{4,12},{8,0},{12,4},{16,24},{20,28},{24,16},{28,20},{1,9},{5... | collective-permute-start | bytes 196616 | tf_op jit(solution)/shard_map/ppermute | solution.py:181
  38.5 3.6 %collective-permute-start.4 = (bf16[32,1024]{1,0:T(8,128)(2,1)S(1)}, bf16[32,1024]{1,0:T(8,128)(2,1)S(1)}, u32[]{:S(2)}, u32[]{:S(2)}) collective-permute-start(bf16[32,1024]{1,0:T(8,128)(2,1)S(1)} %get-tuple-element.16.refs_0_), channel_id=1, source_target_pairs={{0,4},{4,0},{8,12},{12,8},{16,20},{20,16},{24,28},{28,24},{1,5},{5... | collective-permute-start | bytes 196616 | tf_op jit(solution)/shard_map/ppermute | solution.py:181
  42.1 1.3 %collective-permute-start.10 = (bf16[32,1024]{1,0:T(8,128)(2,1)S(1)}, bf16[32,1024]{1,0:T(8,128)(2,1)S(1)}, u32[]{:S(2)}, u32[]{:S(2)}) collective-permute-start(bf16[32,1024]{1,0:T(8,128)(2,1)S(1)} %collective-permute-done.9.refs_6_), channel_id=1, source_target_pairs={{0,4},{4,0},{8,12},{12,8},{16,20},{20,16},{24,28},{28,24},{1,5},{5... | collective-permute-start | bytes 196616 | tf_op jit(solution)/shard_map/ppermute | solution.py:181
  42.1 7.8 %collective-permute-start.14 = (bf16[96,1024]{1,0:T(8,128)(2,1)S(1)}, bf16[96,1024]{1,0:T(8,128)(2,1)S(1)}, u32[]{:S(2)}, u32[]{:S(2)}) collective-permute-start(bf16[96,1024]{1,0:T(8,128)(2,1)S(1)} %constant_dynamic-update-slice_fusion.refs_0_), channel_id=1, source_target_pairs={{0,4},{4,0},{8,12},{12,8},{16,20},{20,16},{24,28},{28,24},{1,5},{5... | collective-permute-start | bytes 589832 | tf_op jit(solution)/shard_map/ppermute | solution.py:181
  42.6 7.3 %collective-permute-start.20 = (bf16[96,1024]{1,0:T(8,128)(2,1)S(1)}, bf16[96,1024]{1,0:T(8,128)(2,1)S(1)}, u32[]{:S(2)}, u32[]{:S(2)}) collective-permute-start(bf16[96,1024]{1,0:T(8,128)(2,1)S(1)} %collective-permute-done.19.refs_6_), channel_id=1, source_target_pairs={{0,4},{4,0},{8,12},{12,8},{16,20},{20,16},{24,28},{28,24},{1,5},{5... | collective-permute-start | bytes 589832 | tf_op jit(solution)/shard_map/ppermute | solution.py:181
  42.7 7.2 %collective-permute-start.18 = (bf16[96,1024]{1,0:T(8,128)(2,1)S(1)}, bf16[96,1024]{1,0:T(8,128)(2,1)S(1)}, u32[]{:S(2)}, u32[]{:S(2)}) collective-permute-start(bf16[96,1024]{1,0:T(8,128)(2,1)S(1)} %collective-permute-done.17.refs_4_), channel_id=1, source_target_pairs={{0,4},{4,0},{8,12},{12,8},{16,20},{20,16},{24,28},{28,24},{1,5},{5... | collective-permute-start | bytes 589832 | tf_op jit(solution)/shard_map/ppermute | solution.py:181
  43.1 6.8 %collective-permute-start.16 = (bf16[96,1024]{1,0:T(8,128)(2,1)S(1)}, bf16[96,1024]{1,0:T(8,128)(2,1)S(1)}, u32[]{:S(2)}, u32[]{:S(2)}) collective-permute-start(bf16[96,1024]{1,0:T(8,128)(2,1)S(1)} %collective-permute-done.15.refs_2_), channel_id=1, source_target_pairs={{0,4},{4,0},{8,12},{12,8},{16,20},{20,16},{24,28},{28,24},{1,5},{5... | collective-permute-start | bytes 589832 | tf_op jit(solution)/shard_map/ppermute | solution.py:181
  43.3 1.4 %collective-permute-start.8 = (bf16[32,1024]{1,0:T(8,128)(2,1)S(1)}, bf16[32,1024]{1,0:T(8,128)(2,1)S(1)}, u32[]{:S(2)}, u32[]{:S(2)}) collective-permute-start(bf16[32,1024]{1,0:T(8,128)(2,1)S(1)} %collective-permute-done.7.refs_4_), channel_id=1, source_target_pairs={{0,4},{4,0},{8,12},{12,8},{16,20},{20,16},{24,28},{28,24},{1,5},{5... | collective-permute-start | bytes 196616 | tf_op jit(solution)/shard_map/ppermute | solution.py:181
  44.7 1.3 %collective-permute-start.6 = (bf16[32,1024]{1,0:T(8,128)(2,1)S(1)}, bf16[32,1024]{1,0:T(8,128)(2,1)S(1)}, u32[]{:S(2)}, u32[]{:S(2)}) collective-permute-start(bf16[32,1024]{1,0:T(8,128)(2,1)S(1)} %collective-permute-done.5.refs_2_), channel_id=1, source_target_pairs={{0,4},{4,0},{8,12},{12,8},{16,20},{20,16},{24,28},{28,24},{1,5},{5... | collective-permute-start | bytes 196616 | tf_op jit(solution)/shard_map/ppermute | solution.py:181

commit v2 on v0

v2 whole, which is shorter than its diff:
```python
import functools

import jax
import jax.numpy as jnp
from jax import lax
from jax.experimental import pallas as pl
from jax.experimental.pallas import tpu as pltpu
from jax.sharding import PartitionSpec as P

BLOCK = 128
MIB = 1 << 20

outer_lr = 0.7
outer_mu = 0.9

HBM = pl.BlockSpec(memory_space=pltpu.HBM)
VMEM = pl.BlockSpec(memory_space=pltpu.VMEM)


def params(mib=8):
    return pltpu.CompilerParams(vmem_limit_bytes=mib * MIB)


def columns(chunk, width):
    return pl.ds(pl.multiple_of(chunk * width, width), width)


def decoded_block(base, replica):
    delta = base - replica.astype(jnp.float32)
    scale = jnp.max(jnp.abs(delta), axis=1, keepdims=True) + 1e-06
    code = (delta / scale).astype(jnp.bfloat16)
    return (code.astype(jnp.float32) * scale).astype(jnp.bfloat16)


def encode_kernel(flip, base_hbm, local_hbm, out_ref, base_ref, local_ref, sems):
    chips, rows, width = out_ref.shape
    me = lax.axis_index("rep")
    copies = []
    for j in range(chips):
        cols = columns(me ^ (flip ^ (2 * j)), width)
        pair = (
            pltpu.make_async_copy(base_hbm.at[:, cols], base_ref.at[j], sems.at[0, j]),
            pltpu.make_async_copy(local_hbm.at[0, :, cols], local_ref.at[j], sems.at[1, j]),
        )
        for copy in pair:
            copy.start()
        copies.append(pair)
    for j in range(chips):
        for copy in copies[j]:
            copy.wait()
        for b in range(width // BLOCK):
            cols = slice(b * BLOCK, (b + 1) * BLOCK)
            out_ref[j, :, cols] = decoded_block(base_ref[j, :, cols], local_ref[j, :, cols])


def encode(base, local, flip, chips, width):
    rows = base.shape[0]
    return pl.pallas_call(
        functools.partial(encode_kernel, flip),
        out_shape=jax.ShapeDtypeStruct((chips, rows, width), jnp.bfloat16),
        in_specs=[HBM, HBM],
        out_specs=VMEM,
        scratch_shapes=[
            pltpu.VMEM((chips, rows, width), jnp.float32),
            pltpu.VMEM((chips, rows, width), jnp.bfloat16),
            pltpu.SemaphoreType.DMA((2, chips)),
        ],
        compiler_params=params(),
    )(base, local)


def chip_sum_kernel(keep_ref, recv_ref, *out_refs):
    for j, out_ref in enumerate(out_refs):
        total = keep_ref[j].astype(jnp.float32) + recv_ref[j].astype(jnp.float32)
        out_ref[...] = total.astype(out_ref.dtype)


def chip_sum(keep, recv):
    chips, rows, width = keep.shape
    return pl.pallas_call(
        chip_sum_kernel,
        out_shape=[
            jax.ShapeDtypeStruct((rows, width), jnp.float32 if j == 0 else jnp.bfloat16)
            for j in range(chips)
        ],
        compiler_params=params(),
    )(keep, recv)


def stepped(average, base, momentum):
    moved = outer_mu * momentum + average
    return base - outer_lr * (average + outer_mu * moved), moved


def chunk_step_kernel(replicas, base_ref, mom_ref, own_ref, *refs):
    parts, (avg_ref, fresh_ref) = refs[:-2], refs[-2:]
    cols = columns(lax.axis_index("rep"), own_ref.shape[1])
    total = own_ref[...]
    for part in parts:
        total = total + part[...].astype(jnp.float32)
    average = (total / replicas).astype(jnp.bfloat16)
    avg_ref[...] = average
    new_base, _ = stepped(average.astype(jnp.float32), base_ref[:, cols], mom_ref[:, cols])
    fresh_ref[...] = new_base.astype(jnp.bfloat16)


def chunk_step(base, momentum, own, parts, replicas):
    return pl.pallas_call(
        functools.partial(chunk_step_kernel, replicas),
        out_shape=[jax.ShapeDtypeStruct(own.shape, jnp.bfloat16)] * 2,
        compiler_params=params(),
    )(base, momentum, own, *parts)


def outer_kernel(replicas, base_ref, mom_ref, *refs):
    firsts, (new_base_hbm, new_mom_hbm, fresh_ref) = refs[:replicas], refs[replicas:-3]
    new_base_ref, new_mom_ref, sems = refs[-3:]
    rows, width = fresh_ref.shape[1:]
    me = lax.axis_index("rep")
    copies = []
    for k, first in enumerate(firsts):
        cols = columns(me ^ k, width)
        average = first[:rows, :].astype(jnp.float32)
        new_base, moved = stepped(average, base_ref[:, cols], mom_ref[:, cols])
        new_base_ref[k] = new_base
        new_mom_ref[k] = moved
        fresh_ref[k] = new_base.astype(jnp.bfloat16)
        for which, (ref, hbm) in enumerate(
            ((new_base_ref, new_base_hbm), (new_mom_ref, new_mom_hbm))
        ):
            copy = pltpu.make_async_copy(ref.at[k], hbm.at[:, cols], sems.at[which, k])
            copy.start()
            copies.append(copy)
    for copy in copies:
        copy.wait()


def outer(base, momentum, firsts, width):
    rows = base.shape[0]
    replicas = len(firsts)
    return pl.pallas_call(
        functools.partial(outer_kernel, replicas),
        out_shape=[
            jax.ShapeDtypeStruct(base.shape, jnp.float32),
            jax.ShapeDtypeStruct(base.shape, jnp.float32),
            jax.ShapeDtypeStruct((replicas, rows, width), jnp.bfloat16),
        ],
        out_specs=[HBM, HBM, VMEM],
        scratch_shapes=[
            pltpu.VMEM((replicas, rows, width), jnp.float32),
            pltpu.VMEM((replicas, rows, width), jnp.float32),
            pltpu.SemaphoreType.DMA((2, replicas)),
        ],
        compiler_params=params(),
    )(base, momentum, *firsts)


def project_kernel(places, near, tok_ref, own_ref, *refs):
    count = len(places)
    firsts, seconds = refs[:count], refs[count : 2 * count]
    out_hbm, rhs_ref, out_ref, sems = refs[-4:]
    rows, width = own_ref.shape[1:]
    me, here = lax.axis_index("rep"), lax.axis_index("fsdp")

    def at(s):
        return pl.ds(pl.multiple_of((here ^ s) * rows, rows), rows)

    copies = []
    for i, k in enumerate(places):
        rhs_ref[i, at(0), :] = own_ref[k]
        for s in range(1, near + 1):
            rhs_ref[i, at(s), :] = firsts[i][s * rows : (s + 1) * rows, :]
        for s in range(seconds[i].shape[0] // rows):
            rhs_ref[i, at(s + near + 1), :] = seconds[i][s * rows : (s + 1) * rows, :]
        out_ref[i] = jnp.dot(
            tok_ref[...], rhs_ref[i], preferred_element_type=jnp.float32
        ).astype(out_ref.dtype)
        copy = pltpu.make_async_copy(
            out_ref.at[i], out_hbm.at[:, columns(me ^ k, width)], sems.at[i]
        )
        copy.start()
        copies.append(copy)
    for copy in copies:
        copy.wait()


def project(out, tokens, own, firsts, seconds, places, near):
    replicas, rows, width = own.shape
    tall, depth = tokens.shape
    count = len(places)
    args = [tokens, own] + [firsts[k] for k in places] + [seconds[k] for k in places]
    specs = [VMEM] * len(args)
    alias = {}
    if out is not None:
        alias = {len(args): 0}
        args.append(out)
        specs.append(HBM)
    return pl.pallas_call(
        functools.partial(project_kernel, places, near),
        out_shape=jax.ShapeDtypeStruct((tall, width * replicas), jnp.bfloat16),
        in_specs=specs,
        out_specs=HBM,
        input_output_aliases=alias,
        scratch_shapes=[
            pltpu.VMEM((count, depth, width), jnp.bfloat16),
            pltpu.VMEM((count, tall, width), jnp.bfloat16),
            pltpu.SemaphoreType.DMA((count,)),
        ],
        compiler_params=params(16),
    )(*args)


def swap(x, axis, flip):
    return lax.ppermute(x, axis, [(i, i ^ flip) for i in range(lax.axis_size(axis))])


def spread(own, chips):
    held = [own] + [swap(own, "rep", 2 * j) for j in range(1, chips)]
    return [x for a in held for x in (a, swap(a, "rep", 1))]


def on_device(base, local, momentum, tokens):
    replicas, groups = lax.axis_size("rep"), lax.axis_size("fsdp")
    chips = replicas // 2
    near = groups // 4
    width = base.shape[1] // replicas

    send = encode(base, local, 1, chips, width)
    recv = swap(send, "rep", 1)
    keep = encode(base, local, 0, chips, width)
    sums = chip_sum(keep, recv)
    parts = [swap(sums[j], "rep", 2 * j) for j in range(1, chips)]
    average, fresh = chunk_step(base, momentum, sums[0], parts, replicas)

    far = [swap(fresh, "fsdp", s) for s in range(1, groups)]
    firsts = spread(jnp.concatenate([average] + far[:near], axis=0), chips)
    seconds = spread(jnp.concatenate(far[near:], axis=0), chips)

    new_base, new_momentum, own = outer(base, momentum, firsts, width)
    projected = None
    for j in [0] + list(range(chips - 1, 0, -1)):
        projected = project(projected, tokens, own, firsts, seconds, (2 * j, 2 * j + 1), near)
    return new_base, new_momentum, projected


def solution(mesh):
    in_specs = (P("fsdp", None), P("rep", "fsdp", None), P("fsdp", None), P(("rep", "fsdp"), None))
    out_specs = (P("fsdp", None), P("fsdp", None), P(("rep", "fsdp"), None))
    return jax.shard_map(
        on_device, mesh=mesh, in_specs=in_specs, out_specs=out_specs, check_vma=False
    )
```

time: 136 us -> 40.8 us (0.30)
  waiting for transfers between devices: 103 us -> 11 us
  starting transfers between devices: 0.08 us -> 17.9 us
  between operations: 14.1 us -> 0.77 us
  Pallas kernels: 0 us -> 8.55 us
  other arithmetic: 6.84 us -> 0 us
  matrix products: 4.81 us -> 0 us
  local copies, waits for them, and re-layouts: 6.85 us -> 2.29 us
    psum x1 -> x0, waiting for transfers between devices: 57.3 us -> none  [on_device(): lax.psum(decode(codes, scales).astype(jnp.bfloat16), 'rep')]
    all_gather x1 -> x0, waiting for transfers between devices: 45.4 us -> none  [on_device(): all_rows = lax.all_gather(fresh, 'fsdp', axis=0, tiled=True)]
    ppermute x0 -> x21, starting transfers between devices: none -> 17.9 us  [swap(): lax.ppermute(x, axis, [(i, i ^ flip) for i in range(lax.axis_size(axis))])]
    ppermute x0 -> x21, waiting for transfers between devices: none -> 11 us  [swap(): lax.ppermute(x, axis, [(i, i ^ flip) for i in range(lax.axis_size(axis))])]
    pallas_call x0 -> x9, Pallas kernels: none -> 8.55 us  [the longest x4 5.27 us: project(): pl.pallas_call(functools.partial(project_kernel, places, near), out_shape...]
    convert_element_type x3 -> x0, other arithmetic: 4.91 us -> none  [the longest x1 2.81 us: on_device(): fresh = new_base.astype(jnp.bfloat16)]
    dot_general x1 -> x0, matrix products: 4.81 us -> none  [on_device(): projected = jnp.dot(tokens, all_rows, preferred_element_type=jnp.float32)]
    unnamed x10 -> x12, local copies, waits for them, and re-layouts: 6.53 us -> 2.28 us
  transfers between devices with their start and end apart: 2 -> 21, of which waited for: 2 -> 9; matrix products, arithmetic and copies ran while one was open for 0% -> 0% of each run, Pallas kernels for 0% -> 15%
where the time goes in v2:
time: 40.8 us; the launch traced here: 40.6 us
  starting transfers between devices  17.9 us (44%)
  waiting for transfers between devices  11 us (27%)
  Pallas kernels  8.55 us (21%)
  local copies, waits for them, and re-layouts  2.29 us (6%)
  between operations  0.77 us (2%)
    ppermute x21, starting transfers between devices, swap(): lax.ppermute(x, axis, [(i, i ^ flip) for i in range(lax.axis_size(axis))])  17.9 us
    ppermute x21, waiting for transfers between devices, swap(): lax.ppermute(x, axis, [(i, i ^ flip) for i in range(lax.axis_size(axis))])  11 us
    pallas_call x4, Pallas kernels, project(): pl.pallas_call(functools.partial(project_kernel, places, near), out_shape...  5.27 us
    unnamed x12, local copies, waits for them, and re-layouts  2.28 us
    pallas_call x2, Pallas kernels, encode(): pl.pallas_call(functools.partial(encode_kernel, flip), out_shape=jax.Shap...  1.66 us
    pallas_call x1, Pallas kernels, outer(): pl.pallas_call(functools.partial(outer_kernel, replicas), out_shape=[jax....  1.48 us
  transfers between devices with their start and end apart: 21, of which 9 were waited for; matrix products, arithmetic and copies ran while one was open for 0% of the time, Pallas kernels for 15%

profile of v2, /device:TPU:0, one launch (start us, length us, event | category | flops | bytes accessed | tf_op | source)
XLA Modules:
  0.0 40.6 jit_solution(12670353177723984125)
XLA Ops:
  0.6 1.2 %copy-done = f32[32,8192]{1,0:T(8,128)S(1)} copy-done((f32[32,8192]{1,0:T(8,128)S(1)}, f32[32,8192]{1,0:T(8,128)}, u32[]{:S(2)}) %copy-start) | copy-done | bytes 1048600
  1.9 1.0 %copy-done.3 = bf16[1,32,8192]{2,1,0:T(8,128)(2,1)S(1)} copy-done((bf16[1,32,8192]{2,1,0:T(8,128)(2,1)S(1)}, bf16[1,32,8192]{2,1,0:T(8,128)(2,1)}, u32[]{:S(2)}) %copy-start.3) | copy-done | bytes 524312
  2.9 0.8 %shard_map.68 = bf16[4,32,1024]{2,1,0:T(8,128)(2,1)S(1)} custom-call(f32[32,8192]{1,0:T(8,128)S(1)} %copy-done, bf16[1,32,8192]{2,1,0:T(8,128)(2,1)S(1)} %copy-done.3), custom_call_target="tpu_custom_call" | custom-call | tf_op jit(solution)/shard_map/pallas_call | solution.py:58
  3.8 0.5 %collective-permute-start = (bf16[4,32,1024]{2,1,0:T(8,128)(2,1)S(1)}, bf16[4,32,1024]{2,1,0:T(8,128)(2,1)S(1)}, u32[]{:S(2)}, u32[]{:S(2)}) collective-permute-start(bf16[4,32,1024]{2,1,0:T(8,128)(2,1)S(1)} %shard_map.68), channel_id=1, source_target_pairs={{0,4},{4,0},{8,12},{12,8},{16,20},{20,16},{24,28},{28,24},{1,5},{5... | collective-permute-start | bytes 786440 | tf_op jit(solution)/shard_map/ppermute | solution.py:214
  4.3 0.8 %shard_map.67.keep_ref = bf16[4,32,1024]{2,1,0:T(8,128)(2,1)S(1)} custom-call(f32[32,8192]{1,0:T(8,128)S(1)} %copy-done, bf16[1,32,8192]{2,1,0:T(8,128)(2,1)S(1)} %copy-done.3), custom_call_target="tpu_custom_call" | custom-call | tf_op jit(solution)/shard_map/pallas_call | solution.py:58
  5.1 0.3 collective-permute-done.recv_ref
  5.5 2.9 %collective-permute-start.1 = (bf16[32,1024]{1,0:T(8,128)(2,1)S(1)}, bf16[32,1024]{1,0:T(8,128)(2,1)S(1)}, u32[]{:S(2)}, u32[]{:S(2)}) collective-permute-start(bf16[32,1024]{1,0:T(8,128)(2,1)S(1)} %get-tuple-element.13), channel_id=1, source_target_pairs={{0,8},{4,12},{8,0},{12,4},{16,24},{20,28},{24,16},{28,20},{1,9},{5... | collective-permute-start | bytes 196616 | tf_op jit(solution)/shard_map/ppermute | solution.py:214
  8.4 1.5 %collective-permute-start.2 = (bf16[32,1024]{1,0:T(8,128)(2,1)S(1)}, bf16[32,1024]{1,0:T(8,128)(2,1)S(1)}, u32[]{:S(2)}, u32[]{:S(2)}) collective-permute-start(bf16[32,1024]{1,0:T(8,128)(2,1)S(1)} %get-tuple-element.14), channel_id=1, source_target_pairs={{0,16},{4,20},{8,24},{12,28},{16,0},{20,4},{24,8},{28,12},{1,17},{... | collective-permute-start | bytes 196616 | tf_op jit(solution)/shard_map/ppermute | solution.py:214
  10.0 0.9 %collective-permute-done.1.refs_0_ = bf16[32,1024]{1,0:T(8,128)(2,1)S(1)} collective-permute-done((bf16[32,1024]{1,0:T(8,128)(2,1)S(1)}, bf16[32,1024]{1,0:T(8,128)(2,1)S(1)}, u32[]{:S(2)}, u32[]{:S(2)}) %collective-permute-start.1) | collective-permute-done | bytes 65568 | tf_op jit(solution)/shard_map/ppermute | solution.py:214
  10.8 1.9 %collective-permute-done.2.refs_1_ = bf16[32,1024]{1,0:T(8,128)(2,1)S(1)} collective-permute-done((bf16[32,1024]{1,0:T(8,128)(2,1)S(1)}, bf16[32,1024]{1,0:T(8,128)(2,1)S(1)}, u32[]{:S(2)}, u32[]{:S(2)}) %collective-permute-start.2) | collective-permute-done | bytes 65568 | tf_op jit(solution)/shard_map/ppermute | solution.py:214
  12.7 2.4 %collective-permute-done.3.refs_2_ = bf16[32,1024]{1,0:T(8,128)(2,1)S(1)} collective-permute-done((bf16[32,1024]{1,0:T(8,128)(2,1)S(1)}, bf16[32,1024]{1,0:T(8,128)(2,1)S(1)}, u32[]{:S(2)}, u32[]{:S(2)}) %collective-permute-start.3) | collective-permute-done | bytes 65568 | tf_op jit(solution)/shard_map/ppermute | solution.py:214
  15.2 1.6 %collective-permute-start.4 = (bf16[32,1024]{1,0:T(8,128)(2,1)S(1)}, bf16[32,1024]{1,0:T(8,128)(2,1)S(1)}, u32[]{:S(2)}, u32[]{:S(2)}) collective-permute-start(bf16[32,1024]{1,0:T(8,128)(2,1)S(1)} %get-tuple-element.17), channel_id=1, source_target_pairs={{0,1},{1,0},{2,3},{3,2},{4,5},{5,4},{6,7},{7,6},{8,9},{9,8},{10,11... | collective-permute-start | bytes 196616 | tf_op jit(solution)/shard_map/ppermute | solution.py:214
  16.8 2.6 %collective-permute-start.12 = (bf16[32,1024]{1,0:T(8,128)(2,1)S(1)}, bf16[32,1024]{1,0:T(8,128)(2,1)S(1)}, u32[]{:S(2)}, u32[]{:S(2)}) collective-permute-start(bf16[32,1024]{1,0:T(8,128)(2,1)S(1)} %get-tuple-element.17), channel_id=1, source_target_pairs={{0,2},{1,3},{2,0},{3,1},{4,6},{5,7},{6,4},{7,5},{8,10},{9,11},{10,... | collective-permute-start | bytes 196616 | tf_op jit(solution)/shard_map/ppermute | solution.py:214
  19.4 0.2 collective-permute-start.13
  19.7 0.2 collective-permute-done.4
  19.8 0.6 %collective-permute-start.10 = (bf16[64,1024]{1,0:T(8,128)(2,1)S(1)}, bf16[64,1024]{1,0:T(8,128)(2,1)S(1)}, u32[]{:S(2)}, u32[]{:S(2)}) collective-permute-start(bf16[64,1024]{1,0:T(8,128)(2,1)S(1)} %constant_dynamic-update-slice_fusion.refs_0_), channel_id=1, source_target_pairs={{0,24},{4,28},{8,16},{12,20},{16,8},{20,12},{24,0},{28,4},{1,25},{... | collective-permute-start | bytes 393224 | tf_op jit(solution)/shard_map/ppermute | solution.py:214
  20.4 1.4 %collective-permute-start.6 = (bf16[64,1024]{1,0:T(8,128)(2,1)S(1)}, bf16[64,1024]{1,0:T(8,128)(2,1)S(1)}, u32[]{:S(2)}, u32[]{:S(2)}) collective-permute-start(bf16[64,1024]{1,0:T(8,128)(2,1)S(1)} %constant_dynamic-update-slice_fusion.refs_0_), channel_id=1, source_target_pairs={{0,8},{4,12},{8,0},{12,4},{16,24},{20,28},{24,16},{28,20},{1,9},{5... | collective-permute-start | bytes 393224 | tf_op jit(solution)/shard_map/ppermute | solution.py:214
  21.9 1.4 %collective-permute-start.8 = (bf16[64,1024]{1,0:T(8,128)(2,1)S(1)}, bf16[64,1024]{1,0:T(8,128)(2,1)S(1)}, u32[]{:S(2)}, u32[]{:S(2)}) collective-permute-start(bf16[64,1024]{1,0:T(8,128)(2,1)S(1)} %constant_dynamic-update-slice_fusion.refs_0_), channel_id=1, source_target_pairs={{0,16},{4,20},{8,24},{12,28},{16,0},{20,4},{24,8},{28,12},{1,17},{... | collective-permute-start | bytes 393224 | tf_op jit(solution)/shard_map/ppermute | solution.py:214
  23.4 2.1 %collective-permute-done.13 = bf16[32,1024]{1,0:T(8,128)(2,1)S(1)} collective-permute-done((bf16[32,1024]{1,0:T(8,128)(2,1)S(1)}, bf16[32,1024]{1,0:T(8,128)(2,1)S(1)}, u32[]{:S(2)}, u32[]{:S(2)}) %collective-permute-start.13) | collective-permute-done | bytes 65568 | tf_op jit(solution)/shard_map/ppermute | solution.py:214
  25.5 0.5 %collective-permute-start.18 = (bf16[64,1024]{1,0:T(8,128)(2,1)S(1)}, bf16[64,1024]{1,0:T(8,128)(2,1)S(1)}, u32[]{:S(2)}, u32[]{:S(2)}) collective-permute-start(bf16[64,1024]{1,0:T(8,128)(2,1)S(1)} %constant_dynamic-update-slice_fusion.2.refs_2_), channel_id=1, source_target_pairs={{0,24},{4,28},{8,16},{12,20},{16,8},{20,12},{24,0},{28,4},{1,25},{... | collective-permute-start | bytes 393224 | tf_op jit(solution)/shard_map/ppermute | solution.py:214
  26.0 1.5 %collective-permute-start.16 = (bf16[64,1024]{1,0:T(8,128)(2,1)S(1)}, bf16[64,1024]{1,0:T(8,128)(2,1)S(1)}, u32[]{:S(2)}, u32[]{:S(2)}) collective-permute-start(bf16[64,1024]{1,0:T(8,128)(2,1)S(1)} %constant_dynamic-update-slice_fusion.2.refs_2_), channel_id=1, source_target_pairs={{0,16},{4,20},{8,24},{12,28},{16,0},{20,4},{24,8},{28,12},{1,17},{... | collective-permute-start | bytes 393224 | tf_op jit(solution)/shard_map/ppermute | solution.py:214
  27.5 1.5 %collective-permute-start.14 = (bf16[64,1024]{1,0:T(8,128)(2,1)S(1)}, bf16[64,1024]{1,0:T(8,128)(2,1)S(1)}, u32[]{:S(2)}, u32[]{:S(2)}) collective-permute-start(bf16[64,1024]{1,0:T(8,128)(2,1)S(1)} %constant_dynamic-update-slice_fusion.2.refs_2_), channel_id=1, source_target_pairs={{0,8},{4,12},{8,0},{12,4},{16,24},{20,28},{24,16},{28,20},{1,9},{5... | collective-permute-start | bytes 393224 | tf_op jit(solution)/shard_map/ppermute | solution.py:214
  29.0 0.5 %collective-permute-start.7 = (bf16[64,1024]{1,0:T(8,128)(2,1)S(1)}, bf16[64,1024]{1,0:T(8,128)(2,1)S(1)}, u32[]{:S(2)}, u32[]{:S(2)}) collective-permute-start(bf16[64,1024]{1,0:T(8,128)(2,1)S(1)} %collective-permute-done.6.refs_2_.refs_0_), channel_id=1, source_target_pairs={{0,4},{4,0},{8,12},{12,8},{16,20},{20,16},{24,28},{28,24},{1,5},{5... | collective-permute-start | bytes 393224 | tf_op jit(solution)/shard_map/ppermute | solution.py:214
  29.5 2.4 %collective-permute-done.18.refs_2_ = bf16[64,1024]{1,0:T(8,128)(2,1)S(1)} collective-permute-done((bf16[64,1024]{1,0:T(8,128)(2,1)S(1)}, bf16[64,1024]{1,0:T(8,128)(2,1)S(1)}, u32[]{:S(2)}, u32[]{:S(2)}) %collective-permute-start.18) | collective-permute-done | bytes 131104 | tf_op jit(solution)/shard_map/ppermute | solution.py:214
  31.9 0.8 %collective-permute-done.16.refs_2_ = bf16[64,1024]{1,0:T(8,128)(2,1)S(1)} collective-permute-done((bf16[64,1024]{1,0:T(8,128)(2,1)S(1)}, bf16[64,1024]{1,0:T(8,128)(2,1)S(1)}, u32[]{:S(2)}, u32[]{:S(2)}) %collective-permute-start.16) | collective-permute-done | bytes 131104 | tf_op jit(solution)/shard_map/ppermute | solution.py:214
  32.7 0.5 %collective-permute-start.19 = (bf16[64,1024]{1,0:T(8,128)(2,1)S(1)}, bf16[64,1024]{1,0:T(8,128)(2,1)S(1)}, u32[]{:S(2)}, u32[]{:S(2)}) collective-permute-start(bf16[64,1024]{1,0:T(8,128)(2,1)S(1)} %collective-permute-done.18.refs_2_), channel_id=1, source_target_pairs={{0,4},{4,0},{8,12},{12,8},{16,20},{20,16},{24,28},{28,24},{1,5},{5... | collective-permute-start | bytes 393224 | tf_op jit(solution)/shard_map/ppermute | solution.py:214
  33.3 0.4 %collective-permute-start.15 = (bf16[64,1024]{1,0:T(8,128)(2,1)S(1)}, bf16[64,1024]{1,0:T(8,128)(2,1)S(1)}, u32[]{:S(2)}, u32[]{:S(2)}) collective-permute-start(bf16[64,1024]{1,0:T(8,128)(2,1)S(1)} %collective-permute-done.14.refs_2_), channel_id=1, source_target_pairs={{0,4},{4,0},{8,12},{12,8},{16,20},{20,16},{24,28},{28,24},{1,5},{5... | collective-permute-start | bytes 393224 | tf_op jit(solution)/shard_map/ppermute | solution.py:214
  33.7 1.5 %shard_map.71 = (f32[32,8192]{1,0:T(8,128)}, f32[32,8192]{1,0:T(8,128)}, bf16[8,32,1024]{2,1,0:T(8,128)(2,1)S(1)}) custom-call(f32[32,8192]{1,0:T(8,128)S(1)} %copy-done.1, f32[32,8192]{1,0:T(8,128)S(1)} %copy-done.2, bf16[64,1024]{1,0:T(8,128)(2,1)S(1)} %constant_dynamic-update-slice_fusion.refs_0_, bf16[64,1024]{1,0:T(8,128)(2,1)S(1)} %collective-permute-done.5.refs_1_, ...), custom_call_target="tpu_custom_call" | custom-call | tf_op jit(solution)/shard_map/pallas_call | solution.py:141
  35.3 1.3 %shard_map.72.refs_4_ = bf16[256,8192]{1,0:T(8,128)(2,1)} custom-call(bf16[256,128]{1,0:T(8,128)(2,1)S(1)} %copy-done.4, bf16[8,32,1024]{2,1,0:T(8,128)(2,1)S(1)} %get-tuple-element.20.own_ref, bf16[64,1024]{1,0:T(8,128)(2,1)S(1)} %constant_dynamic-update-slice_fusion.refs_0_, bf16[64,1024]{1,0:T(8,128)(2,1)S(1)} %collective-permute-done.5.refs_1_, ...), custom_call_target="tpu_custom_call" | custom-call | tf_op jit(solution)/shard_map/pallas_call | solution.py:198
  36.6 1.3 %shard_map.73.refs_4_ = bf16[256,8192]{1,0:T(8,128)(2,1)} custom-call(bf16[256,128]{1,0:T(8,128)(2,1)S(1)} %copy-done.4, bf16[8,32,1024]{2,1,0:T(8,128)(2,1)S(1)} %get-tuple-element.20.own_ref, bf16[64,1024]{1,0:T(8,128)(2,1)S(1)} %collective-permute-done.10.refs_6_.refs_0_, ...), custom_call_target="tpu_custom_call", output_to_operand_aliasing={{}: (6, {})} | custom-call | tf_op jit(solution)/shard_map/pallas_call | solution.py:198
  37.9 1.3 %shard_map.74.refs_4_ = bf16[256,8192]{1,0:T(8,128)(2,1)} custom-call(bf16[256,128]{1,0:T(8,128)(2,1)S(1)} %copy-done.4, bf16[8,32,1024]{2,1,0:T(8,128)(2,1)S(1)} %get-tuple-element.20.own_ref, bf16[64,1024]{1,0:T(8,128)(2,1)S(1)} %collective-permute-done.8.refs_4_.refs_0_, ...), custom_call_target="tpu_custom_call", output_to_operand_aliasing={{}: (6, {})} | custom-call | tf_op jit(solution)/shard_map/pallas_call | solution.py:198
  39.3 1.3 %shard_map.75 = bf16[256,8192]{1,0:T(8,128)(2,1)} custom-call(bf16[256,128]{1,0:T(8,128)(2,1)S(1)} %copy-done.4, bf16[8,32,1024]{2,1,0:T(8,128)(2,1)S(1)} %get-tuple-element.20.own_ref, bf16[64,1024]{1,0:T(8,128)(2,1)S(1)} %collective-permute-done.6.refs_2_.refs_0_, ...), custom_call_target="tpu_custom_call", output_to_operand_aliasing={{}: (6, {})} | custom-call | tf_op jit(solution)/shard_map/pallas_call | solution.py:198
  (33 shorter events, 0.4 us)
Async XLA Ops:
  0.6 1.2 %copy-start = (f32[32,8192]{1,0:T(8,128)S(1)}, f32[32,8192]{1,0:T(8,128)}, u32[]{:S(2)}) copy-start(f32[32,8192]{1,0:T(8,128)} %base_ref.3) | copy-start | bytes 3145732
  1.9 1.0 %copy-start.3 = (bf16[1,32,8192]{2,1,0:T(8,128)(2,1)S(1)}, bf16[1,32,8192]{2,1,0:T(8,128)(2,1)}, u32[]{:S(2)}) copy-start(bf16[1,32,8192]{2,1,0:T(8,128)(2,1)} %local_hbm.3) | copy-start | bytes 1572868
  2.9 12.2 %copy-start.1 = (f32[32,8192]{1,0:T(8,128)S(1)}, f32[32,8192]{1,0:T(8,128)}, u32[]{:S(2)}) copy-start(f32[32,8192]{1,0:T(8,128)} %base_ref.3) | copy-start | bytes 3145732
  2.9 12.2 %copy-start.2 = (f32[32,8192]{1,0:T(8,128)S(1)}, f32[32,8192]{1,0:T(8,128)}, u32[]{:S(2)}) copy-start(f32[32,8192]{1,0:T(8,128)} %mom_ref.3) | copy-start | bytes 3145732
  3.7 31.5 %copy-start.4 = (bf16[256,128]{1,0:T(8,128)(2,1)S(1)}, bf16[256,128]{1,0:T(8,128)(2,1)}, u32[]{:S(2)}) copy-start(bf16[256,128]{1,0:T(8,128)(2,1)} %tok_ref.7) | copy-start | bytes 196612
  3.8 1.7 %collective-permute-start = (bf16[4,32,1024]{2,1,0:T(8,128)(2,1)S(1)}, bf16[4,32,1024]{2,1,0:T(8,128)(2,1)S(1)}, u32[]{:S(2)}, u32[]{:S(2)}) collective-permute-start(bf16[4,32,1024]{2,1,0:T(8,128)(2,1)S(1)} %shard_map.68), channel_id=1, source_target_pairs={{0,4},{4,0},{8,12},{12,8},{16,20},{20,16},{24,28},{28,24},{1,5},{5... | collective-permute-start | bytes 786440 | tf_op jit(solution)/shard_map/ppermute | solution.py:214
  5.5 5.3 %collective-permute-start.1 = (bf16[32,1024]{1,0:T(8,128)(2,1)S(1)}, bf16[32,1024]{1,0:T(8,128)(2,1)S(1)}, u32[]{:S(2)}, u32[]{:S(2)}) collective-permute-start(bf16[32,1024]{1,0:T(8,128)(2,1)S(1)} %get-tuple-element.13), channel_id=1, source_target_pairs={{0,8},{4,12},{8,0},{12,4},{16,24},{20,28},{24,16},{28,20},{1,9},{5... | collective-permute-start | bytes 196616 | tf_op jit(solution)/shard_map/ppermute | solution.py:214
  8.4 4.3 %collective-permute-start.2 = (bf16[32,1024]{1,0:T(8,128)(2,1)S(1)}, bf16[32,1024]{1,0:T(8,128)(2,1)S(1)}, u32[]{:S(2)}, u32[]{:S(2)}) collective-permute-start(bf16[32,1024]{1,0:T(8,128)(2,1)S(1)} %get-tuple-element.14), channel_id=1, source_target_pairs={{0,16},{4,20},{8,24},{12,28},{16,0},{20,4},{24,8},{28,12},{1,17},{... | collective-permute-start | bytes 196616 | tf_op jit(solution)/shard_map/ppermute | solution.py:214
  9.9 5.2 %collective-permute-start.3 = (bf16[32,1024]{1,0:T(8,128)(2,1)S(1)}, bf16[32,1024]{1,0:T(8,128)(2,1)S(1)}, u32[]{:S(2)}, u32[]{:S(2)}) collective-permute-start(bf16[32,1024]{1,0:T(8,128)(2,1)S(1)} %get-tuple-element.15), channel_id=1, source_target_pairs={{0,24},{4,28},{8,16},{12,20},{16,8},{20,12},{24,0},{28,4},{1,25},{... | collective-permute-start | bytes 196616 | tf_op jit(solution)/shard_map/ppermute | solution.py:214
  15.2 4.6 %collective-permute-start.4 = (bf16[32,1024]{1,0:T(8,128)(2,1)S(1)}, bf16[32,1024]{1,0:T(8,128)(2,1)S(1)}, u32[]{:S(2)}, u32[]{:S(2)}) collective-permute-start(bf16[32,1024]{1,0:T(8,128)(2,1)S(1)} %get-tuple-element.17), channel_id=1, source_target_pairs={{0,1},{1,0},{2,3},{3,2},{4,5},{5,4},{6,7},{7,6},{8,9},{9,8},{10,11... | collective-permute-start | bytes 196616 | tf_op jit(solution)/shard_map/ppermute | solution.py:214
  16.8 6.6 %collective-permute-start.12 = (bf16[32,1024]{1,0:T(8,128)(2,1)S(1)}, bf16[32,1024]{1,0:T(8,128)(2,1)S(1)}, u32[]{:S(2)}, u32[]{:S(2)}) collective-permute-start(bf16[32,1024]{1,0:T(8,128)(2,1)S(1)} %get-tuple-element.17), channel_id=1, source_target_pairs={{0,2},{1,3},{2,0},{3,1},{4,6},{5,7},{6,4},{7,5},{8,10},{9,11},{10,... | collective-permute-start | bytes 196616 | tf_op jit(solution)/shard_map/ppermute | solution.py:214
  19.4 6.1 %collective-permute-start.13 = (bf16[32,1024]{1,0:T(8,128)(2,1)S(1)}, bf16[32,1024]{1,0:T(8,128)(2,1)S(1)}, u32[]{:S(2)}, u32[]{:S(2)}) collective-permute-start(bf16[32,1024]{1,0:T(8,128)(2,1)S(1)} %get-tuple-element.17), channel_id=1, source_target_pairs={{0,3},{1,2},{2,1},{3,0},{4,7},{5,6},{6,5},{7,4},{8,11},{9,10},{10,... | collective-permute-start | bytes 196616 | tf_op jit(solution)/shard_map/ppermute | solution.py:214
  19.8 6.2 %collective-permute-start.10 = (bf16[64,1024]{1,0:T(8,128)(2,1)S(1)}, bf16[64,1024]{1,0:T(8,128)(2,1)S(1)}, u32[]{:S(2)}, u32[]{:S(2)}) collective-permute-start(bf16[64,1024]{1,0:T(8,128)(2,1)S(1)} %constant_dynamic-update-slice_fusion.refs_0_), channel_id=1, source_target_pairs={{0,24},{4,28},{8,16},{12,20},{16,8},{20,12},{24,0},{28,4},{1,25},{... | collective-permute-start | bytes 393224 | tf_op jit(solution)/shard_map/ppermute | solution.py:214
  20.4 7.0 %collective-permute-start.6 = (bf16[64,1024]{1,0:T(8,128)(2,1)S(1)}, bf16[64,1024]{1,0:T(8,128)(2,1)S(1)}, u32[]{:S(2)}, u32[]{:S(2)}) collective-permute-start(bf16[64,1024]{1,0:T(8,128)(2,1)S(1)} %constant_dynamic-update-slice_fusion.refs_0_), channel_id=1, source_target_pairs={{0,8},{4,12},{8,0},{12,4},{16,24},{20,28},{24,16},{28,20},{1,9},{5... | collective-permute-start | bytes 393224 | tf_op jit(solution)/shard_map/ppermute | solution.py:214
  21.9 7.1 %collective-permute-start.8 = (bf16[64,1024]{1,0:T(8,128)(2,1)S(1)}, bf16[64,1024]{1,0:T(8,128)(2,1)S(1)}, u32[]{:S(2)}, u32[]{:S(2)}) collective-permute-start(bf16[64,1024]{1,0:T(8,128)(2,1)S(1)} %constant_dynamic-update-slice_fusion.refs_0_), channel_id=1, source_target_pairs={{0,16},{4,20},{8,24},{12,28},{16,0},{20,4},{24,8},{28,12},{1,17},{... | collective-permute-start | bytes 393224 | tf_op jit(solution)/shard_map/ppermute | solution.py:214
  23.4 5.6 %collective-permute-start.5 = (bf16[64,1024]{1,0:T(8,128)(2,1)S(1)}, bf16[64,1024]{1,0:T(8,128)(2,1)S(1)}, u32[]{:S(2)}, u32[]{:S(2)}) collective-permute-start(bf16[64,1024]{1,0:T(8,128)(2,1)S(1)} %constant_dynamic-update-slice_fusion.refs_0_), channel_id=1, source_target_pairs={{0,4},{4,0},{8,12},{12,8},{16,20},{20,16},{24,28},{28,24},{1,5},{5... | collective-permute-start | bytes 393224 | tf_op jit(solution)/shard_map/ppermute | solution.py:214
  25.5 6.4 %collective-permute-start.18 = (bf16[64,1024]{1,0:T(8,128)(2,1)S(1)}, bf16[64,1024]{1,0:T(8,128)(2,1)S(1)}, u32[]{:S(2)}, u32[]{:S(2)}) collective-permute-start(bf16[64,1024]{1,0:T(8,128)(2,1)S(1)} %constant_dynamic-update-slice_fusion.2.refs_2_), channel_id=1, source_target_pairs={{0,24},{4,28},{8,16},{12,20},{16,8},{20,12},{24,0},{28,4},{1,25},{... | collective-permute-start | bytes 393224 | tf_op jit(solution)/shard_map/ppermute | solution.py:214
  26.0 6.7 %collective-permute-start.16 = (bf16[64,1024]{1,0:T(8,128)(2,1)S(1)}, bf16[64,1024]{1,0:T(8,128)(2,1)S(1)}, u32[]{:S(2)}, u32[]{:S(2)}) collective-permute-start(bf16[64,1024]{1,0:T(8,128)(2,1)S(1)} %constant_dynamic-update-slice_fusion.2.refs_2_), channel_id=1, source_target_pairs={{0,16},{4,20},{8,24},{12,28},{16,0},{20,4},{24,8},{28,12},{1,17},{... | collective-permute-start | bytes 393224 | tf_op jit(solution)/shard_map/ppermute | solution.py:214
  27.5 5.2 %collective-permute-start.14 = (bf16[64,1024]{1,0:T(8,128)(2,1)S(1)}, bf16[64,1024]{1,0:T(8,128)(2,1)S(1)}, u32[]{:S(2)}, u32[]{:S(2)}) collective-permute-start(bf16[64,1024]{1,0:T(8,128)(2,1)S(1)} %constant_dynamic-update-slice_fusion.2.refs_2_), channel_id=1, source_target_pairs={{0,8},{4,12},{8,0},{12,4},{16,24},{20,28},{24,16},{28,20},{1,9},{5... | collective-permute-start | bytes 393224 | tf_op jit(solution)/shard_map/ppermute | solution.py:214
  29.0 4.2 %collective-permute-start.11 = (bf16[64,1024]{1,0:T(8,128)(2,1)S(1)}, bf16[64,1024]{1,0:T(8,128)(2,1)S(1)}, u32[]{:S(2)}, u32[]{:S(2)}) collective-permute-start(bf16[64,1024]{1,0:T(8,128)(2,1)S(1)} %collective-permute-done.10.refs_6_.refs_0_), channel_id=1, source_target_pairs={{0,4},{4,0},{8,12},{12,8},{16,20},{20,16},{24,28},{28,24},{1,5},{5... | collective-permute-start | bytes 393224 | tf_op jit(solution)/shard_map/ppermute | solution.py:214
  29.0 4.3 %collective-permute-start.7 = (bf16[64,1024]{1,0:T(8,128)(2,1)S(1)}, bf16[64,1024]{1,0:T(8,128)(2,1)S(1)}, u32[]{:S(2)}, u32[]{:S(2)}) collective-permute-start(bf16[64,1024]{1,0:T(8,128)(2,1)S(1)} %collective-permute-done.6.refs_2_.refs_0_), channel_id=1, source_target_pairs={{0,4},{4,0},{8,12},{12,8},{16,20},{20,16},{24,28},{28,24},{1,5},{5... | collective-permute-start | bytes 393224 | tf_op jit(solution)/shard_map/ppermute | solution.py:214
  31.9 1.9 %collective-permute-start.9 = (bf16[64,1024]{1,0:T(8,128)(2,1)S(1)}, bf16[64,1024]{1,0:T(8,128)(2,1)S(1)}, u32[]{:S(2)}, u32[]{:S(2)}) collective-permute-start(bf16[64,1024]{1,0:T(8,128)(2,1)S(1)} %collective-permute-done.8.refs_4_.refs_0_), channel_id=1, source_target_pairs={{0,4},{4,0},{8,12},{12,8},{16,20},{20,16},{24,28},{28,24},{1,5},{5... | collective-permute-start | bytes 393224 | tf_op jit(solution)/shard_map/ppermute | solution.py:214
  32.7 2.5 %collective-permute-start.20 = (bf16[64,1024]{1,0:T(8,128)(2,1)S(1)}, bf16[64,1024]{1,0:T(8,128)(2,1)S(1)}, u32[]{:S(2)}, u32[]{:S(2)}) collective-permute-start(bf16[64,1024]{1,0:T(8,128)(2,1)S(1)} %constant_dynamic-update-slice_fusion.2.refs_2_), channel_id=1, source_target_pairs={{0,4},{4,0},{8,12},{12,8},{16,20},{20,16},{24,28},{28,24},{1,5},{5... | collective-permute-start | bytes 393224 | tf_op jit(solution)/shard_map/ppermute | solution.py:214
  32.7 3.9 %collective-permute-start.19 = (bf16[64,1024]{1,0:T(8,128)(2,1)S(1)}, bf16[64,1024]{1,0:T(8,128)(2,1)S(1)}, u32[]{:S(2)}, u32[]{:S(2)}) collective-permute-start(bf16[64,1024]{1,0:T(8,128)(2,1)S(1)} %collective-permute-done.18.refs_2_), channel_id=1, source_target_pairs={{0,4},{4,0},{8,12},{12,8},{16,20},{20,16},{24,28},{28,24},{1,5},{5... | collective-permute-start | bytes 393224 | tf_op jit(solution)/shard_map/ppermute | solution.py:214
  33.2 4.7 %collective-permute-start.17 = (bf16[64,1024]{1,0:T(8,128)(2,1)S(1)}, bf16[64,1024]{1,0:T(8,128)(2,1)S(1)}, u32[]{:S(2)}, u32[]{:S(2)}) collective-permute-start(bf16[64,1024]{1,0:T(8,128)(2,1)S(1)} %collective-permute-done.16.refs_2_), channel_id=1, source_target_pairs={{0,4},{4,0},{8,12},{12,8},{16,20},{20,16},{24,28},{28,24},{1,5},{5... | collective-permute-start | bytes 393224 | tf_op jit(solution)/shard_map/ppermute | solution.py:214
  33.3 6.0 %collective-permute-start.15 = (bf16[64,1024]{1,0:T(8,128)(2,1)S(1)}, bf16[64,1024]{1,0:T(8,128)(2,1)S(1)}, u32[]{:S(2)}, u32[]{:S(2)}) collective-permute-start(bf16[64,1024]{1,0:T(8,128)(2,1)S(1)} %collective-permute-done.14.refs_2_), channel_id=1, source_target_pairs={{0,4},{4,0},{8,12},{12,8},{16,20},{20,16},{24,28},{28,24},{1,5},{5... | collective-permute-start | bytes 393224 | tf_op jit(solution)/shard_map/ppermute | solution.py:214

commit v3 on v2

--- a/solution.py
+++ b/solution.py
@@ -15,6 +15,7 @@
 
 HBM = pl.BlockSpec(memory_space=pltpu.HBM)
 VMEM = pl.BlockSpec(memory_space=pltpu.VMEM)
+COST = pl.CostEstimate(flops=1 << 34, transcendentals=0, bytes_accessed=1 << 26)
 
 
 def params(mib=8):
@@ -55,6 +56,8 @@
 
 def encode(base, local, flip, chips, width):
     rows = base.shape[0]
+    base = pltpu.with_memory_space_constraint(base, pltpu.HBM)
+    local = pltpu.with_memory_space_constraint(local, pltpu.HBM)
     return pl.pallas_call(
         functools.partial(encode_kernel, flip),
         out_shape=jax.ShapeDtypeStruct((chips, rows, width), jnp.bfloat16),
@@ -65,6 +68,7 @@
             pltpu.VMEM((chips, rows, width), jnp.bfloat16),
             pltpu.SemaphoreType.DMA((2, chips)),
         ],
+        cost_estimate=COST,
         compiler_params=params(),
     )(base, local)
 
@@ -83,6 +87,7 @@
             jax.ShapeDtypeStruct((rows, width), jnp.float32 if j == 0 else jnp.bfloat16)
             for j in range(chips)
         ],
+        cost_estimate=COST,
         compiler_params=params(),
     )(keep, recv)
 
@@ -108,105 +113,140 @@
     return pl.pallas_call(
         functools.partial(chunk_step_kernel, replicas),
         out_shape=[jax.ShapeDtypeStruct(own.shape, jnp.bfloat16)] * 2,
+        cost_estimate=COST,
         compiler_params=params(),
     )(base, momentum, own, *parts)
 
 
-def outer_kernel(replicas, base_ref, mom_ref, *refs):
-    firsts, (new_base_hbm, new_mom_hbm, fresh_ref) = refs[:replicas], refs[replicas:-3]
-    new_base_ref, new_mom_ref, sems = refs[-3:]
+def outer_kernel(base_ref, mom_ref, *refs):
+    firsts, (new_base_ref, new_mom_ref, fresh_ref) = refs[:-3], refs[-3:]
     rows, width = fresh_ref.shape[1:]
     me = lax.axis_index("rep")
-    copies = []
     for k, first in enumerate(firsts):
         cols = columns(me ^ k, width)
         average = first[:rows, :].astype(jnp.float32)
         new_base, moved = stepped(average, base_ref[:, cols], mom_ref[:, cols])
-        new_base_ref[k] = new_base
-        new_mom_ref[k] = moved
+        new_base_ref[:, cols] = new_base
+        new_mom_ref[:, cols] = moved
         fresh_ref[k] = new_base.astype(jnp.bfloat16)
-        for which, (ref, hbm) in enumerate(
-            ((new_base_ref, new_base_hbm), (new_mom_ref, new_mom_hbm))
-        ):
-            copy = pltpu.make_async_copy(ref.at[k], hbm.at[:, cols], sems.at[which, k])
-            copy.start()
-            copies.append(copy)
-    for copy in copies:
-        copy.wait()
 
 
 def outer(base, momentum, firsts, width):
     rows = base.shape[0]
     replicas = len(firsts)
     return pl.pallas_call(
-        functools.partial(outer_kernel, replicas),
+        outer_kernel,
         out_shape=[
             jax.ShapeDtypeStruct(base.shape, jnp.float32),
             jax.ShapeDtypeStruct(base.shape, jnp.float32),
             jax.ShapeDtypeStruct((replicas, rows, width), jnp.bfloat16),
         ],
-        out_specs=[HBM, HBM, VMEM],
-        scratch_shapes=[
-            pltpu.VMEM((replicas, rows, width), jnp.float32),
-            pltpu.VMEM((replicas, rows, width), jnp.float32),
-            pltpu.SemaphoreType.DMA((2, replicas)),
-        ],
+        cost_estimate=COST,
         compiler_params=params(),
     )(base, momentum, *firsts)
 
 
-def project_kernel(places, near, tok_ref, own_ref, *refs):
+def stack(rhs_ref, i, own, first, second, near):
+    rows = own.shape[0]
+    here = lax.axis_index("fsdp")
+    pieces = [own[...]]
+    pieces += [first[s * rows : (s + 1) * rows, :] for s in range(1, near + 1)]
+    pieces += [second[s * rows : (s + 1) * rows, :] for s in range(second.shape[0] // rows)]
+    for s, piece in enumerate(pieces):
+        rhs_ref[i, pl.ds(pl.multiple_of((here ^ s) * rows, rows), rows), :] = piece
+
+
+def stack_kernel(places, near, own_ref, *refs):
     count = len(places)
-    firsts, seconds = refs[:count], refs[count : 2 * count]
-    out_hbm, rhs_ref, out_ref, sems = refs[-4:]
-    rows, width = own_ref.shape[1:]
-    me, here = lax.axis_index("rep"), lax.axis_index("fsdp")
-
-    def at(s):
-        return pl.ds(pl.multiple_of((here ^ s) * rows, rows), rows)
-
+    out_ref, rhs_ref, sems = refs[-3:]
     copies = []
     for i, k in enumerate(places):
-        rhs_ref[i, at(0), :] = own_ref[k]
-        for s in range(1, near + 1):
-            rhs_ref[i, at(s), :] = firsts[i][s * rows : (s + 1) * rows, :]
-        for s in range(seconds[i].shape[0] // rows):
-            rhs_ref[i, at(s + near + 1), :] = seconds[i][s * rows : (s + 1) * rows, :]
-        out_ref[i] = jnp.dot(
-            tok_ref[...], rhs_ref[i], preferred_element_type=jnp.float32
-        ).astype(out_ref.dtype)
+        stack(rhs_ref, i, own_ref.at[k], refs[i], refs[count + i], near)
+        copies.append(pltpu.make_async_copy(rhs_ref.at[i], out_ref.at[k], sems.at[i]))
+        copies[-1].start()
+    for copy in copies:
+        copy.wait()
+
+
+def stacked(rhs, depth, own, firsts, seconds, places, near):
+    replicas, rows, width = own.shape
+    count = len(places)
+    args = [own] + [firsts[k] for k in places] + [seconds[k] for k in places]
+    specs = [VMEM] * len(args)
+    alias = {}
+    if rhs is not None:
+        alias = {len(args): 0}
+        args.append(rhs)
+        specs.append(pl.BlockSpec(memory_space=pl.ANY))
+    return pl.pallas_call(
+        functools.partial(stack_kernel, places, near),
+        out_shape=jax.ShapeDtypeStruct((replicas, depth, width), jnp.bfloat16),
+        in_specs=specs,
+        out_specs=pl.BlockSpec(memory_space=pl.ANY),
+        input_output_aliases=alias,
+        scratch_shapes=[
+            pltpu.VMEM((count, depth, width), jnp.bfloat16),
+            pltpu.SemaphoreType.DMA((count,)),
+        ],
+        cost_estimate=COST,
+        compiler_params=params(),
+    )(*args)
+
+
+def project_kernel(places, near, tok_ref, own_ref, base_ref, mom_ref, *refs):
+    count = len(places)
+    replicas, rows, width = own_ref.shape
+    firsts, seconds, stacked_ref = refs[:count], refs[count : 2 * count], refs[2 * count]
+    out_hbm, new_base_hbm, new_mom_hbm, rhs_ref, out_ref, sems = refs[-6:]
+    me = lax.axis_index("rep")
+    copies = [
+        pltpu.make_async_copy(base_ref, new_base_hbm, sems.at[replicas]),
+        pltpu.make_async_copy(mom_ref, new_mom_hbm, sems.at[replicas + 1]),
+    ]
+    for copy in copies:
+        copy.start()
+
+    def emit(k, rhs):
+        out_ref[k] = jnp.dot(tok_ref[...], rhs, preferred_element_type=jnp.float32).astype(
+            out_ref.dtype
+        )
         copy = pltpu.make_async_copy(
-            out_ref.at[i], out_hbm.at[:, columns(me ^ k, width)], sems.at[i]
+            out_ref.at[k], out_hbm.at[:, columns(me ^ k, width)], sems.at[k]
         )
         copy.start()
         copies.append(copy)
+
+    for k in range(replicas):
+        if k not in places:
+            emit(k, stacked_ref[k])
+    for i, k in enumerate(places):
+        stack(rhs_ref, i, own_ref.at[k], firsts[i], seconds[i], near)
+        emit(k, rhs_ref[i])
     for copy in copies:
         copy.wait()
 
 
-def project(out, tokens, own, firsts, seconds, places, near):
+def project(rhs, tokens, own, new_base, new_mom, firsts, seconds, places, near):
     replicas, rows, width = own.shape
     tall, depth = tokens.shape
     count = len(places)
-    args = [tokens, own] + [firsts[k] for k in places] + [seconds[k] for k in places]
-    specs = [VMEM] * len(args)
-    alias = {}
-    if out is not None:
-        alias = {len(args): 0}
-        args.append(out)
-        specs.append(HBM)
+    args = [tokens, own, new_base, new_mom]
+    args += [firsts[k] for k in places] + [seconds[k] for k in places] + [rhs]
     return pl.pallas_call(
         functools.partial(project_kernel, places, near),
-        out_shape=jax.ShapeDtypeStruct((tall, width * replicas), jnp.bfloat16),
-        in_specs=specs,
-        out_specs=HBM,
-        input_output_aliases=alias,
+        out_shape=[
+            jax.ShapeDtypeStruct((tall, width * replicas), jnp.bfloat16),
+            jax.ShapeDtypeStruct(new_base.shape, jnp.float32),
+            jax.ShapeDtypeStruct(new_base.shape, jnp.float32),
+        ],
+        out_specs=[HBM, HBM, HBM],
         scratch_shapes=[
             pltpu.VMEM((count, depth, width), jnp.bfloat16),
-            pltpu.VMEM((count, tall, width), jnp.bfloat16),
-            pltpu.SemaphoreType.DMA((count,)),
-        ],
-        compiler_params=params(16),
+            pltpu.VMEM((replicas, tall, width), jnp.bfloat16),
+            pltpu.SemaphoreType.DMA((replicas + 2,)),
+        ],
+        cost_estimate=COST,
+        compiler_params=params(),
     )(*args)
 
 
@@ -214,9 +254,20 @@
     return lax.ppermute(x, axis, [(i, i ^ flip) for i in range(lax.axis_size(axis))])
 
 
-def spread(own, chips):
-    held = [own] + [swap(own, "rep", 2 * j) for j in range(1, chips)]
-    return [x for a in held for x in (a, swap(a, "rep", 1))]
+def join_kernel(*refs):
+    at = 0
+    for ref in refs[:-1]:
+        refs[-1][at : at + ref.shape[0], :] = ref[...]
+        at += ref.shape[0]
+
+
+def join(xs):
+    return pl.pallas_call(
+        join_kernel,
+        out_shape=jax.ShapeDtypeStruct((sum(x.shape[0] for x in xs),) + xs[0].shape[1:], xs[0].dtype),
+        cost_estimate=COST,
+        compiler_params=params(),
+    )(*xs)
 
 
 def on_device(base, local, momentum, tokens):
@@ -233,13 +284,23 @@
     average, fresh = chunk_step(base, momentum, sums[0], parts, replicas)
 
     far = [swap(fresh, "fsdp", s) for s in range(1, groups)]
-    firsts = spread(jnp.concatenate([average] + far[:near], axis=0), chips)
-    seconds = spread(jnp.concatenate(far[near:], axis=0), chips)
-
+    first = join([average] + far[:near])
+    second = join(far[near:])
+    firsts = [first] + [swap(first, "rep", 2 * j) for j in range(1, chips)]
+    seconds = [second] + [swap(second, "rep", 2 * j) for j in range(1, chips)]
+    last = swap(second, "rep", 1)
+    firsts = [x for a in firsts for x in (a, swap(a, "rep", 1))]
     new_base, new_momentum, own = outer(base, momentum, firsts, width)
-    projected = None
-    for j in [0] + list(range(chips - 1, 0, -1)):
-        projected = project(projected, tokens, own, firsts, seconds, (2 * j, 2 * j + 1), near)
+    lasts = [last] + [swap(a, "rep", 1) for a in seconds[:0:-1]][::-1]
+    seconds = [x for pair in zip(seconds, lasts) for x in pair]
+
+    order = [(2 * j, 2 * j + 1) for j in [0] + list(range(chips - 1, 0, -1))]
+    rhs = None
+    for places in order[:-1]:
+        rhs = stacked(rhs, tokens.shape[1], own, firsts, seconds, places, near)
+    projected, new_base, new_momentum = project(
+        rhs, tokens, own, new_base, new_momentum, firsts, seconds, order[-1], near
+    )
     return new_base, new_momentum, projected
 
 

time: 40.8 us -> 36.2 us (0.89)
  Pallas kernels: 8.55 us -> 6.49 us
  local copies, waits for them, and re-layouts: 2.29 us -> 0.45 us
  starting transfers between devices: 17.9 us -> 17.4 us
    pallas_call x4 -> x1, Pallas kernels: 5.27 us -> 2.73 us  [project(): pl.pallas_call(functools.partial(project_kernel, places, near), out_shape...]
    unnamed x12 -> x6, local copies, waits for them, and re-layouts: 2.28 us -> 0.45 us
    pallas_call x2, Pallas kernels: 1.66 us -> 2.98 us  [encode(): pl.pallas_call(functools.partial(encode_kernel, flip), out_shape=jax.Shap...]
    pallas_call x1 -> x6, Pallas kernels: 1.48 us -> 0.65 us  [the longest x1 0.31 us: outer(): pl.pallas_call(outer_kernel, out_shape=[jax.ShapeDtypeStruct(base.shape,...]
    ppermute x21, starting transfers between devices: 17.9 us -> 17.4 us  [swap(): lax.ppermute(x, axis, [(i, i ^ flip) for i in range(lax.axis_size(axis))])]
  transfers between devices with their start and end apart: 21 -> 21, of which waited for: 9 -> 11; matrix products, arithmetic and copies ran while one was open for 0% -> 0% of each run, Pallas kernels for 15% -> 6%
where the time goes in v3:
time: 36.2 us; the launch traced here: 35.7 us
  starting transfers between devices  17.4 us (48%)
  waiting for transfers between devices  10.6 us (29%)
  Pallas kernels  6.49 us (18%)
  between operations  0.76 us (2%)
  local copies, waits for them, and re-layouts  0.45 us (1%)
    ppermute x21, starting transfers between devices, swap(): lax.ppermute(x, axis, [(i, i ^ flip) for i in range(lax.axis_size(axis))])  17.4 us
    ppermute x21, waiting for transfers between devices, swap(): lax.ppermute(x, axis, [(i, i ^ flip) for i in range(lax.axis_size(axis))])  10.6 us
    pallas_call x2, Pallas kernels, encode(): pl.pallas_call(functools.partial(encode_kernel, flip), out_shape=jax.Shap...  2.98 us
    pallas_call x1, Pallas kernels, project(): pl.pallas_call(functools.partial(project_kernel, places, near), out_shape...  2.73 us
  transfers between devices with their start and end apart: 21, of which 11 were waited for; matrix products, arithmetic and copies ran while one was open for 0% of the time, Pallas kernels for 6%

profile of v3, /device:TPU:0, one launch (start us, length us, event | category | flops | bytes accessed | tf_op | source)
XLA Modules:
  0.0 35.7 jit_solution(11641395647101198148)
XLA Ops:
  0.6 1.5 %shard_map.68 = bf16[4,32,1024]{2,1,0:T(8,128)(2,1)S(1)} custom-call(f32[32,8192]{1,0:T(8,128)} %base_ref.3, bf16[1,32,8192]{2,1,0:T(8,128)(2,1)} %local_hbm.3), custom_call_target="tpu_custom_call" | custom-call | flops 17179869184 | bytes 67108864 | tf_op jit(solution)/shard_map/pallas_call | solution.py:61
  2.1 0.5 %collective-permute-start = (bf16[4,32,1024]{2,1,0:T(8,128)(2,1)S(1)}, bf16[4,32,1024]{2,1,0:T(8,128)(2,1)S(1)}, u32[]{:S(2)}, u32[]{:S(2)}) collective-permute-start(bf16[4,32,1024]{2,1,0:T(8,128)(2,1)S(1)} %shard_map.68), channel_id=1, source_target_pairs={{0,4},{4,0},{8,12},{12,8},{16,20},{20,16},{24,28},{28,24},{1,5},{5... | collective-permute-start | bytes 786440 | tf_op jit(solution)/shard_map/ppermute | solution.py:254
  2.6 1.5 %shard_map.67.keep_ref = bf16[4,32,1024]{2,1,0:T(8,128)(2,1)S(1)} custom-call(f32[32,8192]{1,0:T(8,128)} %base_ref.3, bf16[1,32,8192]{2,1,0:T(8,128)(2,1)} %local_hbm.3), custom_call_target="tpu_custom_call" | custom-call | flops 17179869184 | bytes 67108864 | tf_op jit(solution)/shard_map/pallas_call | solution.py:61
  4.2 2.6 %collective-permute-start.1 = (bf16[32,1024]{1,0:T(8,128)(2,1)S(1)}, bf16[32,1024]{1,0:T(8,128)(2,1)S(1)}, u32[]{:S(2)}, u32[]{:S(2)}) collective-permute-start(bf16[32,1024]{1,0:T(8,128)(2,1)S(1)} %get-tuple-element.16), channel_id=1, source_target_pairs={{0,8},{4,12},{8,0},{12,4},{16,24},{20,28},{24,16},{28,20},{1,9},{5... | collective-permute-start | bytes 196616 | tf_op jit(solution)/shard_map/ppermute | solution.py:254
  6.8 1.5 %collective-permute-start.2 = (bf16[32,1024]{1,0:T(8,128)(2,1)S(1)}, bf16[32,1024]{1,0:T(8,128)(2,1)S(1)}, u32[]{:S(2)}, u32[]{:S(2)}) collective-permute-start(bf16[32,1024]{1,0:T(8,128)(2,1)S(1)} %get-tuple-element.17), channel_id=1, source_target_pairs={{0,16},{4,20},{8,24},{12,28},{16,0},{20,4},{24,8},{28,12},{1,17},{... | collective-permute-start | bytes 196616 | tf_op jit(solution)/shard_map/ppermute | solution.py:254
  8.4 1.2 %collective-permute-done.1.refs_0_ = bf16[32,1024]{1,0:T(8,128)(2,1)S(1)} collective-permute-done((bf16[32,1024]{1,0:T(8,128)(2,1)S(1)}, bf16[32,1024]{1,0:T(8,128)(2,1)S(1)}, u32[]{:S(2)}, u32[]{:S(2)}) %collective-permute-start.1) | collective-permute-done | bytes 65568 | tf_op jit(solution)/shard_map/ppermute | solution.py:254
  9.6 1.5 %collective-permute-done.2.refs_1_ = bf16[32,1024]{1,0:T(8,128)(2,1)S(1)} collective-permute-done((bf16[32,1024]{1,0:T(8,128)(2,1)S(1)}, bf16[32,1024]{1,0:T(8,128)(2,1)S(1)}, u32[]{:S(2)}, u32[]{:S(2)}) %collective-permute-start.2) | collective-permute-done | bytes 65568 | tf_op jit(solution)/shard_map/ppermute | solution.py:254
  11.1 2.4 %collective-permute-done.3.refs_2_ = bf16[32,1024]{1,0:T(8,128)(2,1)S(1)} collective-permute-done((bf16[32,1024]{1,0:T(8,128)(2,1)S(1)}, bf16[32,1024]{1,0:T(8,128)(2,1)S(1)}, u32[]{:S(2)}, u32[]{:S(2)}) %collective-permute-start.3) | collective-permute-done | bytes 65568 | tf_op jit(solution)/shard_map/ppermute | solution.py:254
  13.6 1.6 %collective-permute-start.4 = (bf16[32,1024]{1,0:T(8,128)(2,1)S(1)}, bf16[32,1024]{1,0:T(8,128)(2,1)S(1)}, u32[]{:S(2)}, u32[]{:S(2)}) collective-permute-start(bf16[32,1024]{1,0:T(8,128)(2,1)S(1)} %get-tuple-element.20), channel_id=1, source_target_pairs={{0,1},{1,0},{2,3},{3,2},{4,5},{5,4},{6,7},{7,6},{8,9},{9,8},{10,11... | collective-permute-start | bytes 196616 | tf_op jit(solution)/shard_map/ppermute | solution.py:254
  15.2 2.5 %collective-permute-start.13 = (bf16[32,1024]{1,0:T(8,128)(2,1)S(1)}, bf16[32,1024]{1,0:T(8,128)(2,1)S(1)}, u32[]{:S(2)}, u32[]{:S(2)}) collective-permute-start(bf16[32,1024]{1,0:T(8,128)(2,1)S(1)} %get-tuple-element.20), channel_id=1, source_target_pairs={{0,3},{1,2},{2,1},{3,0},{4,7},{5,6},{6,5},{7,4},{8,11},{9,10},{10,... | collective-permute-start | bytes 196616 | tf_op jit(solution)/shard_map/ppermute | solution.py:254
  17.7 0.1 collective-permute-start.12
  17.9 0.6 %collective-permute-start.10 = (bf16[64,1024]{1,0:T(8,128)(2,1)S(1)}, bf16[64,1024]{1,0:T(8,128)(2,1)S(1)}, u32[]{:S(2)}, u32[]{:S(2)}) collective-permute-start(bf16[64,1024]{1,0:T(8,128)(2,1)S(1)} %shard_map.71.refs_0_), channel_id=1, source_target_pairs={{0,24},{4,28},{8,16},{12,20},{16,8},{20,12},{24,0},{28,4},{1,25},{... | collective-permute-start | bytes 393224 | tf_op jit(solution)/shard_map/ppermute | solution.py:254
  18.5 1.5 %collective-permute-start.8 = (bf16[64,1024]{1,0:T(8,128)(2,1)S(1)}, bf16[64,1024]{1,0:T(8,128)(2,1)S(1)}, u32[]{:S(2)}, u32[]{:S(2)}) collective-permute-start(bf16[64,1024]{1,0:T(8,128)(2,1)S(1)} %shard_map.71.refs_0_), channel_id=1, source_target_pairs={{0,16},{4,20},{8,24},{12,28},{16,0},{20,4},{24,8},{28,12},{1,17},{... | collective-permute-start | bytes 393224 | tf_op jit(solution)/shard_map/ppermute | solution.py:254
  20.0 1.5 %collective-permute-start.6 = (bf16[64,1024]{1,0:T(8,128)(2,1)S(1)}, bf16[64,1024]{1,0:T(8,128)(2,1)S(1)}, u32[]{:S(2)}, u32[]{:S(2)}) collective-permute-start(bf16[64,1024]{1,0:T(8,128)(2,1)S(1)} %shard_map.71.refs_0_), channel_id=1, source_target_pairs={{0,8},{4,12},{8,0},{12,4},{16,24},{20,28},{24,16},{28,20},{1,9},{5... | collective-permute-start | bytes 393224 | tf_op jit(solution)/shard_map/ppermute | solution.py:254
  21.5 2.1 %collective-permute-done.12.refs_0_ = bf16[32,1024]{1,0:T(8,128)(2,1)S(1)} collective-permute-done((bf16[32,1024]{1,0:T(8,128)(2,1)S(1)}, bf16[32,1024]{1,0:T(8,128)(2,1)S(1)}, u32[]{:S(2)}, u32[]{:S(2)}) %collective-permute-start.12) | collective-permute-done | bytes 65568 | tf_op jit(solution)/shard_map/ppermute | solution.py:254
  23.6 0.5 %collective-permute-start.18 = (bf16[64,1024]{1,0:T(8,128)(2,1)S(1)}, bf16[64,1024]{1,0:T(8,128)(2,1)S(1)}, u32[]{:S(2)}, u32[]{:S(2)}) collective-permute-start(bf16[64,1024]{1,0:T(8,128)(2,1)S(1)} %shard_map.73.refs_2_), channel_id=1, source_target_pairs={{0,24},{4,28},{8,16},{12,20},{16,8},{20,12},{24,0},{28,4},{1,25},{... | collective-permute-start | bytes 393224 | tf_op jit(solution)/shard_map/ppermute | solution.py:254
  24.1 1.5 %collective-permute-start.16 = (bf16[64,1024]{1,0:T(8,128)(2,1)S(1)}, bf16[64,1024]{1,0:T(8,128)(2,1)S(1)}, u32[]{:S(2)}, u32[]{:S(2)}) collective-permute-start(bf16[64,1024]{1,0:T(8,128)(2,1)S(1)} %shard_map.73.refs_2_), channel_id=1, source_target_pairs={{0,16},{4,20},{8,24},{12,28},{16,0},{20,4},{24,8},{28,12},{1,17},{... | collective-permute-start | bytes 393224 | tf_op jit(solution)/shard_map/ppermute | solution.py:254
  25.7 1.5 %collective-permute-start.14 = (bf16[64,1024]{1,0:T(8,128)(2,1)S(1)}, bf16[64,1024]{1,0:T(8,128)(2,1)S(1)}, u32[]{:S(2)}, u32[]{:S(2)}) collective-permute-start(bf16[64,1024]{1,0:T(8,128)(2,1)S(1)} %shard_map.73.refs_2_), channel_id=1, source_target_pairs={{0,8},{4,12},{8,0},{12,4},{16,24},{20,28},{24,16},{28,20},{1,9},{5... | collective-permute-start | bytes 393224 | tf_op jit(solution)/shard_map/ppermute | solution.py:254
  27.2 0.5 %collective-permute-start.9 = (bf16[64,1024]{1,0:T(8,128)(2,1)S(1)}, bf16[64,1024]{1,0:T(8,128)(2,1)S(1)}, u32[]{:S(2)}, u32[]{:S(2)}) collective-permute-start(bf16[64,1024]{1,0:T(8,128)(2,1)S(1)} %collective-permute-done.8.refs_4_.refs_0_), channel_id=1, source_target_pairs={{0,4},{4,0},{8,12},{12,8},{16,20},{20,16},{24,28},{28,24},{1,5},{5... | collective-permute-start | bytes 393224 | tf_op jit(solution)/shard_map/ppermute | solution.py:254
  27.7 2.3 %collective-permute-done.18.refs_2_ = bf16[64,1024]{1,0:T(8,128)(2,1)S(1)} collective-permute-done((bf16[64,1024]{1,0:T(8,128)(2,1)S(1)}, bf16[64,1024]{1,0:T(8,128)(2,1)S(1)}, u32[]{:S(2)}, u32[]{:S(2)}) %collective-permute-start.18) | collective-permute-done | bytes 131104 | tf_op jit(solution)/shard_map/ppermute | solution.py:254
  29.9 0.6 %collective-permute-done.16.refs_2_ = bf16[64,1024]{1,0:T(8,128)(2,1)S(1)} collective-permute-done((bf16[64,1024]{1,0:T(8,128)(2,1)S(1)}, bf16[64,1024]{1,0:T(8,128)(2,1)S(1)}, u32[]{:S(2)}, u32[]{:S(2)}) %collective-permute-start.16) | collective-permute-done | bytes 131104 | tf_op jit(solution)/shard_map/ppermute | solution.py:254
  30.5 0.1 collective-permute-done.14.refs_2_
  30.6 0.4 %collective-permute-start.19 = (bf16[64,1024]{1,0:T(8,128)(2,1)S(1)}, bf16[64,1024]{1,0:T(8,128)(2,1)S(1)}, u32[]{:S(2)}, u32[]{:S(2)}) collective-permute-start(bf16[64,1024]{1,0:T(8,128)(2,1)S(1)} %collective-permute-done.18.refs_2_), channel_id=1, source_target_pairs={{0,4},{4,0},{8,12},{12,8},{16,20},{20,16},{24,28},{28,24},{1,5},{5... | collective-permute-start | bytes 393224 | tf_op jit(solution)/shard_map/ppermute | solution.py:254
  31.0 0.1 collective-permute-start.17
  31.1 0.4 %collective-permute-start.15 = (bf16[64,1024]{1,0:T(8,128)(2,1)S(1)}, bf16[64,1024]{1,0:T(8,128)(2,1)S(1)}, u32[]{:S(2)}, u32[]{:S(2)}) collective-permute-start(bf16[64,1024]{1,0:T(8,128)(2,1)S(1)} %collective-permute-done.14.refs_2_), channel_id=1, source_target_pairs={{0,4},{4,0},{8,12},{12,8},{16,20},{20,16},{24,28},{28,24},{1,5},{5... | collective-permute-start | bytes 393224 | tf_op jit(solution)/shard_map/ppermute | solution.py:254
  31.5 0.3 shard_map.72
  31.9 0.1 shard_map.74.refs_4_
  32.0 0.1 shard_map.75.refs_4_
  32.2 0.2 collective-permute-done.17.refs_3_
  32.4 0.1 shard_map.76.refs_4_
  32.6 0.4 %copy-done.2 = bf16[256,128]{1,0:T(8,128)(2,1)S(1)} copy-done((bf16[256,128]{1,0:T(8,128)(2,1)S(1)}, bf16[256,128]{1,0:T(8,128)(2,1)}, u32[]{:S(2)}) %copy-start.2) | copy-done | bytes 65560
  33.0 2.7 %shard_map.77 = (bf16[256,8192]{1,0:T(8,128)(2,1)}, f32[32,8192]{1,0:T(8,128)}, f32[32,8192]{1,0:T(8,128)}) custom-call(bf16[256,128]{1,0:T(8,128)(2,1)S(1)} %copy-done.2, bf16[8,32,1024]{2,1,0:T(8,128)(2,1)S(1)} %get-tuple-element.21.own_ref, f32[32,8192]{1,0:T(8,128)S(1)} %get-tuple-element.22.base_ref, f32[32,8192]{1,0:T(8,128)S(1)} %get-tuple-element.23.mom_ref, ...), custom_call_target="tpu_custom_call" | custom-call | flops 17179869184 | bytes 67108864 | tf_op jit(solution)/shard_map/pallas_call | solution.py:235
  (27 shorter events, 0.5 us)
Async XLA Ops:
  2.1 2.0 %collective-permute-start = (bf16[4,32,1024]{2,1,0:T(8,128)(2,1)S(1)}, bf16[4,32,1024]{2,1,0:T(8,128)(2,1)S(1)}, u32[]{:S(2)}, u32[]{:S(2)}) collective-permute-start(bf16[4,32,1024]{2,1,0:T(8,128)(2,1)S(1)} %shard_map.68), channel_id=1, source_target_pairs={{0,4},{4,0},{8,12},{12,8},{16,20},{20,16},{24,28},{28,24},{1,5},{5... | collective-permute-start | bytes 786440 | tf_op jit(solution)/shard_map/ppermute | solution.py:254
  4.1 9.4 %copy-start = (f32[32,8192]{1,0:T(8,128)S(1)}, f32[32,8192]{1,0:T(8,128)}, u32[]{:S(2)}) copy-start(f32[32,8192]{1,0:T(8,128)} %base_ref.3) | copy-start | bytes 3145732
  4.2 9.4 %copy-start.1 = (f32[32,8192]{1,0:T(8,128)S(1)}, f32[32,8192]{1,0:T(8,128)}, u32[]{:S(2)}) copy-start(f32[32,8192]{1,0:T(8,128)} %mom_ref.3) | copy-start | bytes 3145732
  4.2 5.3 %collective-permute-start.1 = (bf16[32,1024]{1,0:T(8,128)(2,1)S(1)}, bf16[32,1024]{1,0:T(8,128)(2,1)S(1)}, u32[]{:S(2)}, u32[]{:S(2)}) collective-permute-start(bf16[32,1024]{1,0:T(8,128)(2,1)S(1)} %get-tuple-element.16), channel_id=1, source_target_pairs={{0,8},{4,12},{8,0},{12,4},{16,24},{20,28},{24,16},{28,20},{1,9},{5... | collective-permute-start | bytes 196616 | tf_op jit(solution)/shard_map/ppermute | solution.py:254
  6.8 4.3 %collective-permute-start.2 = (bf16[32,1024]{1,0:T(8,128)(2,1)S(1)}, bf16[32,1024]{1,0:T(8,128)(2,1)S(1)}, u32[]{:S(2)}, u32[]{:S(2)}) collective-permute-start(bf16[32,1024]{1,0:T(8,128)(2,1)S(1)} %get-tuple-element.17), channel_id=1, source_target_pairs={{0,16},{4,20},{8,24},{12,28},{16,0},{20,4},{24,8},{28,12},{1,17},{... | collective-permute-start | bytes 196616 | tf_op jit(solution)/shard_map/ppermute | solution.py:254
  8.3 5.2 %collective-permute-start.3 = (bf16[32,1024]{1,0:T(8,128)(2,1)S(1)}, bf16[32,1024]{1,0:T(8,128)(2,1)S(1)}, u32[]{:S(2)}, u32[]{:S(2)}) collective-permute-start(bf16[32,1024]{1,0:T(8,128)(2,1)S(1)} %get-tuple-element.18), channel_id=1, source_target_pairs={{0,24},{4,28},{8,16},{12,20},{16,8},{20,12},{24,0},{28,4},{1,25},{... | collective-permute-start | bytes 196616 | tf_op jit(solution)/shard_map/ppermute | solution.py:254
  13.6 4.3 %collective-permute-start.4 = (bf16[32,1024]{1,0:T(8,128)(2,1)S(1)}, bf16[32,1024]{1,0:T(8,128)(2,1)S(1)}, u32[]{:S(2)}, u32[]{:S(2)}) collective-permute-start(bf16[32,1024]{1,0:T(8,128)(2,1)S(1)} %get-tuple-element.20), channel_id=1, source_target_pairs={{0,1},{1,0},{2,3},{3,2},{4,5},{5,4},{6,7},{7,6},{8,9},{9,8},{10,11... | collective-permute-start | bytes 196616 | tf_op jit(solution)/shard_map/ppermute | solution.py:254
  15.2 6.3 %collective-permute-start.13 = (bf16[32,1024]{1,0:T(8,128)(2,1)S(1)}, bf16[32,1024]{1,0:T(8,128)(2,1)S(1)}, u32[]{:S(2)}, u32[]{:S(2)}) collective-permute-start(bf16[32,1024]{1,0:T(8,128)(2,1)S(1)} %get-tuple-element.20), channel_id=1, source_target_pairs={{0,3},{1,2},{2,1},{3,0},{4,7},{5,6},{6,5},{7,4},{8,11},{9,10},{10,... | collective-permute-start | bytes 196616 | tf_op jit(solution)/shard_map/ppermute | solution.py:254
  17.7 5.9 %collective-permute-start.12 = (bf16[32,1024]{1,0:T(8,128)(2,1)S(1)}, bf16[32,1024]{1,0:T(8,128)(2,1)S(1)}, u32[]{:S(2)}, u32[]{:S(2)}) collective-permute-start(bf16[32,1024]{1,0:T(8,128)(2,1)S(1)} %get-tuple-element.20), channel_id=1, source_target_pairs={{0,2},{1,3},{2,0},{3,1},{4,6},{5,7},{6,4},{7,5},{8,10},{9,11},{10,... | collective-permute-start | bytes 196616 | tf_op jit(solution)/shard_map/ppermute | solution.py:254
  17.9 6.2 %collective-permute-start.10 = (bf16[64,1024]{1,0:T(8,128)(2,1)S(1)}, bf16[64,1024]{1,0:T(8,128)(2,1)S(1)}, u32[]{:S(2)}, u32[]{:S(2)}) collective-permute-start(bf16[64,1024]{1,0:T(8,128)(2,1)S(1)} %shard_map.71.refs_0_), channel_id=1, source_target_pairs={{0,24},{4,28},{8,16},{12,20},{16,8},{20,12},{24,0},{28,4},{1,25},{... | collective-permute-start | bytes 393224 | tf_op jit(solution)/shard_map/ppermute | solution.py:254
  18.5 7.2 %collective-permute-start.8 = (bf16[64,1024]{1,0:T(8,128)(2,1)S(1)}, bf16[64,1024]{1,0:T(8,128)(2,1)S(1)}, u32[]{:S(2)}, u32[]{:S(2)}) collective-permute-start(bf16[64,1024]{1,0:T(8,128)(2,1)S(1)} %shard_map.71.refs_0_), channel_id=1, source_target_pairs={{0,16},{4,20},{8,24},{12,28},{16,0},{20,4},{24,8},{28,12},{1,17},{... | collective-permute-start | bytes 393224 | tf_op jit(solution)/shard_map/ppermute | solution.py:254
  20.0 7.2 %collective-permute-start.6 = (bf16[64,1024]{1,0:T(8,128)(2,1)S(1)}, bf16[64,1024]{1,0:T(8,128)(2,1)S(1)}, u32[]{:S(2)}, u32[]{:S(2)}) collective-permute-start(bf16[64,1024]{1,0:T(8,128)(2,1)S(1)} %shard_map.71.refs_0_), channel_id=1, source_target_pairs={{0,8},{4,12},{8,0},{12,4},{16,24},{20,28},{24,16},{28,20},{1,9},{5... | collective-permute-start | bytes 393224 | tf_op jit(solution)/shard_map/ppermute | solution.py:254
  21.5 5.7 %collective-permute-start.5 = (bf16[64,1024]{1,0:T(8,128)(2,1)S(1)}, bf16[64,1024]{1,0:T(8,128)(2,1)S(1)}, u32[]{:S(2)}, u32[]{:S(2)}) collective-permute-start(bf16[64,1024]{1,0:T(8,128)(2,1)S(1)} %shard_map.71.refs_0_), channel_id=1, source_target_pairs={{0,4},{4,0},{8,12},{12,8},{16,20},{20,16},{24,28},{28,24},{1,5},{5... | collective-permute-start | bytes 393224 | tf_op jit(solution)/shard_map/ppermute | solution.py:254
  23.6 6.4 %collective-permute-start.18 = (bf16[64,1024]{1,0:T(8,128)(2,1)S(1)}, bf16[64,1024]{1,0:T(8,128)(2,1)S(1)}, u32[]{:S(2)}, u32[]{:S(2)}) collective-permute-start(bf16[64,1024]{1,0:T(8,128)(2,1)S(1)} %shard_map.73.refs_2_), channel_id=1, source_target_pairs={{0,24},{4,28},{8,16},{12,20},{16,8},{20,12},{24,0},{28,4},{1,25},{... | collective-permute-start | bytes 393224 | tf_op jit(solution)/shard_map/ppermute | solution.py:254
  24.1 6.4 %collective-permute-start.16 = (bf16[64,1024]{1,0:T(8,128)(2,1)S(1)}, bf16[64,1024]{1,0:T(8,128)(2,1)S(1)}, u32[]{:S(2)}, u32[]{:S(2)}) collective-permute-start(bf16[64,1024]{1,0:T(8,128)(2,1)S(1)} %shard_map.73.refs_2_), channel_id=1, source_target_pairs={{0,16},{4,20},{8,24},{12,28},{16,0},{20,4},{24,8},{28,12},{1,17},{... | collective-permute-start | bytes 393224 | tf_op jit(solution)/shard_map/ppermute | solution.py:254
  25.7 5.0 %collective-permute-start.14 = (bf16[64,1024]{1,0:T(8,128)(2,1)S(1)}, bf16[64,1024]{1,0:T(8,128)(2,1)S(1)}, u32[]{:S(2)}, u32[]{:S(2)}) collective-permute-start(bf16[64,1024]{1,0:T(8,128)(2,1)S(1)} %shard_map.73.refs_2_), channel_id=1, source_target_pairs={{0,8},{4,12},{8,0},{12,4},{16,24},{20,28},{24,16},{28,20},{1,9},{5... | collective-permute-start | bytes 393224 | tf_op jit(solution)/shard_map/ppermute | solution.py:254
  27.2 3.9 %collective-permute-start.11 = (bf16[64,1024]{1,0:T(8,128)(2,1)S(1)}, bf16[64,1024]{1,0:T(8,128)(2,1)S(1)}, u32[]{:S(2)}, u32[]{:S(2)}) collective-permute-start(bf16[64,1024]{1,0:T(8,128)(2,1)S(1)} %collective-permute-done.10.refs_6_.refs_0_), channel_id=1, source_target_pairs={{0,4},{4,0},{8,12},{12,8},{16,20},{20,16},{24,28},{28,24},{1,5},{5... | collective-permute-start | bytes 393224 | tf_op jit(solution)/shard_map/ppermute | solution.py:254
  27.2 4.0 %collective-permute-start.9 = (bf16[64,1024]{1,0:T(8,128)(2,1)S(1)}, bf16[64,1024]{1,0:T(8,128)(2,1)S(1)}, u32[]{:S(2)}, u32[]{:S(2)}) collective-permute-start(bf16[64,1024]{1,0:T(8,128)(2,1)S(1)} %collective-permute-done.8.refs_4_.refs_0_), channel_id=1, source_target_pairs={{0,4},{4,0},{8,12},{12,8},{16,20},{20,16},{24,28},{28,24},{1,5},{5... | collective-permute-start | bytes 393224 | tf_op jit(solution)/shard_map/ppermute | solution.py:254
  29.9 1.6 %collective-permute-start.7 = (bf16[64,1024]{1,0:T(8,128)(2,1)S(1)}, bf16[64,1024]{1,0:T(8,128)(2,1)S(1)}, u32[]{:S(2)}, u32[]{:S(2)}) collective-permute-start(bf16[64,1024]{1,0:T(8,128)(2,1)S(1)} %collective-permute-done.6.refs_2_.refs_0_), channel_id=1, source_target_pairs={{0,4},{4,0},{8,12},{12,8},{16,20},{20,16},{24,28},{28,24},{1,5},{5... | collective-permute-start | bytes 393224 | tf_op jit(solution)/shard_map/ppermute | solution.py:254
  30.5 1.4 %collective-permute-start.20 = (bf16[64,1024]{1,0:T(8,128)(2,1)S(1)}, bf16[64,1024]{1,0:T(8,128)(2,1)S(1)}, u32[]{:S(2)}, u32[]{:S(2)}) collective-permute-start(bf16[64,1024]{1,0:T(8,128)(2,1)S(1)} %shard_map.73.refs_2_), channel_id=1, source_target_pairs={{0,4},{4,0},{8,12},{12,8},{16,20},{20,16},{24,28},{28,24},{1,5},{5... | collective-permute-start | bytes 393224 | tf_op jit(solution)/shard_map/ppermute | solution.py:254
  30.6 1.4 %collective-permute-start.19 = (bf16[64,1024]{1,0:T(8,128)(2,1)S(1)}, bf16[64,1024]{1,0:T(8,128)(2,1)S(1)}, u32[]{:S(2)}, u32[]{:S(2)}) collective-permute-start(bf16[64,1024]{1,0:T(8,128)(2,1)S(1)} %collective-permute-done.18.refs_2_), channel_id=1, source_target_pairs={{0,4},{4,0},{8,12},{12,8},{16,20},{20,16},{24,28},{28,24},{1,5},{5... | collective-permute-start | bytes 393224 | tf_op jit(solution)/shard_map/ppermute | solution.py:254
  31.0 1.3 %collective-permute-start.17 = (bf16[64,1024]{1,0:T(8,128)(2,1)S(1)}, bf16[64,1024]{1,0:T(8,128)(2,1)S(1)}, u32[]{:S(2)}, u32[]{:S(2)}) collective-permute-start(bf16[64,1024]{1,0:T(8,128)(2,1)S(1)} %collective-permute-done.16.refs_2_), channel_id=1, source_target_pairs={{0,4},{4,0},{8,12},{12,8},{16,20},{20,16},{24,28},{28,24},{1,5},{5... | collective-permute-start | bytes 393224 | tf_op jit(solution)/shard_map/ppermute | solution.py:254
  31.1 1.4 %collective-permute-start.15 = (bf16[64,1024]{1,0:T(8,128)(2,1)S(1)}, bf16[64,1024]{1,0:T(8,128)(2,1)S(1)}, u32[]{:S(2)}, u32[]{:S(2)}) collective-permute-start(bf16[64,1024]{1,0:T(8,128)(2,1)S(1)} %collective-permute-done.14.refs_2_), channel_id=1, source_target_pairs={{0,4},{4,0},{8,12},{12,8},{16,20},{20,16},{24,28},{28,24},{1,5},{5... | collective-permute-start | bytes 393224 | tf_op jit(solution)/shard_map/ppermute | solution.py:254
  32.2 0.8 %copy-start.2 = (bf16[256,128]{1,0:T(8,128)(2,1)S(1)}, bf16[256,128]{1,0:T(8,128)(2,1)}, u32[]{:S(2)}) copy-start(bf16[256,128]{1,0:T(8,128)(2,1)} %tok_ref.1) | copy-start | bytes 196612

commit v4 on v3

--- a/solution.py
+++ b/solution.py
@@ -33,10 +33,14 @@
     return (code.astype(jnp.float32) * scale).astype(jnp.bfloat16)
 
 
-def encode_kernel(flip, base_hbm, local_hbm, out_ref, base_ref, local_ref, sems):
+def encode_kernel(flip, base_hbm, local_hbm, *refs):
+    *staged, tok_ref, base_ref, local_ref, sems = refs
+    out_ref = staged[1] if staged else tok_ref
     chips, rows, width = out_ref.shape
     me = lax.axis_index("rep")
     copies = []
+    if staged:
+        stage = pltpu.make_async_copy(staged[0], tok_ref, sems.at[2, 0])
     for j in range(chips):
         cols = columns(me ^ (flip ^ (2 * j)), width)
         pair = (
@@ -46,31 +50,39 @@
         for copy in pair:
             copy.start()
         copies.append(pair)
+    if staged:
+        stage.start()
     for j in range(chips):
         for copy in copies[j]:
             copy.wait()
         for b in range(width // BLOCK):
             cols = slice(b * BLOCK, (b + 1) * BLOCK)
             out_ref[j, :, cols] = decoded_block(base_ref[j, :, cols], local_ref[j, :, cols])
-
-
-def encode(base, local, flip, chips, width):
+    if staged:
+        stage.wait()
+
+
+def encode(base, local, flip, chips, width, tokens=None):
     rows = base.shape[0]
     base = pltpu.with_memory_space_constraint(base, pltpu.HBM)
     local = pltpu.with_memory_space_constraint(local, pltpu.HBM)
+    args, shapes = [base, local], [jax.ShapeDtypeStruct((chips, rows, width), jnp.bfloat16)]
+    if tokens is not None:
+        args.append(pltpu.with_memory_space_constraint(tokens, pltpu.HBM))
+        shapes.append(jax.ShapeDtypeStruct(tokens.shape, tokens.dtype))
     return pl.pallas_call(
         functools.partial(encode_kernel, flip),
-        out_shape=jax.ShapeDtypeStruct((chips, rows, width), jnp.bfloat16),
-        in_specs=[HBM, HBM],
-        out_specs=VMEM,
+        out_shape=shapes,
+        in_specs=[HBM] * len(args),
+        out_specs=[VMEM] * len(shapes),
         scratch_shapes=[
             pltpu.VMEM((chips, rows, width), jnp.float32),
             pltpu.VMEM((chips, rows, width), jnp.bfloat16),
-            pltpu.SemaphoreType.DMA((2, chips)),
-        ],
-        cost_estimate=COST,
-        compiler_params=params(),
-    )(base, local)
+            pltpu.SemaphoreType.DMA((3, chips)),
+        ],
+        cost_estimate=COST,
+        compiler_params=params(),
+    )(*args)
 
 
 def chip_sum_kernel(keep_ref, recv_ref, *out_refs):
@@ -118,13 +130,28 @@
     )(base, momentum, own, *parts)
 
 
-def outer_kernel(base_ref, mom_ref, *refs):
-    firsts, (new_base_ref, new_mom_ref, fresh_ref) = refs[:-3], refs[-3:]
+def gather_slots(slots):
+    arrays, where = [], []
+    for array, place in slots:
+        known = [i for i, other in enumerate(arrays) if other is array]
+        if not known:
+            arrays.append(array)
+        where.append((known[0] if known else len(arrays) - 1, place))
+    return arrays, where
+
+
+def at_slot(refs, slot):
+    number, place = slot
+    return refs[number] if place is None else refs[number].at[place]
+
+
+def outer_kernel(where, base_ref, mom_ref, *refs):
+    holders, (new_base_ref, new_mom_ref, fresh_ref) = refs[:-3], refs[-3:]
     rows, width = fresh_ref.shape[1:]
     me = lax.axis_index("rep")
-    for k, first in enumerate(firsts):
+    for k, slot in enumerate(where):
         cols = columns(me ^ k, width)
-        average = first[:rows, :].astype(jnp.float32)
+        average = at_slot(holders, slot)[:rows, :].astype(jnp.float32)
         new_base, moved = stepped(average, base_ref[:, cols], mom_ref[:, cols])
         new_base_ref[:, cols] = new_base
         new_mom_ref[:, cols] = moved
@@ -133,17 +160,17 @@
 
 def outer(base, momentum, firsts, width):
     rows = base.shape[0]
-    replicas = len(firsts)
-    return pl.pallas_call(
-        outer_kernel,
+    arrays, where = gather_slots(firsts)
+    return pl.pallas_call(
+        functools.partial(outer_kernel, where),
         out_shape=[
             jax.ShapeDtypeStruct(base.shape, jnp.float32),
             jax.ShapeDtypeStruct(base.shape, jnp.float32),
-            jax.ShapeDtypeStruct((replicas, rows, width), jnp.bfloat16),
-        ],
-        cost_estimate=COST,
-        compiler_params=params(),
-    )(base, momentum, *firsts)
+            jax.ShapeDtypeStruct((len(firsts), rows, width), jnp.bfloat16),
+        ],
+        cost_estimate=COST,
+        compiler_params=params(),
+    )(base, momentum, *arrays)
 
 
 def stack(rhs_ref, i, own, first, second, near):
@@ -156,12 +183,13 @@
         rhs_ref[i, pl.ds(pl.multiple_of((here ^ s) * rows, rows), rows), :] = piece
 
 
-def stack_kernel(places, near, own_ref, *refs):
+def stack_kernel(places, near, where, own_ref, *refs):
     count = len(places)
     out_ref, rhs_ref, sems = refs[-3:]
     copies = []
     for i, k in enumerate(places):
-        stack(rhs_ref, i, own_ref.at[k], refs[i], refs[count + i], near)
+        first, second = at_slot(refs, where[i]), at_slot(refs, where[count + i])
+        stack(rhs_ref, i, own_ref.at[k], first, second, near)
         copies.append(pltpu.make_async_copy(rhs_ref.at[i], out_ref.at[k], sems.at[i]))
         copies[-1].start()
     for copy in copies:
@@ -171,7 +199,8 @@
 def stacked(rhs, depth, own, firsts, seconds, places, near):
     replicas, rows, width = own.shape
     count = len(places)
-    args = [own] + [firsts[k] for k in places] + [seconds[k] for k in places]
+    arrays, where = gather_slots([firsts[k] for k in places] + [seconds[k] for k in places])
+    args = [own] + arrays
     specs = [VMEM] * len(args)
     alias = {}
     if rhs is not None:
@@ -179,7 +208,7 @@
         args.append(rhs)
         specs.append(pl.BlockSpec(memory_space=pl.ANY))
     return pl.pallas_call(
-        functools.partial(stack_kernel, places, near),
+        functools.partial(stack_kernel, places, near, where),
         out_shape=jax.ShapeDtypeStruct((replicas, depth, width), jnp.bfloat16),
         in_specs=specs,
         out_specs=pl.BlockSpec(memory_space=pl.ANY),
@@ -193,11 +222,11 @@
     )(*args)
 
 
-def project_kernel(places, near, tok_ref, own_ref, base_ref, mom_ref, *refs):
+def project_kernel(places, near, where, tok_ref, own_ref, base_ref, mom_ref, *refs):
     count = len(places)
     replicas, rows, width = own_ref.shape
-    firsts, seconds, stacked_ref = refs[:count], refs[count : 2 * count], refs[2 * count]
     out_hbm, new_base_hbm, new_mom_hbm, rhs_ref, out_ref, sems = refs[-6:]
+    stacked_ref = refs[-7]
     me = lax.axis_index("rep")
     copies = [
         pltpu.make_async_copy(base_ref, new_base_hbm, sems.at[replicas]),
@@ -220,7 +249,8 @@
         if k not in places:
             emit(k, stacked_ref[k])
     for i, k in enumerate(places):
-        stack(rhs_ref, i, own_ref.at[k], firsts[i], seconds[i], near)
+        first, second = at_slot(refs, where[i]), at_slot(refs, where[count + i])
+        stack(rhs_ref, i, own_ref.at[k], first, second, near)
         emit(k, rhs_ref[i])
     for copy in copies:
         copy.wait()
@@ -230,10 +260,12 @@
     replicas, rows, width = own.shape
     tall, depth = tokens.shape
     count = len(places)
-    args = [tokens, own, new_base, new_mom]
-    args += [firsts[k] for k in places] + [seconds[k] for k in places] + [rhs]
-    return pl.pallas_call(
-        functools.partial(project_kernel, places, near),
+    arrays, where = gather_slots([firsts[k] for k in places] + [seconds[k] for k in places])
+    args = [tokens, own, new_base, new_mom] + arrays
+    if rhs is not None:
+        args.append(rhs)
+    return pl.pallas_call(
+        functools.partial(project_kernel, places, near, where),
         out_shape=[
             jax.ShapeDtypeStruct((tall, width * replicas), jnp.bfloat16),
             jax.ShapeDtypeStruct(new_base.shape, jnp.float32),
@@ -270,15 +302,45 @@
     )(*xs)
 
 
+def pile_kernel(*refs):
+    for i, ref in enumerate(refs[:-1]):
+        refs[-1][i] = ref[...]
+
+
+def pile(xs):
+    return pl.pallas_call(
+        pile_kernel,
+        out_shape=jax.ShapeDtypeStruct((len(xs),) + xs[0].shape, xs[0].dtype),
+        cost_estimate=COST,
+        compiler_params=params(),
+    )(*xs)
+
+
+def share(held, groups):
+    slots = {2 * j: (x, None) for j, x in enumerate(held)}
+    for group in groups:
+        if len(group) == 1:
+            slots[2 * group[0] + 1] = (swap(held[group[0]], "rep", 1), None)
+        else:
+            got = swap(pile([held[j] for j in group]), "rep", 1)
+            for i, j in enumerate(group):
+                slots[2 * j + 1] = (got, i)
+    return [slots[k] for k in range(2 * len(held))]
+
+
+def after(x, *others):
+    return lax.optimization_barrier((x,) + others)[0]
+
+
 def on_device(base, local, momentum, tokens):
     replicas, groups = lax.axis_size("rep"), lax.axis_size("fsdp")
     chips = replicas // 2
     near = groups // 4
     width = base.shape[1] // replicas
 
-    send = encode(base, local, 1, chips, width)
+    (send,) = encode(base, local, 1, chips, width)
     recv = swap(send, "rep", 1)
-    keep = encode(base, local, 0, chips, width)
+    keep, tokens = encode(base, local, 0, chips, width, tokens)
     sums = chip_sum(keep, recv)
     parts = [swap(sums[j], "rep", 2 * j) for j in range(1, chips)]
     average, fresh = chunk_step(base, momentum, sums[0], parts, replicas)
@@ -288,11 +350,10 @@
     second = join(far[near:])
     firsts = [first] + [swap(first, "rep", 2 * j) for j in range(1, chips)]
     seconds = [second] + [swap(second, "rep", 2 * j) for j in range(1, chips)]
-    last = swap(second, "rep", 1)
-    firsts = [x for a in firsts for x in (a, swap(a, "rep", 1))]
+    firsts = [first] + [after(x, second) for x in firsts[1:]]
+    firsts = share(firsts, [range(chips)])
     new_base, new_momentum, own = outer(base, momentum, firsts, width)
-    lasts = [last] + [swap(a, "rep", 1) for a in seconds[:0:-1]][::-1]
-    seconds = [x for pair in zip(seconds, lasts) for x in pair]
+    seconds = share(seconds, [(0, chips - 1)] + [(j,) for j in range(chips - 2, 0, -1)])
 
     order = [(2 * j, 2 * j + 1) for j in [0] + list(range(chips - 1, 0, -1))]
     rhs = None

time: 36.2 us -> 35 us (0.967)
  starting transfers between devices: 17.4 us -> 16.5 us
  local copies, waits for them, and re-layouts: 0.45 us -> 0.01 us
    ppermute x21 -> x17, starting transfers between devices: 17.4 us -> 16.5 us  [swap(): lax.ppermute(x, axis, [(i, i ^ flip) for i in range(lax.axis_size(axis))])]
    unnamed x6 -> x4, local copies, waits for them, and re-layouts: 0.45 us -> 0.01 us
    ppermute x21 -> x17, waiting for transfers between devices: 10.6 us -> 10.9 us  [swap(): lax.ppermute(x, axis, [(i, i ^ flip) for i in range(lax.axis_size(axis))])]
    pallas_call x7 -> x9, Pallas kernels: 6.33 us -> 6.46 us  [the longest x2 3.05 us: encode(): pl.pallas_call(functools.partial(encode_kernel, flip), out_shape=shapes,...]
  transfers between devices with their start and end apart: 21 -> 17, of which waited for: 11 -> 11; matrix products, arithmetic and copies ran while one was open for 0% -> 0% of each run, Pallas kernels for 6% -> 6%
where the time goes in v4:
time: 35 us; the launch traced here: 34.8 us
  starting transfers between devices  16.5 us (47%)
  waiting for transfers between devices  10.9 us (31%)
  Pallas kernels  6.62 us (19%)
  between operations  0.76 us (2%)
    ppermute x17, starting transfers between devices, swap(): lax.ppermute(x, axis, [(i, i ^ flip) for i in range(lax.axis_size(axis))])  16.5 us
    ppermute x17, waiting for transfers between devices, swap(): lax.ppermute(x, axis, [(i, i ^ flip) for i in range(lax.axis_size(axis))])  10.9 us
    pallas_call x2, Pallas kernels, encode(): pl.pallas_call(functools.partial(encode_kernel, flip), out_shape=shapes,...  3.05 us
    pallas_call x1, Pallas kernels, project(): pl.pallas_call(functools.partial(project_kernel, places, near, where), ou...  2.73 us
  transfers between devices with their start and end apart: 17, of which 11 were waited for; matrix products, arithmetic and copies ran while one was open for 0% of the time, Pallas kernels for 6%

profile of v4, /device:TPU:0, one launch (start us, length us, event | category | flops | bytes accessed | tf_op | source)
XLA Modules:
  0.0 34.8 jit_solution(4380052356907870489)
XLA Ops:
  0.6 1.5 %shard_map.68 = bf16[4,32,1024]{2,1,0:T(8,128)(2,1)S(1)} custom-call(f32[32,8192]{1,0:T(8,128)} %base_ref.3, bf16[1,32,8192]{2,1,0:T(8,128)(2,1)} %local_hbm.3), custom_call_target="tpu_custom_call" | custom-call | flops 17179869184 | bytes 67108864 | tf_op jit(solution)/shard_map/pallas_call | solution.py:73
  2.2 0.5 %collective-permute-start = (bf16[4,32,1024]{2,1,0:T(8,128)(2,1)S(1)}, bf16[4,32,1024]{2,1,0:T(8,128)(2,1)S(1)}, u32[]{:S(2)}, u32[]{:S(2)}) collective-permute-start(bf16[4,32,1024]{2,1,0:T(8,128)(2,1)S(1)} %shard_map.68), channel_id=1, source_target_pairs={{0,4},{4,0},{8,12},{12,8},{16,20},{20,16},{24,28},{28,24},{1,5},{5... | collective-permute-start | bytes 786440 | tf_op jit(solution)/shard_map/ppermute | solution.py:286
  2.7 1.5 %shard_map.67 = (bf16[4,32,1024]{2,1,0:T(8,128)(2,1)S(1)}, bf16[256,128]{1,0:T(8,128)(2,1)S(1)}) custom-call(f32[32,8192]{1,0:T(8,128)} %base_ref.3, bf16[1,32,8192]{2,1,0:T(8,128)(2,1)} %local_hbm.3, bf16[256,128]{1,0:T(8,128)(2,1)} %refs_0_.1), custom_call_target="tpu_custom_call" | custom-call | flops 17179869184 | bytes 67108864 | tf_op jit(solution)/shard_map/pallas_call | solution.py:73
  4.3 2.6 %collective-permute-start.1 = (bf16[32,1024]{1,0:T(8,128)(2,1)S(1)}, bf16[32,1024]{1,0:T(8,128)(2,1)S(1)}, u32[]{:S(2)}, u32[]{:S(2)}) collective-permute-start(bf16[32,1024]{1,0:T(8,128)(2,1)S(1)} %get-tuple-element.23), channel_id=1, source_target_pairs={{0,8},{4,12},{8,0},{12,4},{16,24},{20,28},{24,16},{28,20},{1,9},{5... | collective-permute-start | bytes 196616 | tf_op jit(solution)/shard_map/ppermute | solution.py:286
  6.9 1.5 %collective-permute-start.2 = (bf16[32,1024]{1,0:T(8,128)(2,1)S(1)}, bf16[32,1024]{1,0:T(8,128)(2,1)S(1)}, u32[]{:S(2)}, u32[]{:S(2)}) collective-permute-start(bf16[32,1024]{1,0:T(8,128)(2,1)S(1)} %get-tuple-element.24), channel_id=1, source_target_pairs={{0,16},{4,20},{8,24},{12,28},{16,0},{20,4},{24,8},{28,12},{1,17},{... | collective-permute-start | bytes 196616 | tf_op jit(solution)/shard_map/ppermute | solution.py:286
  8.4 1.2 %collective-permute-done.1.refs_0_ = bf16[32,1024]{1,0:T(8,128)(2,1)S(1)} collective-permute-done((bf16[32,1024]{1,0:T(8,128)(2,1)S(1)}, bf16[32,1024]{1,0:T(8,128)(2,1)S(1)}, u32[]{:S(2)}, u32[]{:S(2)}) %collective-permute-start.1) | collective-permute-done | bytes 65568 | tf_op jit(solution)/shard_map/ppermute | solution.py:286
  9.6 1.5 %collective-permute-done.2.refs_1_ = bf16[32,1024]{1,0:T(8,128)(2,1)S(1)} collective-permute-done((bf16[32,1024]{1,0:T(8,128)(2,1)S(1)}, bf16[32,1024]{1,0:T(8,128)(2,1)S(1)}, u32[]{:S(2)}, u32[]{:S(2)}) %collective-permute-start.2) | collective-permute-done | bytes 65568 | tf_op jit(solution)/shard_map/ppermute | solution.py:286
  11.2 2.4 %collective-permute-done.3.refs_2_ = bf16[32,1024]{1,0:T(8,128)(2,1)S(1)} collective-permute-done((bf16[32,1024]{1,0:T(8,128)(2,1)S(1)}, bf16[32,1024]{1,0:T(8,128)(2,1)S(1)}, u32[]{:S(2)}, u32[]{:S(2)}) %collective-permute-start.3) | collective-permute-done | bytes 65568 | tf_op jit(solution)/shard_map/ppermute | solution.py:286
  13.6 0.1 shard_map.70
  13.7 1.6 %collective-permute-start.4 = (bf16[32,1024]{1,0:T(8,128)(2,1)S(1)}, bf16[32,1024]{1,0:T(8,128)(2,1)S(1)}, u32[]{:S(2)}, u32[]{:S(2)}) collective-permute-start(bf16[32,1024]{1,0:T(8,128)(2,1)S(1)} %get-tuple-element.27), channel_id=1, source_target_pairs={{0,1},{1,0},{2,3},{3,2},{4,5},{5,4},{6,7},{7,6},{8,9},{9,8},{10,11... | collective-permute-start | bytes 196616 | tf_op jit(solution)/shard_map/ppermute | solution.py:286
  15.3 2.5 %collective-permute-start.7 = (bf16[32,1024]{1,0:T(8,128)(2,1)S(1)}, bf16[32,1024]{1,0:T(8,128)(2,1)S(1)}, u32[]{:S(2)}, u32[]{:S(2)}) collective-permute-start(bf16[32,1024]{1,0:T(8,128)(2,1)S(1)} %get-tuple-element.27), channel_id=1, source_target_pairs={{0,3},{1,2},{2,1},{3,0},{4,7},{5,6},{6,5},{7,4},{8,11},{9,10},{10,... | collective-permute-start | bytes 196616 | tf_op jit(solution)/shard_map/ppermute | solution.py:286
  17.8 0.1 collective-permute-start.6
  17.9 0.1 collective-permute-done.4.refs_1_
  18.0 0.6 %collective-permute-start.9 = (bf16[64,1024]{1,0:T(8,128)(2,1)S(1)}, bf16[64,1024]{1,0:T(8,128)(2,1)S(1)}, u32[]{:S(2)}, u32[]{:S(2)}) collective-permute-start(bf16[64,1024]{1,0:T(8,128)(2,1)S(1)} %shard_map.71.refs_0_), channel_id=1, source_target_pairs={{0,24},{4,28},{8,16},{12,20},{16,8},{20,12},{24,0},{28,4},{1,25},{... | collective-permute-start | bytes 393224 | tf_op jit(solution)/shard_map/ppermute | solution.py:286
  18.6 1.5 %collective-permute-start.8 = (bf16[64,1024]{1,0:T(8,128)(2,1)S(1)}, bf16[64,1024]{1,0:T(8,128)(2,1)S(1)}, u32[]{:S(2)}, u32[]{:S(2)}) collective-permute-start(bf16[64,1024]{1,0:T(8,128)(2,1)S(1)} %shard_map.71.refs_0_), channel_id=1, source_target_pairs={{0,16},{4,20},{8,24},{12,28},{16,0},{20,4},{24,8},{28,12},{1,17},{... | collective-permute-start | bytes 393224 | tf_op jit(solution)/shard_map/ppermute | solution.py:286
  20.1 1.5 %collective-permute-start.5 = (bf16[64,1024]{1,0:T(8,128)(2,1)S(1)}, bf16[64,1024]{1,0:T(8,128)(2,1)S(1)}, u32[]{:S(2)}, u32[]{:S(2)}) collective-permute-start(bf16[64,1024]{1,0:T(8,128)(2,1)S(1)} %shard_map.71.refs_0_), channel_id=1, source_target_pairs={{0,8},{4,12},{8,0},{12,4},{16,24},{20,28},{24,16},{28,20},{1,9},{5... | collective-permute-start | bytes 393224 | tf_op jit(solution)/shard_map/ppermute | solution.py:286
  21.6 2.1 %collective-permute-done.6.refs_0_ = bf16[32,1024]{1,0:T(8,128)(2,1)S(1)} collective-permute-done((bf16[32,1024]{1,0:T(8,128)(2,1)S(1)}, bf16[32,1024]{1,0:T(8,128)(2,1)S(1)}, u32[]{:S(2)}, u32[]{:S(2)}) %collective-permute-start.6) | collective-permute-done | bytes 65568 | tf_op jit(solution)/shard_map/ppermute | solution.py:286
  23.7 0.5 %collective-permute-start.15 = (bf16[64,1024]{1,0:T(8,128)(2,1)S(1)}, bf16[64,1024]{1,0:T(8,128)(2,1)S(1)}, u32[]{:S(2)}, u32[]{:S(2)}) collective-permute-start(bf16[64,1024]{1,0:T(8,128)(2,1)S(1)} %shard_map.72.refs_0_.refs_2_), channel_id=1, source_target_pairs={{0,24},{4,28},{8,16},{12,20},{16,8},{20,12},{24,0},{28,4},{1,25},{... | collective-permute-start | bytes 393224 | tf_op jit(solution)/shard_map/ppermute | solution.py:286
  24.2 1.5 %collective-permute-start.13 = (bf16[64,1024]{1,0:T(8,128)(2,1)S(1)}, bf16[64,1024]{1,0:T(8,128)(2,1)S(1)}, u32[]{:S(2)}, u32[]{:S(2)}) collective-permute-start(bf16[64,1024]{1,0:T(8,128)(2,1)S(1)} %shard_map.72.refs_0_.refs_2_), channel_id=1, source_target_pairs={{0,16},{4,20},{8,24},{12,28},{16,0},{20,4},{24,8},{28,12},{1,17},{... | collective-permute-start | bytes 393224 | tf_op jit(solution)/shard_map/ppermute | solution.py:286
  25.7 1.5 %collective-permute-start.11 = (bf16[64,1024]{1,0:T(8,128)(2,1)S(1)}, bf16[64,1024]{1,0:T(8,128)(2,1)S(1)}, u32[]{:S(2)}, u32[]{:S(2)}) collective-permute-start(bf16[64,1024]{1,0:T(8,128)(2,1)S(1)} %shard_map.72.refs_0_.refs_2_), channel_id=1, source_target_pairs={{0,8},{4,12},{8,0},{12,4},{16,24},{20,28},{24,16},{28,20},{1,9},{5... | collective-permute-start | bytes 393224 | tf_op jit(solution)/shard_map/ppermute | solution.py:286
  27.3 2.7 %collective-permute-done.15.refs_1_.refs_2_ = bf16[64,1024]{1,0:T(8,128)(2,1)S(1)} collective-permute-done((bf16[64,1024]{1,0:T(8,128)(2,1)S(1)}, bf16[64,1024]{1,0:T(8,128)(2,1)S(1)}, u32[]{:S(2)}, u32[]{:S(2)}) %collective-permute-start.15) | collective-permute-done | bytes 131104 | tf_op jit(solution)/shard_map/ppermute | solution.py:286
  30.1 0.5 %collective-permute-done.13.refs_2_ = bf16[64,1024]{1,0:T(8,128)(2,1)S(1)} collective-permute-done((bf16[64,1024]{1,0:T(8,128)(2,1)S(1)}, bf16[64,1024]{1,0:T(8,128)(2,1)S(1)}, u32[]{:S(2)}, u32[]{:S(2)}) %collective-permute-start.13) | collective-permute-done | bytes 131104 | tf_op jit(solution)/shard_map/ppermute | solution.py:286
  30.6 0.1 collective-permute-done.11.refs_2_
  30.7 0.4 %collective-permute-start.12 = (bf16[64,1024]{1,0:T(8,128)(2,1)S(1)}, bf16[64,1024]{1,0:T(8,128)(2,1)S(1)}, u32[]{:S(2)}, u32[]{:S(2)}) collective-permute-start(bf16[64,1024]{1,0:T(8,128)(2,1)S(1)} %collective-permute-done.11.refs_2_), channel_id=1, source_target_pairs={{0,4},{4,0},{8,12},{12,8},{16,20},{20,16},{24,28},{28,24},{1,5},{5... | collective-permute-start | bytes 393224 | tf_op jit(solution)/shard_map/ppermute | solution.py:286
  31.1 0.3 shard_map.74
  31.4 0.2 collective-permute-done.16.refs_3_
  31.6 0.1 shard_map.76.refs_4_
  31.7 0.1 shard_map.77.refs_4_
  31.9 0.1 collective-permute-done.14.refs_3_
  31.9 0.1 shard_map.78.refs_4_
  32.0 0.1 collective-permute-done.12.refs_3_
  32.1 2.7 %shard_map.79 = (bf16[256,8192]{1,0:T(8,128)(2,1)}, f32[32,8192]{1,0:T(8,128)}, f32[32,8192]{1,0:T(8,128)}) custom-call(bf16[256,128]{1,0:T(8,128)(2,1)S(1)} %get-tuple-element.20.tok_ref, bf16[8,32,1024]{2,1,0:T(8,128)(2,1)S(1)} %get-tuple-element.31.own_ref, f32[32,8192]{1,0:T(8,128)S(1)} %get-tuple-element.32.base_ref, ...), custom_call_target="tpu_custom_call" | custom-call | flops 17179869184 | bytes 67108864 | tf_op jit(solution)/shard_map/pallas_call | solution.py:267
  (19 shorter events, 0.4 us)
Async XLA Ops:
  2.2 2.0 %collective-permute-start = (bf16[4,32,1024]{2,1,0:T(8,128)(2,1)S(1)}, bf16[4,32,1024]{2,1,0:T(8,128)(2,1)S(1)}, u32[]{:S(2)}, u32[]{:S(2)}) collective-permute-start(bf16[4,32,1024]{2,1,0:T(8,128)(2,1)S(1)} %shard_map.68), channel_id=1, source_target_pairs={{0,4},{4,0},{8,12},{12,8},{16,20},{20,16},{24,28},{28,24},{1,5},{5... | collective-permute-start | bytes 786440 | tf_op jit(solution)/shard_map/ppermute | solution.py:286
  4.2 9.4 %copy-start = (f32[32,8192]{1,0:T(8,128)S(1)}, f32[32,8192]{1,0:T(8,128)}, u32[]{:S(2)}) copy-start(f32[32,8192]{1,0:T(8,128)} %base_ref.3) | copy-start | bytes 3145732
  4.2 9.3 %copy-start.1 = (f32[32,8192]{1,0:T(8,128)S(1)}, f32[32,8192]{1,0:T(8,128)}, u32[]{:S(2)}) copy-start(f32[32,8192]{1,0:T(8,128)} %mom_ref.3) | copy-start | bytes 3145732
  4.3 5.3 %collective-permute-start.1 = (bf16[32,1024]{1,0:T(8,128)(2,1)S(1)}, bf16[32,1024]{1,0:T(8,128)(2,1)S(1)}, u32[]{:S(2)}, u32[]{:S(2)}) collective-permute-start(bf16[32,1024]{1,0:T(8,128)(2,1)S(1)} %get-tuple-element.23), channel_id=1, source_target_pairs={{0,8},{4,12},{8,0},{12,4},{16,24},{20,28},{24,16},{28,20},{1,9},{5... | collective-permute-start | bytes 196616 | tf_op jit(solution)/shard_map/ppermute | solution.py:286
  6.9 4.3 %collective-permute-start.2 = (bf16[32,1024]{1,0:T(8,128)(2,1)S(1)}, bf16[32,1024]{1,0:T(8,128)(2,1)S(1)}, u32[]{:S(2)}, u32[]{:S(2)}) collective-permute-start(bf16[32,1024]{1,0:T(8,128)(2,1)S(1)} %get-tuple-element.24), channel_id=1, source_target_pairs={{0,16},{4,20},{8,24},{12,28},{16,0},{20,4},{24,8},{28,12},{1,17},{... | collective-permute-start | bytes 196616 | tf_op jit(solution)/shard_map/ppermute | solution.py:286
  8.4 5.2 %collective-permute-start.3 = (bf16[32,1024]{1,0:T(8,128)(2,1)S(1)}, bf16[32,1024]{1,0:T(8,128)(2,1)S(1)}, u32[]{:S(2)}, u32[]{:S(2)}) collective-permute-start(bf16[32,1024]{1,0:T(8,128)(2,1)S(1)} %get-tuple-element.25), channel_id=1, source_target_pairs={{0,24},{4,28},{8,16},{12,20},{16,8},{20,12},{24,0},{28,4},{1,25},{... | collective-permute-start | bytes 196616 | tf_op jit(solution)/shard_map/ppermute | solution.py:286
  13.7 4.3 %collective-permute-start.4 = (bf16[32,1024]{1,0:T(8,128)(2,1)S(1)}, bf16[32,1024]{1,0:T(8,128)(2,1)S(1)}, u32[]{:S(2)}, u32[]{:S(2)}) collective-permute-start(bf16[32,1024]{1,0:T(8,128)(2,1)S(1)} %get-tuple-element.27), channel_id=1, source_target_pairs={{0,1},{1,0},{2,3},{3,2},{4,5},{5,4},{6,7},{7,6},{8,9},{9,8},{10,11... | collective-permute-start | bytes 196616 | tf_op jit(solution)/shard_map/ppermute | solution.py:286
  15.3 6.3 %collective-permute-start.7 = (bf16[32,1024]{1,0:T(8,128)(2,1)S(1)}, bf16[32,1024]{1,0:T(8,128)(2,1)S(1)}, u32[]{:S(2)}, u32[]{:S(2)}) collective-permute-start(bf16[32,1024]{1,0:T(8,128)(2,1)S(1)} %get-tuple-element.27), channel_id=1, source_target_pairs={{0,3},{1,2},{2,1},{3,0},{4,7},{5,6},{6,5},{7,4},{8,11},{9,10},{10,... | collective-permute-start | bytes 196616 | tf_op jit(solution)/shard_map/ppermute | solution.py:286
  17.8 5.9 %collective-permute-start.6 = (bf16[32,1024]{1,0:T(8,128)(2,1)S(1)}, bf16[32,1024]{1,0:T(8,128)(2,1)S(1)}, u32[]{:S(2)}, u32[]{:S(2)}) collective-permute-start(bf16[32,1024]{1,0:T(8,128)(2,1)S(1)} %get-tuple-element.27), channel_id=1, source_target_pairs={{0,2},{1,3},{2,0},{3,1},{4,6},{5,7},{6,4},{7,5},{8,10},{9,11},{10,... | collective-permute-start | bytes 196616 | tf_op jit(solution)/shard_map/ppermute | solution.py:286
  18.0 7.7 %collective-permute-start.9 = (bf16[64,1024]{1,0:T(8,128)(2,1)S(1)}, bf16[64,1024]{1,0:T(8,128)(2,1)S(1)}, u32[]{:S(2)}, u32[]{:S(2)}) collective-permute-start(bf16[64,1024]{1,0:T(8,128)(2,1)S(1)} %shard_map.71.refs_0_), channel_id=1, source_target_pairs={{0,24},{4,28},{8,16},{12,20},{16,8},{20,12},{24,0},{28,4},{1,25},{... | collective-permute-start | bytes 393224 | tf_op jit(solution)/shard_map/ppermute | solution.py:286
  18.6 8.7 %collective-permute-start.8 = (bf16[64,1024]{1,0:T(8,128)(2,1)S(1)}, bf16[64,1024]{1,0:T(8,128)(2,1)S(1)}, u32[]{:S(2)}, u32[]{:S(2)}) collective-permute-start(bf16[64,1024]{1,0:T(8,128)(2,1)S(1)} %shard_map.71.refs_0_), channel_id=1, source_target_pairs={{0,16},{4,20},{8,24},{12,28},{16,0},{20,4},{24,8},{28,12},{1,17},{... | collective-permute-start | bytes 393224 | tf_op jit(solution)/shard_map/ppermute | solution.py:286
  20.1 7.2 %collective-permute-start.5 = (bf16[64,1024]{1,0:T(8,128)(2,1)S(1)}, bf16[64,1024]{1,0:T(8,128)(2,1)S(1)}, u32[]{:S(2)}, u32[]{:S(2)}) collective-permute-start(bf16[64,1024]{1,0:T(8,128)(2,1)S(1)} %shard_map.71.refs_0_), channel_id=1, source_target_pairs={{0,8},{4,12},{8,0},{12,4},{16,24},{20,28},{24,16},{28,20},{1,9},{5... | collective-permute-start | bytes 393224 | tf_op jit(solution)/shard_map/ppermute | solution.py:286
  23.7 6.3 %collective-permute-start.15 = (bf16[64,1024]{1,0:T(8,128)(2,1)S(1)}, bf16[64,1024]{1,0:T(8,128)(2,1)S(1)}, u32[]{:S(2)}, u32[]{:S(2)}) collective-permute-start(bf16[64,1024]{1,0:T(8,128)(2,1)S(1)} %shard_map.72.refs_0_.refs_2_), channel_id=1, source_target_pairs={{0,24},{4,28},{8,16},{12,20},{16,8},{20,12},{24,0},{28,4},{1,25},{... | collective-permute-start | bytes 393224 | tf_op jit(solution)/shard_map/ppermute | solution.py:286
  24.2 6.4 %collective-permute-start.13 = (bf16[64,1024]{1,0:T(8,128)(2,1)S(1)}, bf16[64,1024]{1,0:T(8,128)(2,1)S(1)}, u32[]{:S(2)}, u32[]{:S(2)}) collective-permute-start(bf16[64,1024]{1,0:T(8,128)(2,1)S(1)} %shard_map.72.refs_0_.refs_2_), channel_id=1, source_target_pairs={{0,16},{4,20},{8,24},{12,28},{16,0},{20,4},{24,8},{28,12},{1,17},{... | collective-permute-start | bytes 393224 | tf_op jit(solution)/shard_map/ppermute | solution.py:286
  25.7 5.0 %collective-permute-start.11 = (bf16[64,1024]{1,0:T(8,128)(2,1)S(1)}, bf16[64,1024]{1,0:T(8,128)(2,1)S(1)}, u32[]{:S(2)}, u32[]{:S(2)}) collective-permute-start(bf16[64,1024]{1,0:T(8,128)(2,1)S(1)} %shard_map.72.refs_0_.refs_2_), channel_id=1, source_target_pairs={{0,8},{4,12},{8,0},{12,4},{16,24},{20,28},{24,16},{28,20},{1,9},{5... | collective-permute-start | bytes 393224 | tf_op jit(solution)/shard_map/ppermute | solution.py:286
  27.3 3.8 %collective-permute-start.10 = (bf16[4,64,1024]{2,1,0:T(8,128)(2,1)S(1)}, bf16[4,64,1024]{2,1,0:T(8,128)(2,1)S(1)}, u32[]{:S(2)}, u32[]{:S(2)}) collective-permute-start(bf16[4,64,1024]{2,1,0:T(8,128)(2,1)S(1)} %shard_map.73), channel_id=1, source_target_pairs={{0,4},{4,0},{8,12},{12,8},{16,20},{20,16},{24,28},{28,24},{1,5},{5... | collective-permute-start | bytes 1572872 | tf_op jit(solution)/shard_map/ppermute | solution.py:286
  30.0 1.6 %collective-permute-start.16 = (bf16[2,64,1024]{2,1,0:T(8,128)(2,1)S(1)}, bf16[2,64,1024]{2,1,0:T(8,128)(2,1)S(1)}, u32[]{:S(2)}, u32[]{:S(2)}) collective-permute-start(bf16[2,64,1024]{2,1,0:T(8,128)(2,1)S(1)} %shard_map.75), channel_id=1, source_target_pairs={{0,4},{4,0},{8,12},{12,8},{16,20},{20,16},{24,28},{28,24},{1,5},{5... | collective-permute-start | bytes 786440 | tf_op jit(solution)/shard_map/ppermute | solution.py:286
  30.6 1.3 %collective-permute-start.14 = (bf16[64,1024]{1,0:T(8,128)(2,1)S(1)}, bf16[64,1024]{1,0:T(8,128)(2,1)S(1)}, u32[]{:S(2)}, u32[]{:S(2)}) collective-permute-start(bf16[64,1024]{1,0:T(8,128)(2,1)S(1)} %collective-permute-done.13.refs_2_), channel_id=1, source_target_pairs={{0,4},{4,0},{8,12},{12,8},{16,20},{20,16},{24,28},{28,24},{1,5},{5... | collective-permute-start | bytes 393224 | tf_op jit(solution)/shard_map/ppermute | solution.py:286
  30.7 1.4 %collective-permute-start.12 = (bf16[64,1024]{1,0:T(8,128)(2,1)S(1)}, bf16[64,1024]{1,0:T(8,128)(2,1)S(1)}, u32[]{:S(2)}, u32[]{:S(2)}) collective-permute-start(bf16[64,1024]{1,0:T(8,128)(2,1)S(1)} %collective-permute-done.11.refs_2_), channel_id=1, source_target_pairs={{0,4},{4,0},{8,12},{12,8},{16,20},{20,16},{24,28},{28,24},{1,5},{5... | collective-permute-start | bytes 393224 | tf_op jit(solution)/shard_map/ppermute | solution.py:286

commit v5 on v4

--- a/solution.py
+++ b/solution.py
@@ -22,7 +22,8 @@
     return pltpu.CompilerParams(vmem_limit_bytes=mib * MIB)
 
 
-def columns(chunk, width):
+def columns(rep, width, replicas):
+    chunk = lax.rem(rep, 2) * (replicas // 2) + lax.div(rep, 2)
     return pl.ds(pl.multiple_of(chunk * width, width), width)
 
 
@@ -37,27 +38,34 @@
     *staged, tok_ref, base_ref, local_ref, sems = refs
     out_ref = staged[1] if staged else tok_ref
     chips, rows, width = out_ref.shape
+    pieces = sems.shape[1]
     me = lax.axis_index("rep")
+    core, chip = lax.rem(me ^ flip, 2), lax.div(me, 2)
+    piece = chips * width // pieces
     copies = []
     if staged:
         stage = pltpu.make_async_copy(staged[0], tok_ref, sems.at[2, 0])
-    for j in range(chips):
-        cols = columns(me ^ (flip ^ (2 * j)), width)
+    for p in range(pieces):
+        here = slice(p * piece, (p + 1) * piece)
+        there = pl.ds(pl.multiple_of((core * pieces + p) * piece, piece), piece)
         pair = (
-            pltpu.make_async_copy(base_hbm.at[:, cols], base_ref.at[j], sems.at[0, j]),
-            pltpu.make_async_copy(local_hbm.at[0, :, cols], local_ref.at[j], sems.at[1, j]),
+            pltpu.make_async_copy(base_hbm.at[:, there], base_ref.at[:, here], sems.at[0, p]),
+            pltpu.make_async_copy(local_hbm.at[0, :, there], local_ref.at[:, here], sems.at[1, p]),
         )
         for copy in pair:
             copy.start()
         copies.append(pair)
     if staged:
         stage.start()
-    for j in range(chips):
-        for copy in copies[j]:
+    for p in range(pieces):
+        for copy in copies[p]:
             copy.wait()
-        for b in range(width // BLOCK):
-            cols = slice(b * BLOCK, (b + 1) * BLOCK)
-            out_ref[j, :, cols] = decoded_block(base_ref[j, :, cols], local_ref[j, :, cols])
+        for c in range(p * chips // pieces, (p + 1) * chips // pieces):
+            for b in range(width // BLOCK):
+                cols = slice(c * width + b * BLOCK, c * width + (b + 1) * BLOCK)
+                out_ref[chip ^ c, :, b * BLOCK : (b + 1) * BLOCK] = decoded_block(
+                    base_ref[:, cols], local_ref[:, cols]
+                )
     if staged:
         stage.wait()
 
@@ -76,9 +84,9 @@
         in_specs=[HBM] * len(args),
         out_specs=[VMEM] * len(shapes),
         scratch_shapes=[
-            pltpu.VMEM((chips, rows, width), jnp.float32),
-            pltpu.VMEM((chips, rows, width), jnp.bfloat16),
-            pltpu.SemaphoreType.DMA((3, chips)),
+            pltpu.VMEM((rows, chips * width), jnp.float32),
+            pltpu.VMEM((rows, chips * width), jnp.bfloat16),
+            pltpu.SemaphoreType.DMA((3, 2)),
         ],
         cost_estimate=COST,
         compiler_params=params(),
@@ -111,7 +119,7 @@
 
 def chunk_step_kernel(replicas, base_ref, mom_ref, own_ref, *refs):
     parts, (avg_ref, fresh_ref) = refs[:-2], refs[-2:]
-    cols = columns(lax.axis_index("rep"), own_ref.shape[1])
+    cols = columns(lax.axis_index("rep"), own_ref.shape[1], replicas)
     total = own_ref[...]
     for part in parts:
         total = total + part[...].astype(jnp.float32)
@@ -150,7 +158,7 @@
     rows, width = fresh_ref.shape[1:]
     me = lax.axis_index("rep")
     for k, slot in enumerate(where):
-        cols = columns(me ^ k, width)
+        cols = columns(me ^ k, width, len(where))
         average = at_slot(holders, slot)[:rows, :].astype(jnp.float32)
         new_base, moved = stepped(average, base_ref[:, cols], mom_ref[:, cols])
         new_base_ref[:, cols] = new_base
@@ -240,7 +248,7 @@
             out_ref.dtype
         )
         copy = pltpu.make_async_copy(
-            out_ref.at[k], out_hbm.at[:, columns(me ^ k, width)], sems.at[k]
+            out_ref.at[k], out_hbm.at[:, columns(me ^ k, width, replicas)], sems.at[k]
         )
         copy.start()
         copies.append(copy)

time: 35 us -> 34.8 us (level)
  no operation moved by 1% of the time
where the time goes in v5:
time: 34.8 us; the launch traced here: 34.6 us
  starting transfers between devices  16.6 us (48%)
  waiting for transfers between devices  11 us (32%)
  Pallas kernels  6.28 us (18%)
  between operations  0.76 us (2%)
    ppermute x17, starting transfers between devices, swap(): lax.ppermute(x, axis, [(i, i ^ flip) for i in range(lax.axis_size(axis))])  16.6 us
    ppermute x17, waiting for transfers between devices, swap(): lax.ppermute(x, axis, [(i, i ^ flip) for i in range(lax.axis_size(axis))])  11 us
    pallas_call x1, Pallas kernels, project(): pl.pallas_call(functools.partial(project_kernel, places, near, where), ou...  2.73 us
    pallas_call x2, Pallas kernels, encode(): pl.pallas_call(functools.partial(encode_kernel, flip), out_shape=shapes,...  2.72 us
  transfers between devices with their start and end apart: 17, of which 11 were waited for; matrix products, arithmetic and copies ran while one was open for 0% of the time, Pallas kernels for 6%

profile of v5, /device:TPU:0, one launch (start us, length us, event | category | flops | bytes accessed | tf_op | source)
XLA Modules:
  0.0 34.6 jit_solution(16219717857559729075)
XLA Ops:
  0.6 1.4 %shard_map.68 = bf16[4,32,1024]{2,1,0:T(8,128)(2,1)S(1)} custom-call(f32[32,8192]{1,0:T(8,128)} %base_ref.3, bf16[1,32,8192]{2,1,0:T(8,128)(2,1)} %local_hbm.3), custom_call_target="tpu_custom_call" | custom-call | flops 17179869184 | bytes 67108864 | tf_op jit(solution)/shard_map/pallas_call | solution.py:81
  2.0 0.5 %collective-permute-start = (bf16[4,32,1024]{2,1,0:T(8,128)(2,1)S(1)}, bf16[4,32,1024]{2,1,0:T(8,128)(2,1)S(1)}, u32[]{:S(2)}, u32[]{:S(2)}) collective-permute-start(bf16[4,32,1024]{2,1,0:T(8,128)(2,1)S(1)} %shard_map.68), channel_id=1, source_target_pairs={{0,4},{4,0},{8,12},{12,8},{16,20},{20,16},{24,28},{28,24},{1,5},{5... | collective-permute-start | bytes 786440 | tf_op jit(solution)/shard_map/ppermute | solution.py:294
  2.5 1.4 %shard_map.67 = (bf16[4,32,1024]{2,1,0:T(8,128)(2,1)S(1)}, bf16[256,128]{1,0:T(8,128)(2,1)S(1)}) custom-call(f32[32,8192]{1,0:T(8,128)} %base_ref.3, bf16[1,32,8192]{2,1,0:T(8,128)(2,1)} %local_hbm.3, bf16[256,128]{1,0:T(8,128)(2,1)} %refs_0_.1), custom_call_target="tpu_custom_call" | custom-call | flops 17179869184 | bytes 67108864 | tf_op jit(solution)/shard_map/pallas_call | solution.py:81
  4.0 2.7 %collective-permute-start.1 = (bf16[32,1024]{1,0:T(8,128)(2,1)S(1)}, bf16[32,1024]{1,0:T(8,128)(2,1)S(1)}, u32[]{:S(2)}, u32[]{:S(2)}) collective-permute-start(bf16[32,1024]{1,0:T(8,128)(2,1)S(1)} %get-tuple-element.23), channel_id=1, source_target_pairs={{0,8},{4,12},{8,0},{12,4},{16,24},{20,28},{24,16},{28,20},{1,9},{5... | collective-permute-start | bytes 196616 | tf_op jit(solution)/shard_map/ppermute | solution.py:294
  6.7 1.5 %collective-permute-start.2 = (bf16[32,1024]{1,0:T(8,128)(2,1)S(1)}, bf16[32,1024]{1,0:T(8,128)(2,1)S(1)}, u32[]{:S(2)}, u32[]{:S(2)}) collective-permute-start(bf16[32,1024]{1,0:T(8,128)(2,1)S(1)} %get-tuple-element.24), channel_id=1, source_target_pairs={{0,16},{4,20},{8,24},{12,28},{16,0},{20,4},{24,8},{28,12},{1,17},{... | collective-permute-start | bytes 196616 | tf_op jit(solution)/shard_map/ppermute | solution.py:294
  8.2 1.1 %collective-permute-done.1.refs_0_ = bf16[32,1024]{1,0:T(8,128)(2,1)S(1)} collective-permute-done((bf16[32,1024]{1,0:T(8,128)(2,1)S(1)}, bf16[32,1024]{1,0:T(8,128)(2,1)S(1)}, u32[]{:S(2)}, u32[]{:S(2)}) %collective-permute-start.1) | collective-permute-done | bytes 65568 | tf_op jit(solution)/shard_map/ppermute | solution.py:294
  9.3 1.6 %collective-permute-done.2.refs_1_ = bf16[32,1024]{1,0:T(8,128)(2,1)S(1)} collective-permute-done((bf16[32,1024]{1,0:T(8,128)(2,1)S(1)}, bf16[32,1024]{1,0:T(8,128)(2,1)S(1)}, u32[]{:S(2)}, u32[]{:S(2)}) %collective-permute-start.2) | collective-permute-done | bytes 65568 | tf_op jit(solution)/shard_map/ppermute | solution.py:294
  11.0 2.4 %collective-permute-done.3.refs_2_ = bf16[32,1024]{1,0:T(8,128)(2,1)S(1)} collective-permute-done((bf16[32,1024]{1,0:T(8,128)(2,1)S(1)}, bf16[32,1024]{1,0:T(8,128)(2,1)S(1)}, u32[]{:S(2)}, u32[]{:S(2)}) %collective-permute-start.3) | collective-permute-done | bytes 65568 | tf_op jit(solution)/shard_map/ppermute | solution.py:294
  13.4 0.1 shard_map.70
  13.5 1.6 %collective-permute-start.4 = (bf16[32,1024]{1,0:T(8,128)(2,1)S(1)}, bf16[32,1024]{1,0:T(8,128)(2,1)S(1)}, u32[]{:S(2)}, u32[]{:S(2)}) collective-permute-start(bf16[32,1024]{1,0:T(8,128)(2,1)S(1)} %get-tuple-element.27), channel_id=1, source_target_pairs={{0,1},{1,0},{2,3},{3,2},{4,5},{5,4},{6,7},{7,6},{8,9},{9,8},{10,11... | collective-permute-start | bytes 196616 | tf_op jit(solution)/shard_map/ppermute | solution.py:294
  15.1 2.5 %collective-permute-start.7 = (bf16[32,1024]{1,0:T(8,128)(2,1)S(1)}, bf16[32,1024]{1,0:T(8,128)(2,1)S(1)}, u32[]{:S(2)}, u32[]{:S(2)}) collective-permute-start(bf16[32,1024]{1,0:T(8,128)(2,1)S(1)} %get-tuple-element.27), channel_id=1, source_target_pairs={{0,3},{1,2},{2,1},{3,0},{4,7},{5,6},{6,5},{7,4},{8,11},{9,10},{10,... | collective-permute-start | bytes 196616 | tf_op jit(solution)/shard_map/ppermute | solution.py:294
  17.6 0.1 collective-permute-start.6
  17.7 0.1 collective-permute-done.4.refs_1_
  17.8 0.6 %collective-permute-start.9 = (bf16[64,1024]{1,0:T(8,128)(2,1)S(1)}, bf16[64,1024]{1,0:T(8,128)(2,1)S(1)}, u32[]{:S(2)}, u32[]{:S(2)}) collective-permute-start(bf16[64,1024]{1,0:T(8,128)(2,1)S(1)} %shard_map.71.refs_0_), channel_id=1, source_target_pairs={{0,24},{4,28},{8,16},{12,20},{16,8},{20,12},{24,0},{28,4},{1,25},{... | collective-permute-start | bytes 393224 | tf_op jit(solution)/shard_map/ppermute | solution.py:294
  18.4 1.5 %collective-permute-start.8 = (bf16[64,1024]{1,0:T(8,128)(2,1)S(1)}, bf16[64,1024]{1,0:T(8,128)(2,1)S(1)}, u32[]{:S(2)}, u32[]{:S(2)}) collective-permute-start(bf16[64,1024]{1,0:T(8,128)(2,1)S(1)} %shard_map.71.refs_0_), channel_id=1, source_target_pairs={{0,16},{4,20},{8,24},{12,28},{16,0},{20,4},{24,8},{28,12},{1,17},{... | collective-permute-start | bytes 393224 | tf_op jit(solution)/shard_map/ppermute | solution.py:294
  19.9 1.5 %collective-permute-start.5 = (bf16[64,1024]{1,0:T(8,128)(2,1)S(1)}, bf16[64,1024]{1,0:T(8,128)(2,1)S(1)}, u32[]{:S(2)}, u32[]{:S(2)}) collective-permute-start(bf16[64,1024]{1,0:T(8,128)(2,1)S(1)} %shard_map.71.refs_0_), channel_id=1, source_target_pairs={{0,8},{4,12},{8,0},{12,4},{16,24},{20,28},{24,16},{28,20},{1,9},{5... | collective-permute-start | bytes 393224 | tf_op jit(solution)/shard_map/ppermute | solution.py:294
  21.4 2.1 %collective-permute-done.6.refs_0_ = bf16[32,1024]{1,0:T(8,128)(2,1)S(1)} collective-permute-done((bf16[32,1024]{1,0:T(8,128)(2,1)S(1)}, bf16[32,1024]{1,0:T(8,128)(2,1)S(1)}, u32[]{:S(2)}, u32[]{:S(2)}) %collective-permute-start.6) | collective-permute-done | bytes 65568 | tf_op jit(solution)/shard_map/ppermute | solution.py:294
  23.5 0.5 %collective-permute-start.15 = (bf16[64,1024]{1,0:T(8,128)(2,1)S(1)}, bf16[64,1024]{1,0:T(8,128)(2,1)S(1)}, u32[]{:S(2)}, u32[]{:S(2)}) collective-permute-start(bf16[64,1024]{1,0:T(8,128)(2,1)S(1)} %shard_map.72.refs_0_.refs_2_), channel_id=1, source_target_pairs={{0,24},{4,28},{8,16},{12,20},{16,8},{20,12},{24,0},{28,4},{1,25},{... | collective-permute-start | bytes 393224 | tf_op jit(solution)/shard_map/ppermute | solution.py:294
  24.0 1.5 %collective-permute-start.13 = (bf16[64,1024]{1,0:T(8,128)(2,1)S(1)}, bf16[64,1024]{1,0:T(8,128)(2,1)S(1)}, u32[]{:S(2)}, u32[]{:S(2)}) collective-permute-start(bf16[64,1024]{1,0:T(8,128)(2,1)S(1)} %shard_map.72.refs_0_.refs_2_), channel_id=1, source_target_pairs={{0,16},{4,20},{8,24},{12,28},{16,0},{20,4},{24,8},{28,12},{1,17},{... | collective-permute-start | bytes 393224 | tf_op jit(solution)/shard_map/ppermute | solution.py:294
  25.5 1.5 %collective-permute-start.11 = (bf16[64,1024]{1,0:T(8,128)(2,1)S(1)}, bf16[64,1024]{1,0:T(8,128)(2,1)S(1)}, u32[]{:S(2)}, u32[]{:S(2)}) collective-permute-start(bf16[64,1024]{1,0:T(8,128)(2,1)S(1)} %shard_map.72.refs_0_.refs_2_), channel_id=1, source_target_pairs={{0,8},{4,12},{8,0},{12,4},{16,24},{20,28},{24,16},{28,20},{1,9},{5... | collective-permute-start | bytes 393224 | tf_op jit(solution)/shard_map/ppermute | solution.py:294
  27.1 2.5 %collective-permute-done.15.refs_1_.refs_2_ = bf16[64,1024]{1,0:T(8,128)(2,1)S(1)} collective-permute-done((bf16[64,1024]{1,0:T(8,128)(2,1)S(1)}, bf16[64,1024]{1,0:T(8,128)(2,1)S(1)}, u32[]{:S(2)}, u32[]{:S(2)}) %collective-permute-start.15) | collective-permute-done | bytes 131104 | tf_op jit(solution)/shard_map/ppermute | solution.py:294
  29.7 0.1 collective-permute-start.16
  29.7 0.6 %collective-permute-done.13.refs_2_ = bf16[64,1024]{1,0:T(8,128)(2,1)S(1)} collective-permute-done((bf16[64,1024]{1,0:T(8,128)(2,1)S(1)}, bf16[64,1024]{1,0:T(8,128)(2,1)S(1)}, u32[]{:S(2)}, u32[]{:S(2)}) %collective-permute-start.13) | collective-permute-done | bytes 131104 | tf_op jit(solution)/shard_map/ppermute | solution.py:294
  30.4 0.1 collective-permute-done.11.refs_2_
  30.5 0.4 %collective-permute-start.12 = (bf16[64,1024]{1,0:T(8,128)(2,1)S(1)}, bf16[64,1024]{1,0:T(8,128)(2,1)S(1)}, u32[]{:S(2)}, u32[]{:S(2)}) collective-permute-start(bf16[64,1024]{1,0:T(8,128)(2,1)S(1)} %collective-permute-done.11.refs_2_), channel_id=1, source_target_pairs={{0,4},{4,0},{8,12},{12,8},{16,20},{20,16},{24,28},{28,24},{1,5},{5... | collective-permute-start | bytes 393224 | tf_op jit(solution)/shard_map/ppermute | solution.py:294
  30.9 0.3 shard_map.74
  31.3 0.1 shard_map.76.refs_4_
  31.4 0.1 shard_map.77.refs_4_
  31.5 0.2 collective-permute-done.14.refs_3_
  31.7 0.1 shard_map.78.refs_4_
  31.8 0.1 collective-permute-done.12.refs_3_
  31.9 2.7 %shard_map.79 = (bf16[256,8192]{1,0:T(8,128)(2,1)}, f32[32,8192]{1,0:T(8,128)}, f32[32,8192]{1,0:T(8,128)}) custom-call(bf16[256,128]{1,0:T(8,128)(2,1)S(1)} %get-tuple-element.20.tok_ref, bf16[8,32,1024]{2,1,0:T(8,128)(2,1)S(1)} %get-tuple-element.31.own_ref, f32[32,8192]{1,0:T(8,128)S(1)} %get-tuple-element.32.base_ref, ...), custom_call_target="tpu_custom_call" | custom-call | flops 17179869184 | bytes 67108864 | tf_op jit(solution)/shard_map/pallas_call | solution.py:275
  (19 shorter events, 0.3 us)
Async XLA Ops:
  2.0 1.9 %collective-permute-start = (bf16[4,32,1024]{2,1,0:T(8,128)(2,1)S(1)}, bf16[4,32,1024]{2,1,0:T(8,128)(2,1)S(1)}, u32[]{:S(2)}, u32[]{:S(2)}) collective-permute-start(bf16[4,32,1024]{2,1,0:T(8,128)(2,1)S(1)} %shard_map.68), channel_id=1, source_target_pairs={{0,4},{4,0},{8,12},{12,8},{16,20},{20,16},{24,28},{28,24},{1,5},{5... | collective-permute-start | bytes 786440 | tf_op jit(solution)/shard_map/ppermute | solution.py:294
  3.9 9.5 %copy-start = (f32[32,8192]{1,0:T(8,128)S(1)}, f32[32,8192]{1,0:T(8,128)}, u32[]{:S(2)}) copy-start(f32[32,8192]{1,0:T(8,128)} %base_ref.3) | copy-start | bytes 3145732
  3.9 9.5 %copy-start.1 = (f32[32,8192]{1,0:T(8,128)S(1)}, f32[32,8192]{1,0:T(8,128)}, u32[]{:S(2)}) copy-start(f32[32,8192]{1,0:T(8,128)} %mom_ref.3) | copy-start | bytes 3145732
  4.0 5.3 %collective-permute-start.1 = (bf16[32,1024]{1,0:T(8,128)(2,1)S(1)}, bf16[32,1024]{1,0:T(8,128)(2,1)S(1)}, u32[]{:S(2)}, u32[]{:S(2)}) collective-permute-start(bf16[32,1024]{1,0:T(8,128)(2,1)S(1)} %get-tuple-element.23), channel_id=1, source_target_pairs={{0,8},{4,12},{8,0},{12,4},{16,24},{20,28},{24,16},{28,20},{1,9},{5... | collective-permute-start | bytes 196616 | tf_op jit(solution)/shard_map/ppermute | solution.py:294
  6.7 4.3 %collective-permute-start.2 = (bf16[32,1024]{1,0:T(8,128)(2,1)S(1)}, bf16[32,1024]{1,0:T(8,128)(2,1)S(1)}, u32[]{:S(2)}, u32[]{:S(2)}) collective-permute-start(bf16[32,1024]{1,0:T(8,128)(2,1)S(1)} %get-tuple-element.24), channel_id=1, source_target_pairs={{0,16},{4,20},{8,24},{12,28},{16,0},{20,4},{24,8},{28,12},{1,17},{... | collective-permute-start | bytes 196616 | tf_op jit(solution)/shard_map/ppermute | solution.py:294
  8.2 5.2 %collective-permute-start.3 = (bf16[32,1024]{1,0:T(8,128)(2,1)S(1)}, bf16[32,1024]{1,0:T(8,128)(2,1)S(1)}, u32[]{:S(2)}, u32[]{:S(2)}) collective-permute-start(bf16[32,1024]{1,0:T(8,128)(2,1)S(1)} %get-tuple-element.25), channel_id=1, source_target_pairs={{0,24},{4,28},{8,16},{12,20},{16,8},{20,12},{24,0},{28,4},{1,25},{... | collective-permute-start | bytes 196616 | tf_op jit(solution)/shard_map/ppermute | solution.py:294
  13.5 4.3 %collective-permute-start.4 = (bf16[32,1024]{1,0:T(8,128)(2,1)S(1)}, bf16[32,1024]{1,0:T(8,128)(2,1)S(1)}, u32[]{:S(2)}, u32[]{:S(2)}) collective-permute-start(bf16[32,1024]{1,0:T(8,128)(2,1)S(1)} %get-tuple-element.27), channel_id=1, source_target_pairs={{0,1},{1,0},{2,3},{3,2},{4,5},{5,4},{6,7},{7,6},{8,9},{9,8},{10,11... | collective-permute-start | bytes 196616 | tf_op jit(solution)/shard_map/ppermute | solution.py:294
  15.1 6.3 %collective-permute-start.7 = (bf16[32,1024]{1,0:T(8,128)(2,1)S(1)}, bf16[32,1024]{1,0:T(8,128)(2,1)S(1)}, u32[]{:S(2)}, u32[]{:S(2)}) collective-permute-start(bf16[32,1024]{1,0:T(8,128)(2,1)S(1)} %get-tuple-element.27), channel_id=1, source_target_pairs={{0,3},{1,2},{2,1},{3,0},{4,7},{5,6},{6,5},{7,4},{8,11},{9,10},{10,... | collective-permute-start | bytes 196616 | tf_op jit(solution)/shard_map/ppermute | solution.py:294
  17.6 5.9 %collective-permute-start.6 = (bf16[32,1024]{1,0:T(8,128)(2,1)S(1)}, bf16[32,1024]{1,0:T(8,128)(2,1)S(1)}, u32[]{:S(2)}, u32[]{:S(2)}) collective-permute-start(bf16[32,1024]{1,0:T(8,128)(2,1)S(1)} %get-tuple-element.27), channel_id=1, source_target_pairs={{0,2},{1,3},{2,0},{3,1},{4,6},{5,7},{6,4},{7,5},{8,10},{9,11},{10,... | collective-permute-start | bytes 196616 | tf_op jit(solution)/shard_map/ppermute | solution.py:294
  17.8 7.7 %collective-permute-start.9 = (bf16[64,1024]{1,0:T(8,128)(2,1)S(1)}, bf16[64,1024]{1,0:T(8,128)(2,1)S(1)}, u32[]{:S(2)}, u32[]{:S(2)}) collective-permute-start(bf16[64,1024]{1,0:T(8,128)(2,1)S(1)} %shard_map.71.refs_0_), channel_id=1, source_target_pairs={{0,24},{4,28},{8,16},{12,20},{16,8},{20,12},{24,0},{28,4},{1,25},{... | collective-permute-start | bytes 393224 | tf_op jit(solution)/shard_map/ppermute | solution.py:294
  18.4 8.7 %collective-permute-start.8 = (bf16[64,1024]{1,0:T(8,128)(2,1)S(1)}, bf16[64,1024]{1,0:T(8,128)(2,1)S(1)}, u32[]{:S(2)}, u32[]{:S(2)}) collective-permute-start(bf16[64,1024]{1,0:T(8,128)(2,1)S(1)} %shard_map.71.refs_0_), channel_id=1, source_target_pairs={{0,16},{4,20},{8,24},{12,28},{16,0},{20,4},{24,8},{28,12},{1,17},{... | collective-permute-start | bytes 393224 | tf_op jit(solution)/shard_map/ppermute | solution.py:294
  19.9 7.2 %collective-permute-start.5 = (bf16[64,1024]{1,0:T(8,128)(2,1)S(1)}, bf16[64,1024]{1,0:T(8,128)(2,1)S(1)}, u32[]{:S(2)}, u32[]{:S(2)}) collective-permute-start(bf16[64,1024]{1,0:T(8,128)(2,1)S(1)} %shard_map.71.refs_0_), channel_id=1, source_target_pairs={{0,8},{4,12},{8,0},{12,4},{16,24},{20,28},{24,16},{28,20},{1,9},{5... | collective-permute-start | bytes 393224 | tf_op jit(solution)/shard_map/ppermute | solution.py:294
  23.5 6.2 %collective-permute-start.15 = (bf16[64,1024]{1,0:T(8,128)(2,1)S(1)}, bf16[64,1024]{1,0:T(8,128)(2,1)S(1)}, u32[]{:S(2)}, u32[]{:S(2)}) collective-permute-start(bf16[64,1024]{1,0:T(8,128)(2,1)S(1)} %shard_map.72.refs_0_.refs_2_), channel_id=1, source_target_pairs={{0,24},{4,28},{8,16},{12,20},{16,8},{20,12},{24,0},{28,4},{1,25},{... | collective-permute-start | bytes 393224 | tf_op jit(solution)/shard_map/ppermute | solution.py:294
  24.0 6.4 %collective-permute-start.13 = (bf16[64,1024]{1,0:T(8,128)(2,1)S(1)}, bf16[64,1024]{1,0:T(8,128)(2,1)S(1)}, u32[]{:S(2)}, u32[]{:S(2)}) collective-permute-start(bf16[64,1024]{1,0:T(8,128)(2,1)S(1)} %shard_map.72.refs_0_.refs_2_), channel_id=1, source_target_pairs={{0,16},{4,20},{8,24},{12,28},{16,0},{20,4},{24,8},{28,12},{1,17},{... | collective-permute-start | bytes 393224 | tf_op jit(solution)/shard_map/ppermute | solution.py:294
  25.5 5.0 %collective-permute-start.11 = (bf16[64,1024]{1,0:T(8,128)(2,1)S(1)}, bf16[64,1024]{1,0:T(8,128)(2,1)S(1)}, u32[]{:S(2)}, u32[]{:S(2)}) collective-permute-start(bf16[64,1024]{1,0:T(8,128)(2,1)S(1)} %shard_map.72.refs_0_.refs_2_), channel_id=1, source_target_pairs={{0,8},{4,12},{8,0},{12,4},{16,24},{20,28},{24,16},{28,20},{1,9},{5... | collective-permute-start | bytes 393224 | tf_op jit(solution)/shard_map/ppermute | solution.py:294
  27.1 3.8 %collective-permute-start.10 = (bf16[4,64,1024]{2,1,0:T(8,128)(2,1)S(1)}, bf16[4,64,1024]{2,1,0:T(8,128)(2,1)S(1)}, u32[]{:S(2)}, u32[]{:S(2)}) collective-permute-start(bf16[4,64,1024]{2,1,0:T(8,128)(2,1)S(1)} %shard_map.73), channel_id=1, source_target_pairs={{0,4},{4,0},{8,12},{12,8},{16,20},{20,16},{24,28},{28,24},{1,5},{5... | collective-permute-start | bytes 1572872 | tf_op jit(solution)/shard_map/ppermute | solution.py:294
  29.7 1.6 %collective-permute-start.16 = (bf16[2,64,1024]{2,1,0:T(8,128)(2,1)S(1)}, bf16[2,64,1024]{2,1,0:T(8,128)(2,1)S(1)}, u32[]{:S(2)}, u32[]{:S(2)}) collective-permute-start(bf16[2,64,1024]{2,1,0:T(8,128)(2,1)S(1)} %shard_map.75), channel_id=1, source_target_pairs={{0,4},{4,0},{8,12},{12,8},{16,20},{20,16},{24,28},{28,24},{1,5},{5... | collective-permute-start | bytes 786440 | tf_op jit(solution)/shard_map/ppermute | solution.py:294
  30.4 1.3 %collective-permute-start.14 = (bf16[64,1024]{1,0:T(8,128)(2,1)S(1)}, bf16[64,1024]{1,0:T(8,128)(2,1)S(1)}, u32[]{:S(2)}, u32[]{:S(2)}) collective-permute-start(bf16[64,1024]{1,0:T(8,128)(2,1)S(1)} %collective-permute-done.13.refs_2_), channel_id=1, source_target_pairs={{0,4},{4,0},{8,12},{12,8},{16,20},{20,16},{24,28},{28,24},{1,5},{5... | collective-permute-start | bytes 393224 | tf_op jit(solution)/shard_map/ppermute | solution.py:294
  30.5 1.4 %collective-permute-start.12 = (bf16[64,1024]{1,0:T(8,128)(2,1)S(1)}, bf16[64,1024]{1,0:T(8,128)(2,1)S(1)}, u32[]{:S(2)}, u32[]{:S(2)}) collective-permute-start(bf16[64,1024]{1,0:T(8,128)(2,1)S(1)} %collective-permute-done.11.refs_2_), channel_id=1, source_target_pairs={{0,4},{4,0},{8,12},{12,8},{16,20},{20,16},{24,28},{28,24},{1,5},{5... | collective-permute-start | bytes 393224 | tf_op jit(solution)/shard_map/ppermute | solution.py:294

commit v6 on v5

--- a/solution.py
+++ b/solution.py
@@ -364,6 +364,7 @@
     seconds = share(seconds, [(0, chips - 1)] + [(j,) for j in range(chips - 2, 0, -1)])
 
     order = [(2 * j, 2 * j + 1) for j in [0] + list(range(chips - 1, 0, -1))]
+    order = order[1:2] + order[:1] + order[2:]
     rhs = None
     for places in order[:-1]:
         rhs = stacked(rhs, tokens.shape[1], own, firsts, seconds, places, near)

time: 34.8 us -> 34.8 us (level)
  no operation moved by 1% of the time
where the time goes in v6:
time: 34.8 us; the launch traced here: 34.6 us
  starting transfers between devices  16.6 us (48%)
  waiting for transfers between devices  11 us (32%)
  Pallas kernels  6.28 us (18%)
  between operations  0.76 us (2%)
    ppermute x17, starting transfers between devices, swap(): lax.ppermute(x, axis, [(i, i ^ flip) for i in range(lax.axis_size(axis))])  16.6 us
    ppermute x17, waiting for transfers between devices, swap(): lax.ppermute(x, axis, [(i, i ^ flip) for i in range(lax.axis_size(axis))])  11 us
    pallas_call x1, Pallas kernels, project(): pl.pallas_call(functools.partial(project_kernel, places, near, where), ou...  2.73 us
    pallas_call x2, Pallas kernels, encode(): pl.pallas_call(functools.partial(encode_kernel, flip), out_shape=shapes,...  2.72 us
  transfers between devices with their start and end apart: 17, of which 11 were waited for; matrix products, arithmetic and copies ran while one was open for 0% of the time, Pallas kernels for 6%

profile of v6, /device:TPU:0, one launch (start us, length us, event | category | flops | bytes accessed | tf_op | source)
XLA Modules:
  0.0 34.6 jit_solution(10295287203014096406)
XLA Ops:
  0.6 1.4 %shard_map.68 = bf16[4,32,1024]{2,1,0:T(8,128)(2,1)S(1)} custom-call(f32[32,8192]{1,0:T(8,128)} %base_ref.3, bf16[1,32,8192]{2,1,0:T(8,128)(2,1)} %local_hbm.3), custom_call_target="tpu_custom_call" | custom-call | flops 17179869184 | bytes 67108864 | tf_op jit(solution)/shard_map/pallas_call | solution.py:81
  2.0 0.5 %collective-permute-start = (bf16[4,32,1024]{2,1,0:T(8,128)(2,1)S(1)}, bf16[4,32,1024]{2,1,0:T(8,128)(2,1)S(1)}, u32[]{:S(2)}, u32[]{:S(2)}) collective-permute-start(bf16[4,32,1024]{2,1,0:T(8,128)(2,1)S(1)} %shard_map.68), channel_id=1, source_target_pairs={{0,4},{4,0},{8,12},{12,8},{16,20},{20,16},{24,28},{28,24},{1,5},{5... | collective-permute-start | bytes 786440 | tf_op jit(solution)/shard_map/ppermute | solution.py:294
  2.5 1.4 %shard_map.67 = (bf16[4,32,1024]{2,1,0:T(8,128)(2,1)S(1)}, bf16[256,128]{1,0:T(8,128)(2,1)S(1)}) custom-call(f32[32,8192]{1,0:T(8,128)} %base_ref.3, bf16[1,32,8192]{2,1,0:T(8,128)(2,1)} %local_hbm.3, bf16[256,128]{1,0:T(8,128)(2,1)} %refs_0_.1), custom_call_target="tpu_custom_call" | custom-call | flops 17179869184 | bytes 67108864 | tf_op jit(solution)/shard_map/pallas_call | solution.py:81
  4.0 2.7 %collective-permute-start.1 = (bf16[32,1024]{1,0:T(8,128)(2,1)S(1)}, bf16[32,1024]{1,0:T(8,128)(2,1)S(1)}, u32[]{:S(2)}, u32[]{:S(2)}) collective-permute-start(bf16[32,1024]{1,0:T(8,128)(2,1)S(1)} %get-tuple-element.23), channel_id=1, source_target_pairs={{0,8},{4,12},{8,0},{12,4},{16,24},{20,28},{24,16},{28,20},{1,9},{5... | collective-permute-start | bytes 196616 | tf_op jit(solution)/shard_map/ppermute | solution.py:294
  6.7 1.5 %collective-permute-start.2 = (bf16[32,1024]{1,0:T(8,128)(2,1)S(1)}, bf16[32,1024]{1,0:T(8,128)(2,1)S(1)}, u32[]{:S(2)}, u32[]{:S(2)}) collective-permute-start(bf16[32,1024]{1,0:T(8,128)(2,1)S(1)} %get-tuple-element.24), channel_id=1, source_target_pairs={{0,16},{4,20},{8,24},{12,28},{16,0},{20,4},{24,8},{28,12},{1,17},{... | collective-permute-start | bytes 196616 | tf_op jit(solution)/shard_map/ppermute | solution.py:294
  8.2 1.1 %collective-permute-done.1.refs_0_ = bf16[32,1024]{1,0:T(8,128)(2,1)S(1)} collective-permute-done((bf16[32,1024]{1,0:T(8,128)(2,1)S(1)}, bf16[32,1024]{1,0:T(8,128)(2,1)S(1)}, u32[]{:S(2)}, u32[]{:S(2)}) %collective-permute-start.1) | collective-permute-done | bytes 65568 | tf_op jit(solution)/shard_map/ppermute | solution.py:294
  9.3 1.6 %collective-permute-done.2.refs_1_ = bf16[32,1024]{1,0:T(8,128)(2,1)S(1)} collective-permute-done((bf16[32,1024]{1,0:T(8,128)(2,1)S(1)}, bf16[32,1024]{1,0:T(8,128)(2,1)S(1)}, u32[]{:S(2)}, u32[]{:S(2)}) %collective-permute-start.2) | collective-permute-done | bytes 65568 | tf_op jit(solution)/shard_map/ppermute | solution.py:294
  11.0 2.4 %collective-permute-done.3.refs_2_ = bf16[32,1024]{1,0:T(8,128)(2,1)S(1)} collective-permute-done((bf16[32,1024]{1,0:T(8,128)(2,1)S(1)}, bf16[32,1024]{1,0:T(8,128)(2,1)S(1)}, u32[]{:S(2)}, u32[]{:S(2)}) %collective-permute-start.3) | collective-permute-done | bytes 65568 | tf_op jit(solution)/shard_map/ppermute | solution.py:294
  13.4 0.1 shard_map.70
  13.5 1.6 %collective-permute-start.4 = (bf16[32,1024]{1,0:T(8,128)(2,1)S(1)}, bf16[32,1024]{1,0:T(8,128)(2,1)S(1)}, u32[]{:S(2)}, u32[]{:S(2)}) collective-permute-start(bf16[32,1024]{1,0:T(8,128)(2,1)S(1)} %get-tuple-element.27), channel_id=1, source_target_pairs={{0,1},{1,0},{2,3},{3,2},{4,5},{5,4},{6,7},{7,6},{8,9},{9,8},{10,11... | collective-permute-start | bytes 196616 | tf_op jit(solution)/shard_map/ppermute | solution.py:294
  15.1 2.5 %collective-permute-start.7 = (bf16[32,1024]{1,0:T(8,128)(2,1)S(1)}, bf16[32,1024]{1,0:T(8,128)(2,1)S(1)}, u32[]{:S(2)}, u32[]{:S(2)}) collective-permute-start(bf16[32,1024]{1,0:T(8,128)(2,1)S(1)} %get-tuple-element.27), channel_id=1, source_target_pairs={{0,3},{1,2},{2,1},{3,0},{4,7},{5,6},{6,5},{7,4},{8,11},{9,10},{10,... | collective-permute-start | bytes 196616 | tf_op jit(solution)/shard_map/ppermute | solution.py:294
  17.6 0.1 collective-permute-start.6
  17.7 0.1 collective-permute-done.4.refs_1_
  17.8 0.6 %collective-permute-start.9 = (bf16[64,1024]{1,0:T(8,128)(2,1)S(1)}, bf16[64,1024]{1,0:T(8,128)(2,1)S(1)}, u32[]{:S(2)}, u32[]{:S(2)}) collective-permute-start(bf16[64,1024]{1,0:T(8,128)(2,1)S(1)} %shard_map.71.refs_0_), channel_id=1, source_target_pairs={{0,24},{4,28},{8,16},{12,20},{16,8},{20,12},{24,0},{28,4},{1,25},{... | collective-permute-start | bytes 393224 | tf_op jit(solution)/shard_map/ppermute | solution.py:294
  18.4 1.5 %collective-permute-start.8 = (bf16[64,1024]{1,0:T(8,128)(2,1)S(1)}, bf16[64,1024]{1,0:T(8,128)(2,1)S(1)}, u32[]{:S(2)}, u32[]{:S(2)}) collective-permute-start(bf16[64,1024]{1,0:T(8,128)(2,1)S(1)} %shard_map.71.refs_0_), channel_id=1, source_target_pairs={{0,16},{4,20},{8,24},{12,28},{16,0},{20,4},{24,8},{28,12},{1,17},{... | collective-permute-start | bytes 393224 | tf_op jit(solution)/shard_map/ppermute | solution.py:294
  19.9 1.5 %collective-permute-start.5 = (bf16[64,1024]{1,0:T(8,128)(2,1)S(1)}, bf16[64,1024]{1,0:T(8,128)(2,1)S(1)}, u32[]{:S(2)}, u32[]{:S(2)}) collective-permute-start(bf16[64,1024]{1,0:T(8,128)(2,1)S(1)} %shard_map.71.refs_0_), channel_id=1, source_target_pairs={{0,8},{4,12},{8,0},{12,4},{16,24},{20,28},{24,16},{28,20},{1,9},{5... | collective-permute-start | bytes 393224 | tf_op jit(solution)/shard_map/ppermute | solution.py:294
  21.4 2.1 %collective-permute-done.6.refs_0_ = bf16[32,1024]{1,0:T(8,128)(2,1)S(1)} collective-permute-done((bf16[32,1024]{1,0:T(8,128)(2,1)S(1)}, bf16[32,1024]{1,0:T(8,128)(2,1)S(1)}, u32[]{:S(2)}, u32[]{:S(2)}) %collective-permute-start.6) | collective-permute-done | bytes 65568 | tf_op jit(solution)/shard_map/ppermute | solution.py:294
  23.5 0.5 %collective-permute-start.15 = (bf16[64,1024]{1,0:T(8,128)(2,1)S(1)}, bf16[64,1024]{1,0:T(8,128)(2,1)S(1)}, u32[]{:S(2)}, u32[]{:S(2)}) collective-permute-start(bf16[64,1024]{1,0:T(8,128)(2,1)S(1)} %shard_map.72.refs_0_.refs_2_), channel_id=1, source_target_pairs={{0,24},{4,28},{8,16},{12,20},{16,8},{20,12},{24,0},{28,4},{1,25},{... | collective-permute-start | bytes 393224 | tf_op jit(solution)/shard_map/ppermute | solution.py:294
  24.0 1.5 %collective-permute-start.13 = (bf16[64,1024]{1,0:T(8,128)(2,1)S(1)}, bf16[64,1024]{1,0:T(8,128)(2,1)S(1)}, u32[]{:S(2)}, u32[]{:S(2)}) collective-permute-start(bf16[64,1024]{1,0:T(8,128)(2,1)S(1)} %shard_map.72.refs_0_.refs_2_), channel_id=1, source_target_pairs={{0,16},{4,20},{8,24},{12,28},{16,0},{20,4},{24,8},{28,12},{1,17},{... | collective-permute-start | bytes 393224 | tf_op jit(solution)/shard_map/ppermute | solution.py:294
  25.5 1.5 %collective-permute-start.11 = (bf16[64,1024]{1,0:T(8,128)(2,1)S(1)}, bf16[64,1024]{1,0:T(8,128)(2,1)S(1)}, u32[]{:S(2)}, u32[]{:S(2)}) collective-permute-start(bf16[64,1024]{1,0:T(8,128)(2,1)S(1)} %shard_map.72.refs_0_.refs_2_), channel_id=1, source_target_pairs={{0,8},{4,12},{8,0},{12,4},{16,24},{20,28},{24,16},{28,20},{1,9},{5... | collective-permute-start | bytes 393224 | tf_op jit(solution)/shard_map/ppermute | solution.py:294
  27.1 2.5 %collective-permute-done.15.refs_1_.refs_2_ = bf16[64,1024]{1,0:T(8,128)(2,1)S(1)} collective-permute-done((bf16[64,1024]{1,0:T(8,128)(2,1)S(1)}, bf16[64,1024]{1,0:T(8,128)(2,1)S(1)}, u32[]{:S(2)}, u32[]{:S(2)}) %collective-permute-start.15) | collective-permute-done | bytes 131104 | tf_op jit(solution)/shard_map/ppermute | solution.py:294
  29.7 0.1 collective-permute-start.16
  29.7 0.6 %collective-permute-done.13.refs_2_ = bf16[64,1024]{1,0:T(8,128)(2,1)S(1)} collective-permute-done((bf16[64,1024]{1,0:T(8,128)(2,1)S(1)}, bf16[64,1024]{1,0:T(8,128)(2,1)S(1)}, u32[]{:S(2)}, u32[]{:S(2)}) %collective-permute-start.13) | collective-permute-done | bytes 131104 | tf_op jit(solution)/shard_map/ppermute | solution.py:294
  30.4 0.1 collective-permute-done.11.refs_2_
  30.5 0.4 %collective-permute-start.12 = (bf16[64,1024]{1,0:T(8,128)(2,1)S(1)}, bf16[64,1024]{1,0:T(8,128)(2,1)S(1)}, u32[]{:S(2)}, u32[]{:S(2)}) collective-permute-start(bf16[64,1024]{1,0:T(8,128)(2,1)S(1)} %collective-permute-done.11.refs_2_), channel_id=1, source_target_pairs={{0,4},{4,0},{8,12},{12,8},{16,20},{20,16},{24,28},{28,24},{1,5},{5... | collective-permute-start | bytes 393224 | tf_op jit(solution)/shard_map/ppermute | solution.py:294
  30.9 0.3 shard_map.74
  31.3 0.1 shard_map.76.refs_4_
  31.4 0.1 shard_map.77.refs_4_
  31.5 0.2 collective-permute-done.14.refs_3_
  31.7 0.1 shard_map.78.refs_4_
  31.8 0.1 collective-permute-done.12.refs_3_
  31.9 2.7 %shard_map.79 = (bf16[256,8192]{1,0:T(8,128)(2,1)}, f32[32,8192]{1,0:T(8,128)}, f32[32,8192]{1,0:T(8,128)}) custom-call(bf16[256,128]{1,0:T(8,128)(2,1)S(1)} %get-tuple-element.20.tok_ref, bf16[8,32,1024]{2,1,0:T(8,128)(2,1)S(1)} %get-tuple-element.31.own_ref, f32[32,8192]{1,0:T(8,128)S(1)} %get-tuple-element.32.base_ref, ...), custom_call_target="tpu_custom_call" | custom-call | flops 17179869184 | bytes 67108864 | tf_op jit(solution)/shard_map/pallas_call | solution.py:275
  (19 shorter events, 0.3 us)
Async XLA Ops:
  2.0 1.9 %collective-permute-start = (bf16[4,32,1024]{2,1,0:T(8,128)(2,1)S(1)}, bf16[4,32,1024]{2,1,0:T(8,128)(2,1)S(1)}, u32[]{:S(2)}, u32[]{:S(2)}) collective-permute-start(bf16[4,32,1024]{2,1,0:T(8,128)(2,1)S(1)} %shard_map.68), channel_id=1, source_target_pairs={{0,4},{4,0},{8,12},{12,8},{16,20},{20,16},{24,28},{28,24},{1,5},{5... | collective-permute-start | bytes 786440 | tf_op jit(solution)/shard_map/ppermute | solution.py:294
  3.9 9.5 %copy-start = (f32[32,8192]{1,0:T(8,128)S(1)}, f32[32,8192]{1,0:T(8,128)}, u32[]{:S(2)}) copy-start(f32[32,8192]{1,0:T(8,128)} %base_ref.3) | copy-start | bytes 3145732
  3.9 9.5 %copy-start.1 = (f32[32,8192]{1,0:T(8,128)S(1)}, f32[32,8192]{1,0:T(8,128)}, u32[]{:S(2)}) copy-start(f32[32,8192]{1,0:T(8,128)} %mom_ref.3) | copy-start | bytes 3145732
  4.0 5.3 %collective-permute-start.1 = (bf16[32,1024]{1,0:T(8,128)(2,1)S(1)}, bf16[32,1024]{1,0:T(8,128)(2,1)S(1)}, u32[]{:S(2)}, u32[]{:S(2)}) collective-permute-start(bf16[32,1024]{1,0:T(8,128)(2,1)S(1)} %get-tuple-element.23), channel_id=1, source_target_pairs={{0,8},{4,12},{8,0},{12,4},{16,24},{20,28},{24,16},{28,20},{1,9},{5... | collective-permute-start | bytes 196616 | tf_op jit(solution)/shard_map/ppermute | solution.py:294
  6.7 4.3 %collective-permute-start.2 = (bf16[32,1024]{1,0:T(8,128)(2,1)S(1)}, bf16[32,1024]{1,0:T(8,128)(2,1)S(1)}, u32[]{:S(2)}, u32[]{:S(2)}) collective-permute-start(bf16[32,1024]{1,0:T(8,128)(2,1)S(1)} %get-tuple-element.24), channel_id=1, source_target_pairs={{0,16},{4,20},{8,24},{12,28},{16,0},{20,4},{24,8},{28,12},{1,17},{... | collective-permute-start | bytes 196616 | tf_op jit(solution)/shard_map/ppermute | solution.py:294
  8.2 5.2 %collective-permute-start.3 = (bf16[32,1024]{1,0:T(8,128)(2,1)S(1)}, bf16[32,1024]{1,0:T(8,128)(2,1)S(1)}, u32[]{:S(2)}, u32[]{:S(2)}) collective-permute-start(bf16[32,1024]{1,0:T(8,128)(2,1)S(1)} %get-tuple-element.25), channel_id=1, source_target_pairs={{0,24},{4,28},{8,16},{12,20},{16,8},{20,12},{24,0},{28,4},{1,25},{... | collective-permute-start | bytes 196616 | tf_op jit(solution)/shard_map/ppermute | solution.py:294
  13.5 4.3 %collective-permute-start.4 = (bf16[32,1024]{1,0:T(8,128)(2,1)S(1)}, bf16[32,1024]{1,0:T(8,128)(2,1)S(1)}, u32[]{:S(2)}, u32[]{:S(2)}) collective-permute-start(bf16[32,1024]{1,0:T(8,128)(2,1)S(1)} %get-tuple-element.27), channel_id=1, source_target_pairs={{0,1},{1,0},{2,3},{3,2},{4,5},{5,4},{6,7},{7,6},{8,9},{9,8},{10,11... | collective-permute-start | bytes 196616 | tf_op jit(solution)/shard_map/ppermute | solution.py:294
  15.1 6.3 %collective-permute-start.7 = (bf16[32,1024]{1,0:T(8,128)(2,1)S(1)}, bf16[32,1024]{1,0:T(8,128)(2,1)S(1)}, u32[]{:S(2)}, u32[]{:S(2)}) collective-permute-start(bf16[32,1024]{1,0:T(8,128)(2,1)S(1)} %get-tuple-element.27), channel_id=1, source_target_pairs={{0,3},{1,2},{2,1},{3,0},{4,7},{5,6},{6,5},{7,4},{8,11},{9,10},{10,... | collective-permute-start | bytes 196616 | tf_op jit(solution)/shard_map/ppermute | solution.py:294
  17.6 5.9 %collective-permute-start.6 = (bf16[32,1024]{1,0:T(8,128)(2,1)S(1)}, bf16[32,1024]{1,0:T(8,128)(2,1)S(1)}, u32[]{:S(2)}, u32[]{:S(2)}) collective-permute-start(bf16[32,1024]{1,0:T(8,128)(2,1)S(1)} %get-tuple-element.27), channel_id=1, source_target_pairs={{0,2},{1,3},{2,0},{3,1},{4,6},{5,7},{6,4},{7,5},{8,10},{9,11},{10,... | collective-permute-start | bytes 196616 | tf_op jit(solution)/shard_map/ppermute | solution.py:294
  17.8 7.7 %collective-permute-start.9 = (bf16[64,1024]{1,0:T(8,128)(2,1)S(1)}, bf16[64,1024]{1,0:T(8,128)(2,1)S(1)}, u32[]{:S(2)}, u32[]{:S(2)}) collective-permute-start(bf16[64,1024]{1,0:T(8,128)(2,1)S(1)} %shard_map.71.refs_0_), channel_id=1, source_target_pairs={{0,24},{4,28},{8,16},{12,20},{16,8},{20,12},{24,0},{28,4},{1,25},{... | collective-permute-start | bytes 393224 | tf_op jit(solution)/shard_map/ppermute | solution.py:294
  18.4 8.7 %collective-permute-start.8 = (bf16[64,1024]{1,0:T(8,128)(2,1)S(1)}, bf16[64,1024]{1,0:T(8,128)(2,1)S(1)}, u32[]{:S(2)}, u32[]{:S(2)}) collective-permute-start(bf16[64,1024]{1,0:T(8,128)(2,1)S(1)} %shard_map.71.refs_0_), channel_id=1, source_target_pairs={{0,16},{4,20},{8,24},{12,28},{16,0},{20,4},{24,8},{28,12},{1,17},{... | collective-permute-start | bytes 393224 | tf_op jit(solution)/shard_map/ppermute | solution.py:294
  19.9 7.2 %collective-permute-start.5 = (bf16[64,1024]{1,0:T(8,128)(2,1)S(1)}, bf16[64,1024]{1,0:T(8,128)(2,1)S(1)}, u32[]{:S(2)}, u32[]{:S(2)}) collective-permute-start(bf16[64,1024]{1,0:T(8,128)(2,1)S(1)} %shard_map.71.refs_0_), channel_id=1, source_target_pairs={{0,8},{4,12},{8,0},{12,4},{16,24},{20,28},{24,16},{28,20},{1,9},{5... | collective-permute-start | bytes 393224 | tf_op jit(solution)/shard_map/ppermute | solution.py:294
  23.5 6.2 %collective-permute-start.15 = (bf16[64,1024]{1,0:T(8,128)(2,1)S(1)}, bf16[64,1024]{1,0:T(8,128)(2,1)S(1)}, u32[]{:S(2)}, u32[]{:S(2)}) collective-permute-start(bf16[64,1024]{1,0:T(8,128)(2,1)S(1)} %shard_map.72.refs_0_.refs_2_), channel_id=1, source_target_pairs={{0,24},{4,28},{8,16},{12,20},{16,8},{20,12},{24,0},{28,4},{1,25},{... | collective-permute-start | bytes 393224 | tf_op jit(solution)/shard_map/ppermute | solution.py:294
  24.0 6.4 %collective-permute-start.13 = (bf16[64,1024]{1,0:T(8,128)(2,1)S(1)}, bf16[64,1024]{1,0:T(8,128)(2,1)S(1)}, u32[]{:S(2)}, u32[]{:S(2)}) collective-permute-start(bf16[64,1024]{1,0:T(8,128)(2,1)S(1)} %shard_map.72.refs_0_.refs_2_), channel_id=1, source_target_pairs={{0,16},{4,20},{8,24},{12,28},{16,0},{20,4},{24,8},{28,12},{1,17},{... | collective-permute-start | bytes 393224 | tf_op jit(solution)/shard_map/ppermute | solution.py:294
  25.5 5.0 %collective-permute-start.11 = (bf16[64,1024]{1,0:T(8,128)(2,1)S(1)}, bf16[64,1024]{1,0:T(8,128)(2,1)S(1)}, u32[]{:S(2)}, u32[]{:S(2)}) collective-permute-start(bf16[64,1024]{1,0:T(8,128)(2,1)S(1)} %shard_map.72.refs_0_.refs_2_), channel_id=1, source_target_pairs={{0,8},{4,12},{8,0},{12,4},{16,24},{20,28},{24,16},{28,20},{1,9},{5... | collective-permute-start | bytes 393224 | tf_op jit(solution)/shard_map/ppermute | solution.py:294
  27.1 3.8 %collective-permute-start.10 = (bf16[4,64,1024]{2,1,0:T(8,128)(2,1)S(1)}, bf16[4,64,1024]{2,1,0:T(8,128)(2,1)S(1)}, u32[]{:S(2)}, u32[]{:S(2)}) collective-permute-start(bf16[4,64,1024]{2,1,0:T(8,128)(2,1)S(1)} %shard_map.73), channel_id=1, source_target_pairs={{0,4},{4,0},{8,12},{12,8},{16,20},{20,16},{24,28},{28,24},{1,5},{5... | collective-permute-start | bytes 1572872 | tf_op jit(solution)/shard_map/ppermute | solution.py:294
  29.7 1.6 %collective-permute-start.16 = (bf16[2,64,1024]{2,1,0:T(8,128)(2,1)S(1)}, bf16[2,64,1024]{2,1,0:T(8,128)(2,1)S(1)}, u32[]{:S(2)}, u32[]{:S(2)}) collective-permute-start(bf16[2,64,1024]{2,1,0:T(8,128)(2,1)S(1)} %shard_map.75), channel_id=1, source_target_pairs={{0,4},{4,0},{8,12},{12,8},{16,20},{20,16},{24,28},{28,24},{1,5},{5... | collective-permute-start | bytes 786440 | tf_op jit(solution)/shard_map/ppermute | solution.py:294
  30.4 1.3 %collective-permute-start.14 = (bf16[64,1024]{1,0:T(8,128)(2,1)S(1)}, bf16[64,1024]{1,0:T(8,128)(2,1)S(1)}, u32[]{:S(2)}, u32[]{:S(2)}) collective-permute-start(bf16[64,1024]{1,0:T(8,128)(2,1)S(1)} %collective-permute-done.13.refs_2_), channel_id=1, source_target_pairs={{0,4},{4,0},{8,12},{12,8},{16,20},{20,16},{24,28},{28,24},{1,5},{5... | collective-permute-start | bytes 393224 | tf_op jit(solution)/shard_map/ppermute | solution.py:294
  30.5 1.4 %collective-permute-start.12 = (bf16[64,1024]{1,0:T(8,128)(2,1)S(1)}, bf16[64,1024]{1,0:T(8,128)(2,1)S(1)}, u32[]{:S(2)}, u32[]{:S(2)}) collective-permute-start(bf16[64,1024]{1,0:T(8,128)(2,1)S(1)} %collective-permute-done.11.refs_2_), channel_id=1, source_target_pairs={{0,4},{4,0},{8,12},{12,8},{16,20},{20,16},{24,28},{28,24},{1,5},{5... | collective-permute-start | bytes 393224 | tf_op jit(solution)/shard_map/ppermute | solution.py:294
